TPU v7x, 32 devices: a whole 2x2x4 slice. The times are simulated.
32 devices in a mesh: stream: 2 (over x), batch: 16 (over z, y, core).
Axes of the slice: x: 2, y: 2, z: 4, core: 2. Of those that a mesh axis runs over, the one named last changes fastest.
Arguments:
- tokens: bfloat16 [2, 256, 64, 768], P('stream', 'batch'), may hold values from -6 to 6
- out_grad: bfloat16 [2, 256, 64, 768], P('stream', 'batch'), may hold values from -6 to 6
- master: float32 [128, 80, 768], P(None, 'batch'), may hold values from -2 to 2, as said below
- first_moment: float32 [128, 80, 768], P(None, 'batch'), may hold values from -32768 to 32768
- second_moment: float32 [128, 80, 768], P(None, 'batch'), may hold values from 0 to 32768, as said below
- small_params: float32 [12, 768], replicated, may hold values from -2 to 2
- small_first: float32 [12, 768], replicated, may hold values from -32768 to 32768
- small_second: float32 [12, 768], replicated, may hold values from 0 to 32768, as said below
- logit_scale: float32 [1], replicated, may hold values from 30 to 60
- scale_first: float32 [1], replicated, may hold values from -16.896 to 16.896
- scale_second: float32 [1], replicated, may hold values from 11.79648 to 190.0544
- pair_lang: int32 [256], replicated, may hold values from 0 to 108
- unit_owner: int32 [72], replicated, may hold values from 0 to 15, as said below
Outputs:
- block_out: bfloat16 [2, 256, 64, 768], P('stream', 'batch')
- input_grad: bfloat16 [2, 256, 64, 768], P('stream', 'batch')
- new_master: float32 [128, 80, 768], P(None, 'batch')
- new_first: float32 [128, 80, 768], P(None, 'batch')
- new_second: float32 [128, 80, 768], P(None, 'batch')
- new_copy: bfloat16 [128, 80, 768], P(None, 'batch')
- new_small: float32 [12, 768], replicated
- new_small_first: float32 [12, 768], replicated
- new_small_second: float32 [12, 768], replicated
- scale_new: float32 [1], replicated
- scale_first_new: float32 [1], replicated
- scale_second_new: float32 [1], replicated
- loss: float32 [1], replicated
Inputs may be any that keep to these rules, and one draw needn't show every extreme that they name: `unit_owner`: each entry names the device of the batch axis that owns weight block u; no device owns more than 5 blocks, and one owns exactly 5. `master`: slots that no block uses hold values of the same kind. `second_moment`: Positive. `small_second`: Positive.
All inputs are finite; a program needn't handle non-finite values.
Results may differ from a plain program's by a relative error of at most 0.012.
Values may be sent and summed in bfloat16 or wider, within the bound.
A program may use at most 320 MiB of HBM per device.

v0:
```python
import jax
import jax.numpy as jnp
from jax import lax
from jax.sharding import PartitionSpec as P

H = 12
HD = 64
FF = 3072
STEP = 10


HIGHEST = lax.Precision.HIGHEST
BETA_ONE = 0.9
BETA_TWO = 0.999
ADAM_EPS = 1e-06
RATE_UNITS = 0.02
RATE_SMALL = 0.1
RATE_SCALE = 2.0
DECAY = 0.01
MARGIN = 0.3
NORM_EPS = 1e-06


def from_partner(shard, axis, apart):
    return lax.ppermute(shard, axis, [(i, i ^ 1 << apart) for i in range(lax.axis_size(axis))])


def shortened(shard):

    def short(part):
        return part.astype(jnp.bfloat16) if part.dtype == jnp.float32 else part

    return jax.tree.map(short, shard)


def unit_positions(owner_list, slot_count):
    unit_total = owner_list.shape[0]
    same_owner = owner_list[:, None] == owner_list[None, :]
    ordinal = jnp.arange(unit_total, dtype=jnp.int32)
    earlier = ordinal[None, :] < ordinal[:, None]
    slot_number = jnp.sum(jnp.where(same_owner & earlier, 1, 0), axis=1).astype(jnp.int32)
    return owner_list * slot_count + slot_number


def layer_norm(resid, gain, shift):
    centre = jnp.mean(resid, axis=-1, keepdims=True)
    centred = resid - centre
    variance = jnp.mean(centred * centred, axis=-1, keepdims=True)
    return centred * lax.rsqrt(variance + NORM_EPS) * gain + shift


def gelu_exact(values):
    return jax.nn.gelu(values, approximate=False)


def normalize(vectors):
    return vectors * lax.rsqrt(jnp.sum(vectors * vectors, axis=-1, keepdims=True) + NORM_EPS)


def adamw(weight_in, gradient, moment_one, moment_two, rate_value, decay_value, fix_one, fix_two):
    new_one = BETA_ONE * moment_one + (1.0 - BETA_ONE) * gradient
    new_two = BETA_TWO * moment_two + (1.0 - BETA_TWO) * gradient * gradient
    stepped = new_one / fix_one / (jnp.sqrt(new_two / fix_two) + ADAM_EPS)
    return (weight_in - rate_value * (stepped + decay_value * weight_in), new_one, new_two)


def project_in(operand, weight):
    blocks = operand.reshape(operand.shape[0], weight.shape[1], weight.shape[0])
    return jnp.einsum("tkr,rkd->td", blocks, weight, preferred_element_type=jnp.float32)


def project_back(operand, weight):
    result = jnp.einsum("td,rkd->tkr", operand, weight, preferred_element_type=jnp.float32)
    return result.reshape(operand.shape[0], weight.shape[1] * weight.shape[0])


def outer_rows(source, target):
    return jnp.einsum("tkc,te->cke", source, target, preferred_element_type=jnp.float32)


def make_loss(my_langs, all_langs, row_offset):

    def local_loss(row_vecs, col_vecs, scale_value):
        cosines = jnp.dot(row_vecs, col_vecs.T, precision=HIGHEST)
        row_ids = row_offset + jnp.arange(row_vecs.shape[0], dtype=jnp.int32)
        col_ids = jnp.arange(col_vecs.shape[0], dtype=jnp.int32)
        diagonal = (row_ids[:, None] == col_ids[None, :]).astype(jnp.float32)
        logits = scale_value * (cosines - MARGIN * diagonal)
        same_group = my_langs[:, None] == all_langs[None, :]
        masked = jnp.where(same_group, logits, -1e30)
        row_top = jnp.max(masked, axis=1, keepdims=True)
        exp_total = jnp.sum(jnp.where(same_group, jnp.exp(masked - row_top), 0.0), axis=1)
        row_lse = jnp.log(exp_total) + row_top[:, 0]
        own_logit = jnp.sum(logits * diagonal, axis=1)
        return (jnp.sum(row_lse - own_logit), row_lse)

    return local_loss


def per_device(
    tokens,
    out_grad,
    master,
    first_moment,
    second_moment,
    small_params,
    small_first,
    small_second,
    logit_scale,
    scale_first,
    scale_second,
    pair_lang,
    unit_owner,
):
    owners = lax.axis_size("batch")
    here_batch = lax.axis_index("batch")
    unit_rows, slot_count, model_width = master.shape
    query_blocks = model_width // unit_rows
    inner_blocks = FF // unit_rows
    edges = [
        0,
        query_blocks,
        2 * query_blocks,
        3 * query_blocks,
        4 * query_blocks,
        4 * query_blocks + inner_blocks,
        4 * query_blocks + 2 * inner_blocks,
    ]
    positions = unit_positions(unit_owner, slot_count)
    table = jnp.arange(owners * slot_count, dtype=jnp.int32)[:, None] == positions[None, :]
    select_low = table.astype(jnp.bfloat16)
    select_full = table.astype(jnp.float32)
    owner_parts = lax.all_to_all(
        master.astype(jnp.bfloat16), "batch", split_axis=0, concat_axis=1, tiled=True
    )
    own_pieces = jnp.einsum(
        "rpd,pu->rud", owner_parts, select_low, preferred_element_type=jnp.float32
    ).astype(jnp.bfloat16)
    all_units = lax.all_gather(own_pieces, "batch", axis=0, tiled=True)
    w_query = all_units[:, edges[0] : edges[1]]
    w_key = all_units[:, edges[1] : edges[2]]
    w_value = all_units[:, edges[2] : edges[3]]
    w_out = all_units[:, edges[3] : edges[4]]
    w_inner = all_units[:, edges[4] : edges[5]]
    w_outer = all_units[:, edges[5] : edges[6]]
    inner_rows = FF // model_width
    bias_query = small_params[0]
    bias_value = small_params[1]
    bias_out = small_params[2]
    bias_inner = small_params[3 : 3 + inner_rows].reshape(FF)
    bias_outer = small_params[3 + inner_rows]
    gain_one = small_params[4 + inner_rows]
    shift_one = small_params[5 + inner_rows]
    gain_two = small_params[6 + inner_rows]
    shift_two = small_params[7 + inner_rows]
    sentences = tokens.shape[1]
    length = tokens.shape[2]
    row_count = sentences * length
    flat_rows = tokens.reshape(row_count, model_width)
    shape_heads = (sentences, length, H, HD)
    score_scale = HD ** (-0.5)
    queries = (project_in(flat_rows, w_query) + bias_query).astype(jnp.bfloat16)
    keys_rows = project_in(flat_rows, w_key).astype(jnp.bfloat16)
    values_rows = (project_in(flat_rows, w_value) + bias_value).astype(jnp.bfloat16)
    query_heads = queries.reshape(shape_heads)
    key_heads = keys_rows.reshape(shape_heads)
    value_heads = values_rows.reshape(shape_heads)
    scores = (
        jnp.einsum("slhe,smhe->shlm", query_heads, key_heads, preferred_element_type=jnp.float32)
        * score_scale
    )
    log_total = jax.nn.logsumexp(scores, axis=-1, keepdims=True)
    softmax_low = jnp.exp(scores - log_total).astype(jnp.bfloat16)
    context = jnp.einsum(
        "shlm,smhe->slhe", softmax_low, value_heads, preferred_element_type=jnp.float32
    )
    context = context.reshape(row_count, model_width).astype(jnp.bfloat16)
    attended = project_in(context, w_out) + bias_out
    hidden_one, norm_one_pull = jax.vjp(
        layer_norm, flat_rows.astype(jnp.float32) + attended, gain_one, shift_one
    )
    hidden_low = hidden_one.astype(jnp.bfloat16)
    inner_act = project_back(hidden_low, w_inner) + bias_inner
    active_full, gelu_pull = jax.vjp(gelu_exact, inner_act)
    active = active_full.astype(jnp.bfloat16)
    outer_out = project_in(active, w_outer) + bias_outer
    output, norm_two_pull = jax.vjp(layer_norm, hidden_one + outer_out, gain_two, shift_two)
    block_out = output.astype(jnp.bfloat16).reshape(tokens.shape)
    cls_rows = output.reshape(sentences, length, model_width)[:, 0, :]
    pooled, pool_pull = jax.vjp(normalize, cls_rows)
    across = from_partner(pooled.astype(jnp.bfloat16), "stream", 0).astype(pooled.dtype)
    others = lax.all_gather(across.astype(jnp.bfloat16), "batch", axis=0, tiled=True).astype(
        across.dtype
    )
    my_langs = lax.dynamic_slice_in_dim(pair_lang, here_batch * sentences, sentences)
    local_loss = make_loss(my_langs, pair_lang, here_batch * sentences)
    loss_local, loss_pull, row_lse = jax.vjp(
        local_loss, pooled, others, logit_scale[0], has_aux=True
    )
    grad_rows, grad_others, grad_scale = loss_pull(jnp.ones_like(loss_local))
    returned = lax.psum_scatter(grad_others, "batch", scatter_dimension=0, tiled=True)
    back_across = jax.tree.map(
        lambda part, own: part.astype(own.dtype),
        from_partner(shortened(returned), "stream", 0),
        returned,
    )
    (grad_cls,) = pool_pull(grad_rows + back_across)
    d_output = out_grad.astype(jnp.float32).reshape(sentences, length, model_width)
    d_output = d_output.at[:, 0, :].add(grad_cls).reshape(row_count, model_width)
    d_resid_two, d_gain_two, d_shift_two = norm_two_pull(d_output)
    d_outer = d_resid_two.astype(jnp.bfloat16)
    d_active = project_back(d_outer, w_outer)
    (d_inner_full,) = gelu_pull(d_active)
    d_inner = d_inner_full.astype(jnp.bfloat16)
    active_blocks = active.reshape(row_count, inner_blocks, unit_rows)
    inner_grad_blocks = d_inner.reshape(row_count, inner_blocks, unit_rows)
    d_hidden = d_resid_two + project_in(d_inner, w_inner)
    d_resid_one, d_gain_one, d_shift_one = norm_one_pull(d_hidden)
    d_attended = d_resid_one.astype(jnp.bfloat16)
    d_context = project_back(d_attended, w_out).astype(jnp.bfloat16)
    d_context_heads = d_context.reshape(shape_heads)
    scores_again = (
        jnp.einsum("slhe,smhe->shlm", query_heads, key_heads, preferred_element_type=jnp.float32)
        * score_scale
    )
    softmax_again = jnp.exp(scores_again - log_total)
    d_softmax = jnp.einsum(
        "slhe,smhe->shlm", d_context_heads, value_heads, preferred_element_type=jnp.float32
    )
    d_scores = (
        softmax_again * (d_softmax - jnp.sum(d_softmax * softmax_again, axis=-1, keepdims=True))
    ).astype(jnp.bfloat16)
    d_queries = (
        jnp.einsum("shlm,smhe->slhe", d_scores, key_heads, preferred_element_type=jnp.float32)
        * score_scale
    )
    d_queries = d_queries.astype(jnp.bfloat16).reshape(row_count, model_width)
    d_keys = (
        jnp.einsum("shlm,slhe->smhe", d_scores, query_heads, preferred_element_type=jnp.float32)
        * score_scale
    )
    d_keys = d_keys.astype(jnp.bfloat16).reshape(row_count, model_width)
    d_values = jnp.einsum(
        "shlm,slhe->smhe",
        softmax_again.astype(jnp.bfloat16),
        d_context_heads,
        preferred_element_type=jnp.float32,
    )
    d_values = d_values.astype(jnp.bfloat16).reshape(row_count, model_width)
    d_tokens = (
        d_resid_one
        + project_back(d_queries, w_query)
        + project_back(d_keys, w_key)
        + project_back(d_values, w_value)
    )
    input_grad = d_tokens.astype(jnp.bfloat16).reshape(tokens.shape)
    flat_blocks = flat_rows.reshape(row_count, query_blocks, unit_rows)
    context_blocks = context.reshape(row_count, query_blocks, unit_rows)
    pieces = lax.psum_scatter(
        jnp.concatenate(
            [
                jnp.concatenate(
                    [
                        outer_rows(flat_blocks, d_queries),
                        outer_rows(flat_blocks, d_keys),
                        outer_rows(flat_blocks, d_values),
                        outer_rows(context_blocks, d_attended),
                    ],
                    axis=1,
                ),
                jnp.concatenate(
                    [outer_rows(inner_grad_blocks, hidden_low), outer_rows(active_blocks, d_outer)],
                    axis=1,
                ),
            ],
            axis=1,
        ),
        "batch",
        scatter_dimension=0,
        tiled=True,
    )
    summed = lax.psum(pieces.astype(jnp.bfloat16), "stream").astype(jnp.float32)
    send_rows = jnp.einsum("rud,pu->rpd", summed, select_full, precision=HIGHEST)
    owned_grad = lax.all_to_all(
        send_rows.astype(jnp.bfloat16), "batch", split_axis=1, concat_axis=0, tiled=True
    ).astype(send_rows.dtype)
    small_grad_local = jnp.concatenate(
        [
            jnp.sum(d_queries, axis=0, dtype=jnp.float32)[None],
            jnp.sum(d_values, axis=0, dtype=jnp.float32)[None],
            jnp.sum(d_attended, axis=0, dtype=jnp.float32)[None],
            jnp.sum(d_inner, axis=0, dtype=jnp.float32).reshape(inner_rows, model_width),
            jnp.sum(d_outer, axis=0, dtype=jnp.float32)[None],
            d_gain_one[None],
            d_shift_one[None],
            d_gain_two[None],
            d_shift_two[None],
        ],
        axis=0,
    )
    small_total, scale_total, loss_total = lax.psum(
        (small_grad_local, grad_scale.reshape(1), loss_local.reshape(1)), ("stream", "batch")
    )
    step_value = float(STEP)
    fix_one = 1.0 - BETA_ONE**step_value
    fix_two = 1.0 - BETA_TWO**step_value
    my_table = lax.dynamic_slice_in_dim(select_full, here_batch * slot_count, slot_count, 0)
    filled = (jnp.sum(my_table, axis=1) > 0.0)[None, :, None]
    moved_weight, moved_first, moved_second = adamw(
        master, owned_grad, first_moment, second_moment, RATE_UNITS, DECAY, fix_one, fix_two
    )
    new_master = jnp.where(filled, moved_weight, master)
    new_first = jnp.where(filled, moved_first, first_moment)
    new_second = jnp.where(filled, moved_second, second_moment)
    new_copy = new_master.astype(jnp.bfloat16)
    new_small, new_small_first, new_small_second = adamw(
        small_params, small_total, small_first, small_second, RATE_SMALL, 0.0, fix_one, fix_two
    )
    scale_new, scale_one, scale_two = adamw(
        logit_scale, scale_total, scale_first, scale_second, RATE_SCALE, 0.0, fix_one, fix_two
    )
    loss_out = loss_total / (2 * owners * sentences)
    return (
        block_out,
        input_grad,
        new_master,
        new_first,
        new_second,
        new_copy,
        new_small,
        new_small_first,
        new_small_second,
        scale_new,
        scale_one,
        scale_two,
        loss_out,
    )


def solution(mesh):
    placed = (
        P("stream", "batch", None, None),
        P("stream", "batch", None, None),
        P(None, "batch", None),
        P(None, "batch", None),
        P(None, "batch", None),
        P(),
        P(),
        P(),
        P(),
        P(),
        P(),
        P(),
        P(),
    )
    return jax.shard_map(
        per_device,
        mesh=mesh,
        in_specs=placed,
        out_specs=(
            P("stream", "batch", None, None),
            P("stream", "batch", None, None),
            P(None, "batch", None),
            P(None, "batch", None),
            P(None, "batch", None),
            P(None, "batch", None),
            P(),
            P(),
            P(),
            P(),
            P(),
            P(),
            P(),
        ),
        check_vma=False,
    )
```

profile of v0, /device:TPU:8, one launch (start us, length us, event | category | flops | bytes accessed | tf_op | source)
XLA Modules:
  0.0 1040.7 jit_solution(12508951128972635456)
XLA Ops:
  10.5 6.3 all-to-all-start
  17.1 34.5 %all-to-all-done = bf16[128,5,768]{2,1,0:T(8,128)(2,1)S(1)} async-done(((bf16[128,5,768]{2,1,0:T(8,128)(2,1)}), bf16[128,5,768]{2,1,0:T(8,128)(2,1)S(1)}, u32[]{:S(2)}, u32[]{:S(2)}) %all-to-all-start) | async-done | bytes 983072 | tf_op jit(solution)/shard_map/all_to_all | solution.py:133
  53.4 2.8 reshape_reshape.2
  56.8 106.8 %all-gather.2.cloned.1.call-done = bf16[128,72,768]{2,1,0:T(8,128)(2,1)} async-done(((bf16[8,72,768]{2,1,0:T(8,128)(2,1)}), bf16[128,72,768]{2,1,0:T(8,128)(2,1)}) %all-gather.2.cloned.1.call-update) | async-done | bytes 14155792 | tf_op jit(solution)/shard_map/all_gather | solution.py:139
  163.6 6.8 fusion.122
  170.4 2.7 copy.359
  175.8 3.8 fusion.67
  179.6 3.3 reshape.274
  183.0 3.0 fusion.66
  186.0 3.3 reshape.273
  189.3 3.9 copy.305
  193.2 5.6 fusion.68
  198.9 5.2 reshape.275
  204.1 5.3 copy.291
  209.4 5.1 multiply_reduce_fusion.1
  218.8 2.4 copy.294
  221.3 3.2 convert_element_type.182
  224.4 4.1 fusion.123
  230.0 6.5 fusion.121
  236.6 48.5 %multiply_convert_fusion = (bf16[1024,24,128]{0,2,1:T(8,128)(2,1)S(1)}, f32[1024,24,128]{0,2,1:T(8,128)}, f32[128,24,1024]{2,0,1:T(8,128)}) fusion(f32[24,128]{1,0:T(8,128)S(1)} %add.236, f32[1024,768]{1,0:T(8,128)S(1)} %get-tuple-element.75, f32[768]{0:T(1024)S(1)} %get-tuple-element.32, f32[768]{0:T(1024)S(1)} %get-tuple-element.33, ...), kind=kOutput, calls=%fused_computation.13 | convolution fusion | flops 5043388416 | bytes 39348224 | tf_op jit(solution)/shard_map/td,rkd->tkr/dot_general | solution.py:73
  285.1 6.2 fusion.124
  297.8 18.4 %all_gather.7 = bf16[256,768]{1,0:T(8,128)(2,1)S(1)} all-gather(bf16[16,768]{1,0:T(8,128)(2,1)S(1)} %collective-permute-done), channel_id=1, replica_groups=mesh['stream'=2,'batch'=16] {'batch'}, dimensions={0}, use_global_device_ids=true | all-gather | bytes 417792 | tf_op jit(solution)/shard_map/all_gather | solution.py:192
  320.1 56.6 %reduce-scatter.3.cloned.1.call-done = f32[16,768]{1,0:T(8,128)} async-done(((f32[256,768]{1,0:T(8,128)}), f32[16,768]{1,0:T(8,128)}) %reduce-scatter.3.cloned.1.call-update) | async-done | bytes 49168 | tf_op jit(solution)/shard_map/reduce_scatter | solution.py:201
  379.0 2.5 copy_convert_fusion
  390.1 15.6 %convert_reduce_fusion = (f32[24,128]{1,0:T(8,128)S(1)}, bf16[1024,24,128]{0,2,1:T(8,128)(2,1)}) fusion(f32[1024,24,128]{0,2,1:T(8,128)} %get-tuple-element.61, bf16[1024,768]{1,0:T(8,128)(2,1)S(1)} %get-tuple-element.49, bf16[128,24,768]{2,1,0:T(8,128)(2,1)S(1)} %bitcast.282, f32[24,128]{1,0:T(8,128)S(1)} %add.236, f32[128,24,1024]{2,0,1:T(8,128)} %get-tuple-element.76), kind=kOutput, calls=%fused_computation.12 | convolution fusion | flops 4885312512 | bytes 37773312 | tf_op jit(solution)/shard_map/td,rkd->tkr/dot_general | solution.py:73
  405.7 8.7 multiply_reduce_fusion.2
  414.4 12.9 %fusion.26 = f32[128,24,768]{2,1,0:T(8,128)} fusion(bf16[1024,24,128]{0,2,1:T(8,128)(2,1)} %get-tuple-element.91, f32[1024,768]{1,0:T(8,128)S(1)} %copy-done.11, f32[768]{0:T(1024)S(1)} %get-tuple-element.32, f32[768]{0:T(1024)S(1)} %get-tuple-element.33, f32[1024]{0:T(1024)S(1)} %fusion.100, f32[1024]{0:T(1024)S(1)} %broadcast_multiply_fusion.1), kind=kOutput, calls=%fused_computation.51 | convolution fusion | flops 4835770368 | bytes 18888704 | tf_op jit(solution)/shard_map/tkc,te->cke/dot_general | solution.py:78
  433.1 2.8 convolution_bitcast_fusion
  435.9 13.4 %fusion.29 = f32[128,24,768]{2,1,0:T(8,128)} fusion(bf16[1024,24,128]{0,2,1:T(8,128)(2,1)S(1)} %bitcast.289, bf16[1024,768]{1,0:T(8,128)(2,1)S(1)} %get-tuple-element.49), kind=kOutput, calls=%fused_computation.52 | convolution fusion | flops 4831838208 | bytes 17301504 | tf_op jit(solution)/shard_map/tkc,te->cke/dot_general | solution.py:78
  449.4 3.3 convert_element_type.196
  452.7 5.5 copy.304
  458.3 7.2 convert_reduce_fusion.1
  465.6 4.5 multiply_reduce_fusion
  470.0 5.0 multiply_convert_fusion.3
  475.1 3.6 fusion.33
  478.7 3.2 convert_reduce_fusion.2
  481.9 2.4 copy.334
  484.3 4.2 copy.315
  488.5 3.2 reshape.312
  491.7 4.9 convolution_bitcast_fusion.2
  496.6 3.7 copy.332
  500.3 5.3 copy.308
  505.5 5.4 reshape.311
  510.9 4.9 convolution_bitcast_fusion.3
  515.8 3.5 copy.331
  519.3 5.3 copy.320
  524.5 5.4 reshape.313
  529.9 4.9 convolution_bitcast_fusion.1
  534.8 3.5 copy.333
  538.3 116.8 %concatenate.8 = f32[128,72,768]{2,1,0:T(8,128)} concatenate(f32[128,6,768]{2,1,0:T(8,128)} %copy.331, f32[128,6,768]{2,1,0:T(8,128)} %copy.332, f32[128,6,768]{2,1,0:T(8,128)} %copy.333, f32[128,6,768]{2,1,0:T(8,128)} %copy.334, f32[128,24,768]{2,1,0:T(8,128)} %fusion.26, f32[128,24,768]{2,1,0:T(8,128)} %fusion.29), dimensions={1} | concatenate | bytes 56623104 | tf_op jit(solution)/shard_map/concatenate | solution.py:260
  655.4 266.3 %reduce-scatter.5.cloned.1.call-done = f32[8,72,768]{2,1,0:T(8,128)} async-done(((f32[128,72,768]{2,1,0:T(8,128)}), f32[8,72,768]{2,1,0:T(8,128)}) %reduce-scatter.5.cloned.1.call-update) | async-done | bytes 1769488 | tf_op jit(solution)/shard_map/reduce_scatter | solution.py:259
  921.7 2.5 convert_element_type.206
  927.0 3.1 reshape.283
  930.2 5.6 reshape.281
  935.8 3.2 reshape.285
  941.4 41.8 %all-reduce = (f32[12,768]{1,0:T(8,128)S(1)}, f32[1]{0:T(128)}, f32[1]{0:T(128)}) all-reduce(f32[12,768]{1,0:T(8,128)S(1)} %concatenate.9, f32[1]{0:T(128)} %bitcast.55, f32[1]{0:T(128)} %bitcast.56), channel_id=1, replica_groups=mesh['stream'=2,'batch'=16] {'stream','batch'}, use_global_device_ids=true, to_apply=%region_31.32 | all-reduce | flops 9218 | bytes 73744 | tf_op jit(solution)/shard_map/psum | solution.py:301
  988.2 6.4 all-to-all-start.1
  994.7 3.2 fusion.54
  1000.2 3.2 fusion.56
  1003.4 2.4 copy.311
  1005.8 4.8 fusion.52
  1010.7 3.8 copy.323
  1015.8 5.5 add_convert_fusion
  1021.3 8.1 fusion.116
  (211 shorter events, 50.7 us)
Async XLA Ops:
  8.8 8.1 copy-start.52
  10.5 41.1 %all-to-all-start = ((bf16[128,5,768]{2,1,0:T(8,128)(2,1)}), bf16[128,5,768]{2,1,0:T(8,128)(2,1)S(1)}, u32[]{:S(2)}, u32[]{:S(2)}) async-start(bf16[128,5,768]{2,1,0:T(8,128)(2,1)} %copy.280), calls=%async_computation | async-start | bytes 3145728 | tf_op jit(solution)/shard_map/all_to_all | solution.py:133
  16.8 36.5 %copy-start.25 = (f32[12,768]{1,0:T(8,128)S(1)}, f32[12,768]{1,0:T(8,128)}, u32[]{:S(2)}) copy-start(f32[12,768]{1,0:T(8,128)} %param.20) | copy-start | bytes 110596
  16.8 36.5 %copy-start.18 = (bf16[1,16,64,768]{3,2,1,0:T(8,128)(2,1)S(1)}, bf16[1,16,64,768]{3,2,1,0:T(8,128)(2,1)}, u32[]{:S(2)}) copy-start(bf16[1,16,64,768]{3,2,1,0:T(8,128)(2,1)} %param.15) | copy-start | bytes 4718596
  16.9 146.8 %all-gather.2.cloned.1.call-start = ((), (), s32[]{:S(2)}) async-start(), calls=%async_computation.4 | async-start | bytes 15040512 | tf_op jit(solution)/shard_map/all_gather | solution.py:139
  17.1 39.1 %copy-start.43 = (s32[72]{0:T(128)}, s32[72]{0:T(128)S(1)}, u32[]{:S(2)}) copy-start(s32[72]{0:T(128)S(1)} %multiply_add_fusion.5) | copy-start | bytes 868
  53.3 323.5 %reduce-scatter.3.cloned.1.call-start = ((), (), s32[]{:S(2)}) async-start(), calls=%async_computation.5 | async-start | bytes 835584 | tf_op jit(solution)/shard_map/reduce_scatter | solution.py:201
  175.8 7.1 copy-start.14
  193.2 23.3 %copy-start.1 = (bf16[16,64,12,64]{3,1,2,0:T(8,128)(2,1)}, bf16[16,64,12,64]{3,1,2,0:T(8,128)(2,1)S(1)}, u32[]{:S(2)}) copy-start(bf16[16,64,12,64]{3,1,2,0:T(8,128)(2,1)S(1)} %copy.305) | copy-start | bytes 4718596
  214.5 2.6 copy-start
  217.0 1.8 copy-start.15
  228.5 56.5 %copy-start.10 = (f32[1024,768]{1,0:T(8,128)}, f32[1024,768]{1,0:T(8,128)S(1)}, u32[]{:S(2)}) copy-start(f32[1024,768]{1,0:T(8,128)S(1)} %get-tuple-element.75) | copy-start | bytes 9437188
  236.6 48.5 %copy-start.12 = (bf16[128,24,768]{2,1,0:T(8,128)(2,1)}, bf16[128,24,768]{2,1,0:T(8,128)(2,1)S(1)}, u32[]{:S(2)}) copy-start(bf16[128,24,768]{2,1,0:T(8,128)(2,1)S(1)} %get-tuple-element.63) | copy-start | bytes 14155780
  236.6 48.5 %copy-start.13 = (bf16[128,24,768]{2,1,0:T(8,128)(2,1)S(1)}, bf16[128,24,768]{2,1,0:T(8,128)(2,1)}, u32[]{:S(2)}) copy-start(bf16[128,24,768]{2,1,0:T(8,128)(2,1)} %get-tuple-element.62) | copy-start | bytes 14155780
  236.6 48.5 %copy-start.45 = (f32[768]{0:T(1024)S(1)}, f32[768]{0:T(1024)}, u32[]{:S(2)}) copy-start(f32[768]{0:T(1024)} %get-tuple-element.31) | copy-start | bytes 9220
  285.1 6.2 copy-start.53
  292.0 4.1 copy-start.34
  294.0 3.8 collective-permute-start
  295.4 86.1 %copy-start.46 = (s32[16]{0:T(128)}, s32[16]{0:T(128)S(1)}, u32[]{:S(2)}) copy-start(s32[16]{0:T(128)S(1)} %iota_add_fusion) | copy-start | bytes 196
  296.2 85.4 %copy-start.39 = (s32[16]{0:T(128)}, s32[16]{0:T(128)S(1)}, u32[]{:S(2)}) copy-start(s32[16]{0:T(128)S(1)} %dynamic_slice.6) | copy-start | bytes 196
  317.5 64.1 %copy-start.23 = (f32[16,256]{1,0:T(8,128)}, f32[16,256]{1,0:T(8,128)S(1)}, u32[]{:S(2)}) copy-start(f32[16,256]{1,0:T(8,128)S(1)} %get-tuple-element.80) | copy-start | bytes 49156
  317.5 64.1 %copy-start.37 = (f32[16]{0:T(128)}, f32[16]{0:T(128)S(1)}, u32[]{:S(2)}) copy-start(f32[16]{0:T(128)S(1)} %get-tuple-element.79) | copy-start | bytes 196
  317.7 63.9 %copy-start.41 = (f32[16]{0:T(128)}, f32[16]{0:T(128)S(1)}, u32[]{:S(2)}) copy-start(f32[16]{0:T(128)S(1)} %broadcast_divide_fusion) | copy-start | bytes 196
  318.3 63.3 %copy-start.48 = (f32[16]{0:T(128)}, f32[16]{0:T(128)S(1)}, u32[]{:S(2)}) copy-start(f32[16]{0:T(128)S(1)} %add_divide_fusion) | copy-start | bytes 196
  320.1 601.6 %reduce-scatter.5.cloned.1.call-start = ((), (), s32[]{:S(2)}) async-start(), calls=%async_computation.6 | async-start | bytes 30081024 | tf_op jit(solution)/shard_map/reduce_scatter | solution.py:259
  377.6 4.0 copy-start.22
  377.6 4.0 collective-permute-start.1
  382.2 1.6 copy-start.5
  387.3 2.8 slice-start.4
  387.3 2.8 slice-start.5
  389.1 16.6 %slice-start.2 = ((s8[4718592]{0:T(1024)(128)(4,1)}), s8[4194304]{0:T(1024)(128)(4,1)S(1)}, s32[]{:S(2)}) async-start(s8[4718592]{0:T(1024)(128)(4,1)} %bitcast.279), calls=%async_computation.10 | async-start | bytes 8388608
  390.0 15.6 %copy-start.11 = (f32[1024,768]{1,0:T(8,128)S(1)}, f32[1024,768]{1,0:T(8,128)}, u32[]{:S(2)}) copy-start(f32[1024,768]{1,0:T(8,128)} %copy-done.10) | copy-start | bytes 9437188
  390.0 15.6 %slice-start.3 = ((s8[4718592]{0:T(1024)(128)(4,1)}), s8[524288]{0:T(1024)(128)(4,1)S(1)}, s32[]{:S(2)}) async-start(s8[4718592]{0:T(1024)(128)(4,1)} %bitcast.279), calls=%async_computation.11 | async-start | bytes 1048576
  414.4 13.0 %copy-start.31 = (f32[1024]{0:T(1024)S(1)}, f32[1024]{0:T(1024)}, u32[]{:S(2)}) copy-start(f32[1024]{0:T(1024)} %copy-done.30) | copy-start | bytes 12292
  429.1 4.0 copy-start.8
  429.1 2.5 copy-start.19
  431.6 4.3 slice-start.6
  433.1 2.9 slice-start.7
  452.7 5.6 copy-start.16
  452.7 12.8 %slice-start = ((s8[6291456]{0:T(1024)(128)(4,1)}), s8[2097152]{0:T(1024)(128)(4,1)S(1)}, s32[]{:S(2)}) async-start(s8[6291456]{0:T(1024)(128)(4,1)} %bitcast.273), calls=%async_computation.8 | async-start | bytes 4194304
  458.2 7.2 slice-start.1
  458.2 7.2 copy-start.2
  458.2 7.3 copy-start.4
  470.0 5.0 copy-start.6
  475.1 3.6 copy-start.7
  478.7 3.2 copy-start.17
  655.2 270.3 %copy-start.44 = (s32[72]{0:T(128)S(1)}, s32[72]{0:T(128)}, u32[]{:S(2)}) copy-start(s32[72]{0:T(128)} %copy-done.43) | copy-start | bytes 868
  655.2 270.5 %copy-start.24 = (f32[16,256]{1,0:T(8,128)S(1)}, f32[16,256]{1,0:T(8,128)}, u32[]{:S(2)}) copy-start(f32[16,256]{1,0:T(8,128)} %copy-done.23) | copy-start | bytes 49156
  655.2 270.5 %copy-start.35 = (s32[256]{0:T(256)S(1)}, s32[256]{0:T(256)}, u32[]{:S(2)}) copy-start(s32[256]{0:T(256)} %param.26) | copy-start | bytes 3076
  655.2 270.5 %copy-start.38 = (f32[16]{0:T(128)S(1)}, f32[16]{0:T(128)}, u32[]{:S(2)}) copy-start(f32[16]{0:T(128)} %copy-done.37) | copy-start | bytes 196
  655.2 270.5 %copy-start.40 = (s32[16]{0:T(128)S(1)}, s32[16]{0:T(128)}, u32[]{:S(2)}) copy-start(s32[16]{0:T(128)} %copy-done.39) | copy-start | bytes 196
  655.3 270.5 %copy-start.42 = (f32[16]{0:T(128)S(1)}, f32[16]{0:T(128)}, u32[]{:S(2)}) copy-start(f32[16]{0:T(128)} %copy-done.41) | copy-start | bytes 196
  655.3 270.5 %copy-start.47 = (s32[16]{0:T(128)S(1)}, s32[16]{0:T(128)}, u32[]{:S(2)}) copy-start(s32[16]{0:T(128)} %copy-done.46) | copy-start | bytes 196
  655.3 270.5 %copy-start.49 = (f32[16]{0:T(128)S(1)}, f32[16]{0:T(128)}, u32[]{:S(2)}) copy-start(f32[16]{0:T(128)} %copy-done.48) | copy-start | bytes 196
  655.3 271.1 %copy-start.51 = (f32[16]{0:T(128)S(1)}, f32[16]{0:T(128)}, u32[]{:S(2)}) copy-start(f32[16]{0:T(128)} %copy-done.50) | copy-start | bytes 196
  655.3 330.0 %all-reduce.3.cloned.1.call-start = ((), (), s32[]{:S(2)}) async-start(), calls=%async_computation.7 | async-start | bytes 1769472 | tf_op jit(solution)/shard_map/psum | solution.py:282
  930.2 5.6 copy-start.3
  935.8 5.3 copy-start.36
  935.8 5.3 copy-start.33
  988.2 33.0 %all-to-all-start.1 = ((bf16[8,80,768]{2,0,1:T(8,128)(2,1)}), bf16[8,80,768]{2,0,1:T(8,128)(2,1)}, u32[]{:S(2)}, u32[]{:S(2)}) async-start(bf16[8,80,768]{2,0,1:T(8,128)(2,1)} %copy.335), calls=%async_computation.3 | async-start | bytes 1966080 | tf_op jit(solution)/shard_map/all_to_all | solution.py:284
  1010.7 4.4 copy-start.26
  1010.7 4.4 copy-start.28
  1010.7 4.4 copy-start.29
  1010.7 5.1 copy-start.9
  (6 other events, 5.1 us)
Sparse Core Ops, SparseCore 0:
  53.4 110.1 all-gather.1
  320.2 56.5 reduce-scatter.2
  655.3 266.3 reduce-scatter.4
  924.5 37.6 all-reduce.2
where the time goes:
time: 1050 us; the launch traced here: 1040 us
  waiting for transfers between devices  466 us (44%)
  local copies, waits for them, and re-layouts  249 us (24%)
  matrix products  183 us (17%)
  blocking collectives  60.2 us (6%)
  other arithmetic  42.5 us (4%)
  between operations  24.2 us (2%)
  starting transfers between devices  15.8 us (2%)
    reduce_scatter x1, waiting for transfers between devices, per_device(): lax.psum_scatter(jnp.concatenate([jnp.concatenate([outer_rows(flat_blocks...  266 us
    concatenate x1, local copies, waits for them, and re-layouts, per_device(): jnp.concatenate([jnp.concatenate([outer_rows(flat_blocks, d_queries), out...  117 us
    all_gather x1, waiting for transfers between devices, per_device(): all_units = lax.all_gather(own_pieces, 'batch', axis=0, tiled=True)  107 us
    dot_general x6, matrix products, project_back(): jnp.einsum('td,rkd->tkr', operand, weight, preferred_element_type=jnp.flo...  76.7 us
    reduce_scatter x1, waiting for transfers between devices, per_device(): lax.psum_scatter(grad_others, 'batch', scatter_dimension=0, tiled=True)  56.6 us
    dot_general x6, matrix products, outer_rows(): jnp.einsum('tkc,te->cke', source, target, preferred_element_type=jnp.floa...  43.8 us
    psum x1, blocking collectives, per_device(): lax.psum((small_grad_local, grad_scale.reshape(1), loss_local.reshape(1))...  41.8 us
    all_to_all x1, waiting for transfers between devices, per_device(): lax.all_to_all(master.astype(jnp.bfloat16), 'batch', split_axis=0, concat...  34.5 us
  transfers between devices with their start and end apart: 8, of which 5 were waited for; matrix products, arithmetic and copies ran while one was open for 5% of the time, Pallas kernels for 0%

commit v1 on v0

v1 whole, which is shorter than its diff:
```python
import functools

import jax
import jax.numpy as jnp
from jax import lax
from jax.experimental import pallas as pl
from jax.experimental.pallas import tpu as pltpu
from jax.sharding import PartitionSpec as P

H = 12
HD = 64
FF = 3072
STEP = 10
ZS = 4
UR_ROWS = 128
LEN_ROWS = 64
VMEM_MOST = 60 << 20
MESH = pl.DeviceIdType.MESH

HIGHEST = lax.Precision.HIGHEST
BETA_ONE = 0.9
BETA_TWO = 0.999
ADAM_EPS = 1e-06
RATE_UNITS = 0.02
RATE_SMALL = 0.1
RATE_SCALE = 2.0
DECAY = 0.01
MARGIN = 0.3
NORM_EPS = 1e-06


def place():
    s = lax.axis_index("stream")
    b = lax.axis_index("batch")
    return s, b // 4, (b // 2) % 2, b % 2


def batch_of(z, y, c):
    return (z * 2 + y) * 2 + c


def greet(s, z, y, c, others):
    barrier = pltpu.get_barrier_semaphore()

    def hello(target):
        pl.semaphore_signal(barrier, inc=1, device_id=target, device_id_type=MESH)

    hello((s, batch_of(z, y, 1 - c)))
    hello((s, batch_of(z, 1 - y, c)))
    hello((1 - s, batch_of(z, y, c)))
    if others == "line":
        for far in range(1, ZS):

            @pl.when(z >= far)
            def _():
                hello((s, batch_of(z - far, y, c)))

            @pl.when(z + far < ZS)
            def _():
                hello((s, batch_of(z + far, y, c)))

        pl.semaphore_wait(barrier, 3 + ZS - 1)
    else:

        @pl.when(z >= 1)
        def _():
            hello((s, batch_of(z - 1, y, c)))

        @pl.when(z + 1 < ZS)
        def _():
            hello((s, batch_of(z + 1, y, c)))

        pl.semaphore_wait(barrier, 3 + (z + 2) // 3 + (5 - z) // 3)


GR = 80
GX = UR_ROWS - GR


def gather_kernel(own_ref, out_ref, low, stage_sem, zl_s, zl_r, zr_s, zr_r, y_s, y_r, x_s, x_r, ca_s, ca_r, cb_s, cb_r):
    s, z, y, c = place()
    slots = own_ref.shape[0]
    steps = ZS * slots
    base = pl.multiple_of(s * GX, 16)
    only = pl.multiple_of(s * GR, 16)
    theirs = pl.multiple_of((1 - s) * GR, 16)

    def at(zz, yy, cc, j):
        return batch_of(zz, yy, cc) * slots + j

    greet(s, z, y, c, "next")

    def push(src, row, start, size, send, recv, target):
        return pltpu.make_async_remote_copy(
            src_ref=src,
            dst_ref=out_ref.at[row, pl.ds(start, size)],
            send_sem=send,
            recv_sem=recv,
            device_id=target,
            device_id_type=MESH,
        )

    left = (s, batch_of(z - 1, y, c))
    right = (s, batch_of(z + 1, y, c))
    across = (s, batch_of(z, 1 - y, c))
    other = (1 - s, batch_of(z, y, c))
    sibling = (s, batch_of(z, y, 1 - c))

    def to_left(src, zz, j):
        row = at(zz, y, c, j)
        return push(src(row), row, base, GR, zl_s.at[zz, j], zl_r.at[zz, j], left)

    def to_right(src, zz, j):
        row = at(zz, y, c, j)
        return push(src(row), row, base, GR, zr_s.at[zz, j], zr_r.at[zz, j], right)

    def to_across(src, zz, j):
        row = at(zz, y, c, j)
        return push(src(row), row, base, GR, y_s.at[zz, j], y_r.at[zz, j], across)

    def to_other(zz, yy, j):
        row = at(zz, yy, c, j)
        return push(out_ref.at[row, pl.ds(only, GX)], row, only, GX, x_s.at[zz, yy, j], x_r.at[zz, yy, j], other)

    def to_sibling(zz, yy, j):
        row = at(zz, yy, c, j)
        return push(out_ref.at[row, pl.ds(base, GR)], row, base, GR, ca_s.at[zz, yy, j], ca_r.at[zz, yy, j], sibling)

    def rest_to_sibling(zz, yy, j):
        row = at(zz, yy, c, j)
        return push(out_ref.at[row, pl.ds(theirs, GX)], row, theirs, GX, cb_s.at[zz, yy, j], cb_r.at[zz, yy, j], sibling)

    def landed(row):
        return out_ref.at[row, pl.ds(base, GR)]

    def from_left(zz, j):
        row = at(zz, y, c, j)
        return push(landed(row), row, base, GR, zr_s.at[zz, j], zr_r.at[zz, j], right)

    def arrived_line(zz, j, onward):
        onward.start()
        to_across(landed, zz, j).start()
        to_other(zz, y, j).start()
        to_sibling(zz, y, j).start()

    def stage(j):
        return pltpu.make_async_copy(low.at[j], out_ref.at[at(z, y, c, j)], stage_sem.at[j])

    for j in range(slots):
        low[j] = own_ref[j].astype(jnp.bfloat16)
        mine = lambda row: low.at[j, pl.ds(base, GR)]

        @pl.when(z > 0)
        def _():
            to_left(mine, z, j).start()

        @pl.when(z < ZS - 1)
        def _():
            to_right(mine, z, j).start()

        to_across(mine, z, j).start()
        row = at(z, y, c, j)
        push(low.at[j, pl.ds(base, GR)], row, base, GR, ca_s.at[z, y, j], ca_r.at[z, y, j], sibling).start()
        push(low.at[j, pl.ds(theirs, GX)], row, theirs, GX, cb_s.at[z, y, j], cb_r.at[z, y, j], sibling).start()
        stage(j).start()

    def line_step(t):
        d = t // slots
        j = t % slots

        @pl.when((d >= 1) & (z - d >= 0))
        def _():
            zz = z - d
            to_right(landed, zz, j).wait_recv()

            @pl.when(z < ZS - 1)
            def _():
                to_right(landed, zz, j).start()

            to_across(landed, zz, j).start()
            to_other(zz, y, j).start()
            to_sibling(zz, y, j).start()

        @pl.when((d >= 1) & (z + d < ZS))
        def _():
            zz = z + d
            to_left(landed, zz, j).wait_recv()

            @pl.when(z > 0)
            def _():
                to_left(landed, zz, j).start()

            to_across(landed, zz, j).start()
            to_other(zz, y, j).start()
            to_sibling(zz, y, j).start()

    def across_one(zz, j):
        row = at(zz, 1 - y, c, j)
        push(landed(row), row, base, GR, y_s.at[zz, j], y_r.at[zz, j], across).wait_recv()
        to_other(zz, 1 - y, j).start()
        to_sibling(zz, 1 - y, j).start()

    def across_step(t):
        d = t // slots
        j = t % slots

        @pl.when(z - d >= 0)
        def _():
            across_one(z - d, j)

        @pl.when((d >= 1) & (z + d < ZS))
        def _():
            across_one(z + d, j)

    def other_one(zz, yy, j):
        row = at(zz, yy, c, j)
        push(
            out_ref.at[row, pl.ds(theirs, GX)], row, theirs, GX, x_s.at[zz, yy, j], x_r.at[zz, yy, j], other
        ).wait_recv()
        rest_to_sibling(zz, yy, j).start()

    def other_step(t, yy, first):
        d = t // slots
        j = t % slots

        @pl.when((d >= first) & (z - d >= 0))
        def _():
            other_one(z - d, yy, j)

        @pl.when((d >= 1) & (z + d < ZS))
        def _():
            other_one(z + d, yy, j)

    @pl.loop(0, steps + 3)
    def _(t):
        @pl.when(t < steps)
        def _():
            line_step(t)

        @pl.when((t >= 1) & (t < steps + 1))
        def _():
            across_step(t - 1)

        @pl.when((t >= 2) & (t < steps + 2))
        def _():
            other_step(t - 2, y, 1)

        @pl.when(t >= 3)
        def _():
            other_step(t - 3, 1 - y, 0)

    for j in range(slots):
        stage(j).wait()

    @pl.loop(0, steps)
    def _(t):
        zz = t // slots
        j = t % slots

        @pl.when((z > 0) & (zz >= z))
        def _():
            to_left(landed, zz, j).wait_send()

        @pl.when((z < ZS - 1) & (zz <= z))
        def _():
            to_right(landed, zz, j).wait_send()

        to_across(landed, zz, j).wait_send()

        @pl.when(zz != z)
        def _():
            to_other(zz, y, j).wait_send()

        to_other(zz, 1 - y, j).wait_send()
        for yy in range(2):
            to_sibling(zz, yy, j).wait_send()
            rest_to_sibling(zz, yy, j).wait_send()
            row = at(zz, yy, 1 - c, j)
            push(landed(row), row, base, GR, ca_s.at[zz, yy, j], ca_r.at[zz, yy, j], sibling).wait_recv()
            push(
                out_ref.at[row, pl.ds(theirs, GX)], row, theirs, GX, cb_s.at[zz, yy, j], cb_r.at[zz, yy, j], sibling
            ).wait_recv()


def gather_units(own):
    slots, rows, width = own.shape
    owners = lax.axis_size("batch")
    line = [pltpu.SemaphoreType.DMA((ZS, slots))] * 6
    plane = [pltpu.SemaphoreType.DMA((ZS, 2, slots))] * 6
    return pl.pallas_call(
        gather_kernel,
        name="gather_units",
        out_shape=jax.ShapeDtypeStruct((owners * slots, rows, width), jnp.bfloat16),
        in_specs=[pl.BlockSpec(memory_space=pltpu.VMEM)],
        out_specs=pl.BlockSpec(memory_space=pl.ANY),
        scratch_shapes=[pltpu.VMEM((slots, rows, width), jnp.bfloat16), pltpu.SemaphoreType.DMA((slots,))] + line + plane,
        compiler_params=pltpu.CompilerParams(collective_id=0, has_side_effects=True, vmem_limit_bytes=24 << 20),
    )(own)


RX = 32
RY = UR_ROWS - RX


def reduce_kernel(g_ref, small_ref, out_ref, small_out, held, c_in, x_in, y_in, z_in, f_in, t_acc, t_in,
                  p_sem, c_s, c_r, x_s, x_r, y_s, y_r, zl_s, zl_r, zr_s, zr_r, f_s, f_r, t_s, t_r):
    s, z, y, c = place()
    slots = out_ref.shape[0]
    steps = ZS * slots
    base = pl.multiple_of(s * RX, 16)
    only = pl.multiple_of(s * RY, 16)
    theirs = pl.multiple_of((1 - s) * RY, 16)
    left = (s, batch_of(z - 1, y, c))
    right = (s, batch_of(z + 1, y, c))
    across = (s, batch_of(z, 1 - y, c))
    other = (1 - s, batch_of(z, y, c))
    sibling = (s, batch_of(z, y, 1 - c))
    round_to = (sibling, across, other, (s, batch_of(z + 1 - 2 * (z % 2), y, c)), (s, batch_of((z + 2) % ZS, y, c)))
    greet(s, z, y, c, "line")

    def remote(src, dst, send, recv, target):
        return pltpu.make_async_remote_copy(
            src_ref=src, dst_ref=dst, send_sem=send, recv_sem=recv, device_id=target, device_id_type=MESH
        )

    def where_of(t):
        return (3 * (t // slots)) % ZS, t % slots

    def to_sibling(zz, yy, j):
        row = batch_of(zz, yy, 1 - c) * slots + j
        return remote(g_ref.at[row], c_in.at[zz, yy, j], c_s.at[zz, yy, j], c_r.at[zz, yy, j], sibling)

    def fetch(zz, yy, j):
        row = batch_of(zz, yy, c) * slots + j
        return pltpu.make_async_copy(g_ref.at[row], held.at[zz, yy, j], p_sem.at[zz, yy, j])

    def to_other(zz, yy, j):
        return remote(held.at[zz, yy, j, pl.ds(theirs, RX)], x_in.at[zz, yy, j], x_s.at[zz, yy, j], x_r.at[zz, yy, j], other)

    def to_across(zz, j):
        return remote(held.at[zz, 1 - y, j, pl.ds(base, RY)], y_in.at[zz, j], y_s.at[zz, j], y_r.at[zz, j], across)

    def to_left(zz, j):
        return remote(held.at[zz, y, j, pl.ds(base, RY)], z_in.at[1, zz, j], zl_s.at[zz, j], zl_r.at[zz, j], left)

    def to_right(zz, j):
        return remote(held.at[zz, y, j, pl.ds(base, RY)], z_in.at[0, zz, j], zr_s.at[zz, j], zr_r.at[zz, j], right)

    def final(j):
        return remote(held.at[z, y, j, pl.ds(base, RY)], f_in.at[j], f_s.at[j], f_r.at[j], other)

    def turn(r):
        return remote(t_acc.at[r], t_in.at[r], t_s.at[r], t_r.at[r], round_to[r])

    def add(zz, yy, j, start, size, got):
        mine = held.at[zz, yy, j, pl.ds(start, size)]
        mine[...] = (mine[...].astype(jnp.float32) + got[...].astype(jnp.float32)).astype(jnp.bfloat16)

    @pl.loop(0, steps)
    def _(t):
        zz, j = where_of(t)
        for yy in (1 - y, y):
            to_sibling(zz, yy, j).start()
            fetch(zz, yy, j).start()

    t_acc[0] = small_ref[...]

    def core_stage(t):
        zz, j = where_of(t)
        for yy in (1 - y, y):
            fetch(zz, yy, j).wait()
            to_sibling(zz, yy, j).wait_recv()
            add(zz, yy, j, 0, UR_ROWS, c_in.at[zz, yy, j])
            to_other(zz, yy, j).start()

    def other_stage(t):
        zz, j = where_of(t)
        for yy in (1 - y, y):
            to_other(zz, yy, j).wait_recv()
            add(zz, yy, j, only, RX, x_in.at[zz, yy, j])
        to_across(zz, j).start()

    def across_stage(t):
        zz, j = where_of(t)
        to_across(zz, j).wait_recv()
        add(zz, y, j, base, RY, y_in.at[zz, j])

    def from_left(zz, j):
        to_right(zz, j).wait_recv()
        add(zz, y, j, base, RY, z_in.at[0, zz, j])

    def from_right(zz, j):
        to_left(zz, j).wait_recv()
        add(zz, y, j, base, RY, z_in.at[1, zz, j])

    def line_stage(t, hops):
        zz, j = where_of(t)

        @pl.when((zz > z) & (z == hops))
        def _():
            if hops > 0:
                from_left(zz, j)
            to_right(zz, j).start()

        @pl.when((zz < z) & (ZS - 1 - z == hops))
        def _():
            if hops > 0:
                from_right(zz, j)
            to_left(zz, j).start()

        @pl.when((zz == z) & (3 - ((z + 2) // 3) * ((5 - z) // 3) == hops))
        def _():
            @pl.when(z > 0)
            def _():
                from_left(zz, j)

            @pl.when(z < ZS - 1)
            def _():
                from_right(zz, j)

            final(j).start()

    def final_stage(t):
        zz, j = where_of(t)

        @pl.when(zz == z)
        def _():
            final(j).wait_recv()
            f32 = jnp.float32
            out_ref[j, pl.ds(only, RX)] = held[z, y, j, pl.ds(only, RX)].astype(f32)
            shared = f_in[j, pl.ds(pl.multiple_of(s * RX, 16), RY - RX)].astype(f32)
            out_ref[j, pl.ds(RX, RY - RX)] = held[z, y, j, pl.ds(RX, RY - RX)].astype(f32) + shared
            out_ref[j, pl.ds(theirs, RX)] = f_in[j, pl.ds(pl.multiple_of((1 - s) * (RY - RX), 16), RX)].astype(f32)

    @pl.loop(0, steps + 6)
    def _(i):
        @pl.when(i < steps)
        def _():
            core_stage(i)

        @pl.when((i >= 1) & (i < steps + 1))
        def _():
            other_stage(i - 1)

        @pl.when((i >= 2) & (i < steps + 2))
        def _():
            across_stage(i - 2)

        for hops in range(ZS):

            @pl.when((i >= 2 + hops) & (i < steps + 2 + hops))
            def _():
                line_stage(i - 2 - hops, hops)

        @pl.when(i >= 6)
        def _():
            final_stage(i - 6)

        for r in range(5):

            @pl.when(i == 3 * r)
            def _():
                turn(r).start()

            @pl.when(i == 3 * r + 2)
            def _():
                turn(r).wait()
                t_acc[r + 1] = t_acc[r] + t_in[r]

    small_out[...] = t_acc[5]

    @pl.loop(0, steps)
    def _(t):
        zz, j = where_of(t)
        for yy in range(2):
            to_sibling(zz, yy, j).wait_send()
            to_other(zz, yy, j).wait_send()
        to_across(zz, j).wait_send()

        @pl.when(zz > z)
        def _():
            to_right(zz, j).wait_send()

        @pl.when(zz < z)
        def _():
            to_left(zz, j).wait_send()

        @pl.when(zz == z)
        def _():
            final(j).wait_send()


def reduce_units(grads, small, slots):
    owners = lax.axis_size("batch")
    _, rows, width = grads.shape
    bf, f32 = jnp.bfloat16, jnp.float32
    dma = pltpu.SemaphoreType.DMA
    return pl.pallas_call(
        reduce_kernel,
        name="reduce_units",
        out_shape=[jax.ShapeDtypeStruct((slots, rows, width), f32), jax.ShapeDtypeStruct(small.shape, f32)],
        in_specs=[pl.BlockSpec(memory_space=pl.ANY), pl.BlockSpec(memory_space=pltpu.VMEM)],
        out_specs=[pl.BlockSpec(memory_space=pltpu.VMEM)] * 2,
        scratch_shapes=[
            pltpu.VMEM((ZS, 2, slots, rows, width), bf),
            pltpu.VMEM((ZS, 2, slots, rows, width), bf),
            pltpu.VMEM((ZS, 2, slots, RX, width), bf),
            pltpu.VMEM((ZS, slots, RY, width), bf),
            pltpu.VMEM((2, ZS, slots, RY, width), bf),
            pltpu.VMEM((slots, RY, width), bf),
            pltpu.VMEM((6,) + small.shape, f32),
            pltpu.VMEM((5,) + small.shape, f32),
        ]
        + [dma((ZS, 2, slots))] * 5
        + [dma((ZS, slots))] * 6
        + [dma((slots,))] * 2
        + [dma((5,))] * 2,
        compiler_params=pltpu.CompilerParams(collective_id=2, has_side_effects=True, vmem_limit_bytes=VMEM_MOST),
    )(grads, small)


def rank_kernel(scale_ref, cls_ref, lang_row, lang_col, dc_ref, stats_ref, every, weights, z_s, z_r, pair_s, pair_r):
    s, z, y, c = place()
    sents, width = cls_ref.shape
    pairs = lang_row.shape[1]
    greet(s, z, y, c, "line")
    cls = cls_ref[...]
    root = lax.rsqrt(jnp.sum(cls * cls, axis=-1, keepdims=True) + NORM_EPS)
    unit = cls * root
    every[s, z, y, c] = unit.astype(jnp.bfloat16)

    def along(to, frm):
        return pltpu.make_async_remote_copy(
            src_ref=every.at[s, frm, y, c], dst_ref=every.at[s, frm, y, c], send_sem=z_s.at[to], recv_sem=z_r.at[frm],
            device_id=(s, batch_of(to, y, c)), device_id_type=MESH,
        )

    for to in range(ZS):

        @pl.when(z != to)
        def _():
            along(to, z).start()

    for frm in range(ZS):

        @pl.when(z != frm)
        def _():
            along(frm, frm).wait_recv()

    def swap(view, n, target):
        copy = pltpu.make_async_remote_copy(
            src_ref=view, dst_ref=view, send_sem=pair_s.at[n], recv_sem=pair_r.at[n], device_id=target,
            device_id_type=MESH,
        )
        copy.start()
        return copy

    first = swap(every.at[s, :, y, c], 0, (s, batch_of(z, 1 - y, c)))
    first.wait_recv()
    then = swap(every.at[s, :, :, c], 1, (1 - s, batch_of(z, y, c)))
    then.wait_recv()
    last = swap(every.at[:, :, :, c], 2, (s, batch_of(z, y, 1 - c)))
    last.wait_recv()
    scale = scale_ref[0]
    e_zero = every[0].reshape(pairs, width)
    e_one = every[1].reshape(pairs, width)
    cosines = lax.dot_general(e_zero, e_one, (((1,), (1,)), ((), ())), preferred_element_type=jnp.float32)
    own = lax.broadcasted_iota(jnp.int32, (pairs, pairs), 0) == lax.broadcasted_iota(jnp.int32, (pairs, pairs), 1)
    same = lang_col[...] == lang_row[...]
    diagonal = jnp.where(own, 1.0, 0.0)
    shifted = cosines - MARGIN * diagonal
    logits = scale * shifted
    masked = jnp.where(same, logits, -1e30)
    both = -2.0 * diagonal
    total = -2.0 * jnp.sum(logits * diagonal)
    for axis in range(2):
        top = jnp.max(masked, axis=axis, keepdims=True)
        grown = jnp.where(same, jnp.exp(masked - top), 0.0)
        summed = jnp.sum(grown, axis=axis, keepdims=True)
        both += grown / summed
        total += jnp.sum(jnp.log(summed) + top)
    line = lax.broadcasted_iota(jnp.int32, stats_ref.shape, 0)
    stats_ref[...] = jnp.where(line == 0, total, jnp.sum(both * shifted))
    weights[0] = both
    weights[1] = both.T
    rows = weights[s, pl.ds(pl.multiple_of(batch_of(z, y, c) * sents, 16), sents), :]
    partners = every[1 - s].reshape(pairs, width)
    high = rows.astype(jnp.bfloat16)
    rest = (rows - high.astype(jnp.float32)).astype(jnp.bfloat16)
    mix = (((1,), (0,)), ((), ()))
    de = lax.dot_general(high, partners, mix, preferred_element_type=jnp.float32)
    de += lax.dot_general(rest, partners, mix, preferred_element_type=jnp.float32)
    de = scale * de
    dc_ref[...] = (de - unit * jnp.sum(unit * de, axis=-1, keepdims=True)) * root
    for to in range(ZS):

        @pl.when(z != to)
        def _():
            along(to, z).wait_send()

    first.wait_send()
    then.wait_send()
    last.wait_send()


def rank_loss(cls, scale, langs):
    sents, width = cls.shape
    pairs = langs.shape[0]
    dma = pltpu.SemaphoreType.DMA
    vmem = pl.BlockSpec(memory_space=pltpu.VMEM)
    return pl.pallas_call(
        rank_kernel,
        name="rank_loss",
        out_shape=[jax.ShapeDtypeStruct((sents, width), jnp.float32), jax.ShapeDtypeStruct((8, 128), jnp.float32)],
        in_specs=[pl.BlockSpec(memory_space=pltpu.SMEM), vmem, vmem, vmem],
        out_specs=[vmem, vmem],
        scratch_shapes=[
            pltpu.VMEM((2, ZS, 2, 2, sents, width), jnp.bfloat16),
            pltpu.VMEM((2, pairs, pairs), jnp.float32),
            dma((ZS,)), dma((ZS,)), dma((3,)), dma((3,)),
        ],
        compiler_params=pltpu.CompilerParams(collective_id=1, has_side_effects=True, vmem_limit_bytes=24 << 20),
    )(scale, cls, langs.reshape(1, pairs), langs.reshape(pairs, 1))


TILE = 256
GROUP = LEN_ROWS


def dot_nn(a, b):
    return lax.dot_general(a, b, (((1,), (0,)), ((), ())), preferred_element_type=jnp.float32)


def dot_nt(a, b):
    return lax.dot_general(a, b, (((1,), (1,)), ((), ())), preferred_element_type=jnp.float32)


def dot_tn(a, b):
    return lax.dot_general(a, b, (((0,), (0,)), ((), ())), preferred_element_type=jnp.float32)


def gelu_parts(u):
    t = 1.0 / (1.0 + (0.3275911 * 0.7071067811865476) * jnp.abs(u))
    bell = jnp.exp(-0.5 * u * u)
    tail = t * (
        0.127414796 + t * (-0.142248368 + t * (0.7107068705 + t * (-0.7265760135 + t * 0.5307027145)))
    ) * bell
    phi_sum = jnp.where(u >= 0.0, 1.0 - tail, tail)
    return u * phi_sum, phi_sum + u * (0.3989422804014327 * bell)


def norm_parts(resid):
    centre = jnp.mean(resid, axis=-1, keepdims=True)
    centred = resid - centre
    rs = lax.rsqrt(jnp.mean(centred * centred, axis=-1, keepdims=True) + NORM_EPS)
    return centred * rs, rs


def norm_back(dy, unit, rs, gain):
    gd = gain * dy
    return rs * (gd - jnp.mean(gd, axis=-1, keepdims=True) - unit * jnp.mean(gd * unit, axis=-1, keepdims=True))


def lane_halves():
    lane = lax.broadcasted_iota(jnp.int32, (1, 2 * HD), 1)
    first = jnp.where(lane < HD, 1.0, 0.0)
    return first.astype(jnp.bfloat16), (1.0 - first).astype(jnp.bfloat16), lane < HD


def both_heads(rows, first, second):
    return jnp.concatenate([rows * first, rows * second], axis=0)


def fetch_all(pos_ref, units_hbm, held, sems, edges, order):
    for m in order:
        for u in range(edges[m], edges[m + 1]):
            pltpu.make_async_copy(units_hbm.at[pos_ref[u]], held.at[u], sems.at[m]).start()


def fetch_wait(units_hbm, held, sems, edges, m):
    lo, hi = edges[m], edges[m + 1]
    pltpu.make_async_copy(units_hbm.at[pl.ds(0, hi - lo)], held.at[pl.ds(lo, hi - lo)], sems.at[m]).wait()


def matrix_of(held, lo, hi):
    block = held[lo:hi]
    return block.reshape((hi - lo) * block.shape[1], block.shape[2])


def forward_kernel(
    edges, pos_ref, x_ref, small_ref, units_hbm,
    out_ref, q_ref, k_ref, v_ref, probs_ref, ctx_ref, n1_ref, rs1_ref, hb_ref, act_ref, slope_ref, n2_ref, rs2_ref,
    cls_ref, held, sems,
):
    first_tile = pl.program_id(0) == 0
    width = x_ref.shape[1]

    def need(m):
        @pl.when(first_tile)
        def _():
            fetch_wait(units_hbm, held, sems, edges, m)

    @pl.when(first_tile)
    def _():
        fetch_all(pos_ref, units_hbm, held, sems, edges, range(6))

    inner_rows = FF // width
    row = lambda r: small_ref[r : r + 1, :]
    x = x_ref[...]
    need(0)
    q = (dot_nn(x, matrix_of(held, edges[0], edges[1])) + row(0)).astype(jnp.bfloat16)
    q_ref[...] = q
    need(1)
    k = dot_nn(x, matrix_of(held, edges[1], edges[2])).astype(jnp.bfloat16)
    k_ref[...] = k
    need(2)
    v = (dot_nn(x, matrix_of(held, edges[2], edges[3])) + row(1)).astype(jnp.bfloat16)
    v_ref[...] = v
    first, second, is_first = lane_halves()
    for sent in range(TILE // GROUP):
        rows = slice(sent * GROUP, (sent + 1) * GROUP)
        for pair in range(H // 2):
            lanes = slice(pair * 2 * HD, (pair + 1) * 2 * HD)
            qq = both_heads(q[rows, lanes], first, second)
            scores = dot_nt(k[rows, lanes], qq) * HD ** (-0.5)
            scores = scores - jnp.max(scores, axis=0, keepdims=True)
            grown = jnp.exp(scores)
            probs = (grown * (1.0 / jnp.sum(grown, axis=0, keepdims=True))).astype(jnp.bfloat16)
            probs_ref[sent, pair] = probs
            mixed = dot_tn(probs, v[rows, lanes])
            ctx_ref[rows, lanes] = jnp.where(is_first, mixed[:GROUP], mixed[GROUP:]).astype(jnp.bfloat16)
    need(3)
    attended = dot_nn(ctx_ref[...], matrix_of(held, edges[3], edges[4])) + row(2)
    n1, rs1 = norm_parts(x.astype(jnp.float32) + attended)
    n1_ref[...] = n1
    rs1_ref[...] = rs1
    h1 = n1 * row(4 + inner_rows) + row(5 + inner_rows)
    hb = h1.astype(jnp.bfloat16)
    hb_ref[...] = hb
    need(4)
    need(5)
    per = (edges[5] - edges[4]) // inner_rows
    total = h1 + row(3 + inner_rows)
    for part in range(inner_rows):
        cols = slice(part * width, (part + 1) * width)
        w_in = matrix_of(held, edges[4] + part * per, edges[4] + (part + 1) * per)
        u = dot_nt(hb, w_in) + row(3 + part)
        value, slope = gelu_parts(u)
        act = value.astype(jnp.bfloat16)
        act_ref[:, cols] = act
        slope_ref[:, cols] = slope.astype(jnp.bfloat16)
        total += dot_nn(act, matrix_of(held, edges[5] + part * per, edges[5] + (part + 1) * per))
    n2, rs2 = norm_parts(total)
    n2_ref[...] = n2
    rs2_ref[...] = rs2
    y = n2 * row(6 + inner_rows) + row(7 + inner_rows)
    out_ref[...] = y.astype(jnp.bfloat16)
    for sent in range(TILE // GROUP):
        cls_ref[0, sent : sent + 1, :] = y[sent * GROUP : sent * GROUP + 1, :]


def tiles(shape):
    rest = len(shape) - 1
    return pl.BlockSpec((TILE,) + tuple(shape[1:]), lambda i, *_: (i,) + (0,) * rest)


def whole(shape):
    return pl.BlockSpec(tuple(shape), lambda i, *_: (0,) * len(shape))


def run_forward(x, small, units, positions, edges):
    rows, width = x.shape
    count = rows // TILE
    sents = TILE // GROUP
    bf, f32 = jnp.bfloat16, jnp.float32
    probs_shape = (rows // GROUP, H // 2, GROUP, 2 * HD)
    outs = [
        ((rows, width), bf), ((rows, width), bf), ((rows, width), bf), ((rows, width), bf), (probs_shape, bf),
        ((rows, width), bf), ((rows, width), f32), ((rows, 1), f32), ((rows, width), bf), ((rows, FF), bf),
        ((rows, FF), bf), ((rows, width), f32), ((rows, 1), f32), ((count, sents, width), f32),
    ]
    specs = [tiles(shape) for shape, _ in outs]
    specs[4] = pl.BlockSpec((sents,) + probs_shape[1:], lambda i, *_: (i, 0, 0, 0))
    specs[13] = pl.BlockSpec((1, sents, width), lambda i, *_: (i, 0, 0))
    return pl.pallas_call(
        functools.partial(forward_kernel, edges),
        name="layer_forward",
        grid_spec=pltpu.PrefetchScalarGridSpec(
            num_scalar_prefetch=1,
            grid=(count,),
            in_specs=[tiles(x.shape), whole(small.shape), pl.BlockSpec(memory_space=pl.ANY)],
            out_specs=specs,
            scratch_shapes=[pltpu.VMEM((edges[6],) + units.shape[1:], bf), pltpu.SemaphoreType.DMA((6,))],
        ),
        out_shape=[jax.ShapeDtypeStruct(shape, kind) for shape, kind in outs],
        compiler_params=pltpu.CompilerParams(vmem_limit_bytes=VMEM_MOST),
    )(positions, x, small, units)


def backward_kernel(
    edges, pos_ref, og_ref, dc_ref, small_ref, q_ref, k_ref, v_ref, probs_ref, n1_ref, rs1_ref, slope_ref, n2_ref,
    rs2_ref, units_hbm,
    dx_ref, df_ref, du_ref, da_ref, dq_ref, dk_ref, dv_ref, gsmall_ref, dy_ref, dctx_ref, held, sems,
):
    first_tile = pl.program_id(0) == 0
    width = og_ref.shape[1]
    inner_rows = FF // width

    def need(m):
        @pl.when(first_tile)
        def _():
            fetch_wait(units_hbm, held, sems, edges, m)

    @pl.when(first_tile)
    def _():
        fetch_all(pos_ref, units_hbm, held, sems, edges, (5, 4, 3, 0, 1, 2))
        gsmall_ref[...] = jnp.zeros_like(gsmall_ref)

    row = lambda r: small_ref[r : r + 1, :]

    def add_small(r, values):
        gsmall_ref[r : r + 1, :] += jnp.sum(values.astype(jnp.float32), axis=0, keepdims=True)

    dy_ref[...] = og_ref[...].astype(jnp.float32)
    for sent in range(TILE // GROUP):
        dy_ref[sent * GROUP : sent * GROUP + 1, :] += dc_ref[0, sent : sent + 1, :]
    dy = dy_ref[...]
    n2 = n2_ref[...]
    add_small(6 + inner_rows, dy * n2)
    add_small(7 + inner_rows, dy)
    dr2 = norm_back(dy, n2, rs2_ref[...], row(6 + inner_rows))
    df = dr2.astype(jnp.bfloat16)
    df_ref[...] = df
    add_small(3 + inner_rows, df)
    need(5)
    need(4)
    per = (edges[5] - edges[4]) // inner_rows
    dh1 = dr2
    for part in range(inner_rows):
        cols = slice(part * width, (part + 1) * width)
        da = dot_nt(df, matrix_of(held, edges[5] + part * per, edges[5] + (part + 1) * per))
        du = (da * slope_ref[:, cols].astype(jnp.float32)).astype(jnp.bfloat16)
        du_ref[:, cols] = du
        add_small(3 + part, du)
        dh1 += dot_nn(du, matrix_of(held, edges[4] + part * per, edges[4] + (part + 1) * per))
    n1 = n1_ref[...]
    add_small(4 + inner_rows, dh1 * n1)
    add_small(5 + inner_rows, dh1)
    dr1 = norm_back(dh1, n1, rs1_ref[...], row(4 + inner_rows))
    dattn = dr1.astype(jnp.bfloat16)
    da_ref[...] = dattn
    add_small(2, dattn)
    need(3)
    dctx_ref[...] = dot_nt(dattn, matrix_of(held, edges[3], edges[4])).astype(jnp.bfloat16)
    first, second, is_first = lane_halves()
    for sent in range(TILE // GROUP):
        rows = slice(sent * GROUP, (sent + 1) * GROUP)
        for pair in range(H // 2):
            lanes = slice(pair * 2 * HD, (pair + 1) * 2 * HD)
            dcc = both_heads(dctx_ref[rows, lanes], first, second)
            qq = both_heads(q_ref[rows, lanes], first, second)
            low = probs_ref[sent, pair]
            probs = low.astype(jnp.float32)
            dprobs = dot_nt(v_ref[rows, lanes], dcc)
            dscores = probs * (dprobs - jnp.sum(dprobs * probs, axis=0, keepdims=True))
            dscores = dscores.astype(jnp.bfloat16)
            dv_ref[rows, lanes] = dot_nn(low, dcc).astype(jnp.bfloat16)
            dk_ref[rows, lanes] = (dot_nn(dscores, qq) * HD ** (-0.5)).astype(jnp.bfloat16)
            mixed = dot_tn(dscores, k_ref[rows, lanes]) * HD ** (-0.5)
            dq_ref[rows, lanes] = jnp.where(is_first, mixed[:GROUP], mixed[GROUP:]).astype(jnp.bfloat16)
    dx = dr1
    for m, (ref, r) in enumerate(((dq_ref, 0), (dk_ref, None), (dv_ref, 1))):
        need(m)
        rows = ref[...]
        if r is not None:
            add_small(r, rows)
        dx += dot_nt(rows, matrix_of(held, edges[m], edges[m + 1]))
    dx_ref[...] = dx.astype(jnp.bfloat16)


def run_backward(og, dc, small, saved, units, positions, edges):
    rows, width = og.shape
    count = rows // TILE
    sents = TILE // GROUP
    bf, f32 = jnp.bfloat16, jnp.float32
    _, q, k, v, probs, _, n1, rs1, _, _, slope, n2, rs2, _ = saved
    ins = [og, dc, small, q, k, v, probs, n1, rs1, slope, n2, rs2]
    in_specs = [tiles(a.shape) for a in ins]
    in_specs[1] = pl.BlockSpec((1, sents, width), lambda i, *_: (i, 0, 0))
    in_specs[2] = whole(small.shape)
    in_specs[6] = pl.BlockSpec((sents,) + probs.shape[1:], lambda i, *_: (i, 0, 0, 0))
    outs = [((rows, width), bf)] * 2 + [((rows, FF), bf)] + [((rows, width), bf)] * 4 + [(small.shape, f32)]
    specs = [tiles(shape) for shape, _ in outs]
    specs[7] = whole(small.shape)
    return pl.pallas_call(
        functools.partial(backward_kernel, edges),
        name="layer_backward",
        grid_spec=pltpu.PrefetchScalarGridSpec(
            num_scalar_prefetch=1,
            grid=(count,),
            in_specs=in_specs + [pl.BlockSpec(memory_space=pl.ANY)],
            out_specs=specs,
            scratch_shapes=[
                pltpu.VMEM((TILE, width), f32),
                pltpu.VMEM((TILE, width), bf),
                pltpu.VMEM((edges[6],) + units.shape[1:], bf),
                pltpu.SemaphoreType.DMA((6,)),
            ],
        ),
        out_shape=[jax.ShapeDtypeStruct(shape, kind) for shape, kind in outs],
        compiler_params=pltpu.CompilerParams(vmem_limit_bytes=VMEM_MOST),
    )(positions, *ins, units)


def weight_grad_kernel(
    edges, pos_ref, x_hbm, ctx_hbm, du_hbm, act_hbm, dq_hbm, dk_hbm, dv_hbm, da_hbm, hb_hbm, df_hbm, out_hbm,
    x_v, ctx_v, du_v, act_v, right, staged, sems, out_sems,
):
    width = x_v.shape[1]
    unit_rows = out_hbm.shape[1]
    inner_rows = FF // width
    loads = [(act_hbm, act_v), (df_hbm, right.at[5]), (du_hbm, du_v), (hb_hbm, right.at[4]), (ctx_hbm, ctx_v),
             (da_hbm, right.at[3]), (x_hbm, x_v), (dq_hbm, right.at[0]), (dk_hbm, right.at[1]), (dv_hbm, right.at[2])]
    copies = [pltpu.make_async_copy(src, dst, sems.at[i]) for i, (src, dst) in enumerate(loads)]
    for copy in copies:
        copy.start()
    waited = set()
    per = width // unit_rows
    work = []
    for part in range(inner_rows):
        work.append((act_v, part, 5, edges[5] + part * per, (0, 1)))
    for part in range(inner_rows):
        work.append((du_v, part, 4, edges[4] + part * per, (2, 3)))
    work.append((ctx_v, 0, 3, edges[3], (4, 5)))
    work.append((x_v, 0, 0, edges[0], (6, 7)))
    work.append((x_v, 0, 1, edges[1], (6, 8)))
    work.append((x_v, 0, 2, edges[2], (6, 9)))
    for step, (left, part, m, unit, needs) in enumerate(work):
        slot = step % 2
        for n in needs:
            if n not in waited:
                copies[n].wait()
                waited.add(n)
        if step >= 2:
            pltpu.make_async_copy(out_hbm.at[pl.ds(0, per)], staged.at[slot], out_sems.at[slot]).wait()
        half = per // 2
        for piece in range(2):
            cols = slice(part * width + piece * half * unit_rows, part * width + (piece + 1) * half * unit_rows)
            block = dot_tn(left[:, cols], right[m]).astype(jnp.bfloat16)
            staged[slot, piece * half : (piece + 1) * half] = block.reshape(half, unit_rows, width)
        for n in range(per):
            pltpu.make_async_copy(staged.at[slot, n], out_hbm.at[pos_ref[unit + n]], out_sems.at[slot]).start()
    for slot in range(2):
        pltpu.make_async_copy(out_hbm.at[pl.ds(0, per)], staged.at[slot], out_sems.at[slot]).wait()


def run_weight_grads(x, saved, back, positions, edges, places, unit_rows):
    rows, width = x.shape
    bf = jnp.bfloat16
    ctx, hb, act = saved[5], saved[8], saved[9]
    _, df, du, da, dq, dk, dv, _ = back
    per = width // unit_rows
    anyw = pl.BlockSpec(memory_space=pl.ANY)
    return pl.pallas_call(
        functools.partial(weight_grad_kernel, edges),
        name="weight_grads",
        in_specs=[pl.BlockSpec(memory_space=pltpu.SMEM)] + [anyw] * 10,
        out_specs=anyw,
        scratch_shapes=[
            pltpu.VMEM((rows, width), bf), pltpu.VMEM((rows, width), bf), pltpu.VMEM((rows, FF), bf),
            pltpu.VMEM((rows, FF), bf), pltpu.VMEM((6, rows, width), bf),
            pltpu.VMEM((2, per, unit_rows, width), bf),
            pltpu.SemaphoreType.DMA((10,)), pltpu.SemaphoreType.DMA((2,)),
        ],
        out_shape=jax.ShapeDtypeStruct((places, unit_rows, width), bf),
        compiler_params=pltpu.CompilerParams(vmem_limit_bytes=VMEM_MOST),
    )(positions, x, ctx, du, act, dq, dk, dv, da, hb, df)


def unit_positions(owner_list, slot_count):
    unit_total = owner_list.shape[0]
    same_owner = owner_list[:, None] == owner_list[None, :]
    ordinal = jnp.arange(unit_total, dtype=jnp.int32)
    earlier = ordinal[None, :] < ordinal[:, None]
    slot_number = jnp.sum(jnp.where(same_owner & earlier, 1, 0), axis=1).astype(jnp.int32)
    return owner_list * slot_count + slot_number


def adamw(weight_in, gradient, moment_one, moment_two, rate_value, decay_value, fix_one, fix_two):
    new_one = BETA_ONE * moment_one + (1.0 - BETA_ONE) * gradient
    new_two = BETA_TWO * moment_two + (1.0 - BETA_TWO) * gradient * gradient
    stepped = new_one / fix_one / (jnp.sqrt(new_two / fix_two) + ADAM_EPS)
    return (weight_in - rate_value * (stepped + decay_value * weight_in), new_one, new_two)


def any_size_units(own, positions, owners):
    slots, rows, width = own.shape
    table = jnp.arange(owners * slots, dtype=jnp.int32)[:, None] == positions[None, :]
    bands = lax.all_to_all(
        own.transpose(1, 0, 2).astype(jnp.bfloat16), "batch", split_axis=0, concat_axis=1, tiled=True
    )
    ordered = jnp.einsum(
        "rpd,pu->rud", bands, table.astype(jnp.bfloat16), preferred_element_type=jnp.float32
    ).astype(jnp.bfloat16)
    return lax.all_gather(ordered, "batch", axis=0, tiled=True).transpose(1, 0, 2)


def any_size_sums(grads, positions, owners, slots):
    table = jnp.arange(owners * slots, dtype=jnp.int32)[:, None] == positions[None, :]
    pieces = lax.psum_scatter(grads.transpose(1, 0, 2).astype(jnp.float32), "batch", scatter_dimension=0, tiled=True)
    summed = lax.psum(pieces.astype(jnp.bfloat16), "stream").astype(jnp.float32)
    send_rows = jnp.einsum("rud,pu->rpd", summed, table.astype(jnp.float32), precision=HIGHEST)
    owned = lax.all_to_all(send_rows.astype(jnp.bfloat16), "batch", split_axis=1, concat_axis=0, tiled=True)
    return owned.astype(jnp.float32).transpose(1, 0, 2)


def any_size_rank(cls, scale, langs, owners):
    sents, width = cls.shape
    root = lax.rsqrt(jnp.sum(cls * cls, axis=-1, keepdims=True) + NORM_EPS)
    unit = cls * root
    every = lax.all_gather(unit.astype(jnp.bfloat16), "batch", axis=0, tiled=True)
    every = lax.all_gather(every, "stream", axis=0)
    cosines = jnp.dot(every[0], every[1].T, preferred_element_type=jnp.float32)
    diagonal = jnp.eye(cosines.shape[0], dtype=jnp.float32)
    same = langs[:, None] == langs[None, :]
    shifted = cosines - MARGIN * diagonal
    logits = scale[0] * shifted
    masked = jnp.where(same, logits, -1e30)
    both = -2.0 * diagonal
    total = -2.0 * jnp.sum(logits * diagonal)
    for axis in range(2):
        top = jnp.max(masked, axis=axis, keepdims=True)
        grown = jnp.where(same, jnp.exp(masked - top), 0.0)
        summed = jnp.sum(grown, axis=axis, keepdims=True)
        both += grown / summed
        total += jnp.sum(jnp.log(summed) + top)
    s = lax.axis_index("stream")
    turned = jnp.where(s == 0, both, both.T)
    rows = lax.dynamic_slice_in_dim(turned, lax.axis_index("batch") * sents, sents)
    partners = lax.dynamic_index_in_dim(every, 1 - s, keepdims=False).astype(jnp.float32)
    de = scale[0] * jnp.dot(rows, partners, precision=HIGHEST)
    dc = (de - unit * jnp.sum(unit * de, axis=-1, keepdims=True)) * root
    return dc, total, jnp.sum(both * shifted)


def per_device(
    tokens, out_grad, master, first_moment, second_moment, small_params, small_first, small_second, logit_scale,
    scale_first, scale_second, pair_lang, unit_owner,
):
    owners = lax.axis_size("batch")
    here_batch = lax.axis_index("batch")
    unit_rows, slot_count, width = master.shape
    query_blocks = width // unit_rows
    inner_blocks = FF // unit_rows
    edges = [query_blocks * n for n in range(5)]
    edges += [edges[4] + inner_blocks, edges[4] + 2 * inner_blocks]
    units_total = unit_owner.shape[0]
    positions = unit_positions(unit_owner, slot_count)
    on_block = owners == 4 * ZS
    own = master.transpose(1, 0, 2)
    if on_block:
        units, where, places = gather_units(own), positions, owners * slot_count
    else:
        units = any_size_units(own, positions, owners)
        where, places = jnp.arange(units_total, dtype=jnp.int32), units_total
    sentences, length = tokens.shape[1], tokens.shape[2]
    flat = tokens.reshape(sentences * length, width)
    saved = run_forward(flat, small_params, units, where, edges)
    cls = saved[13]
    if on_block:
        dc, stats = rank_loss(cls.reshape(sentences, width), logit_scale, pair_lang)
        loss_total, grad_scale = stats[0, :1], stats[1, :1]
    else:
        dc, loss_total, grad_scale = any_size_rank(cls.reshape(sentences, width), logit_scale, pair_lang, owners)
        loss_total, grad_scale = loss_total.reshape(1), grad_scale.reshape(1)
    back = run_backward(
        out_grad.reshape(sentences * length, width), dc.reshape(cls.shape), small_params, saved, units, where, edges
    )
    grads = run_weight_grads(flat, saved, back, where, edges, places, unit_rows)
    if on_block:
        owned_grad, small_total = reduce_units(grads, back[7], slot_count)
    else:
        owned_grad = any_size_sums(grads, positions, owners, slot_count)
        small_total = lax.psum(back[7], ("stream", "batch"))
    step_value = float(STEP)
    fix_one = 1.0 - BETA_ONE**step_value
    fix_two = 1.0 - BETA_TWO**step_value
    my_places = here_batch * slot_count + jnp.arange(slot_count, dtype=jnp.int32)
    filled = jnp.any(my_places[:, None] == positions[None, :], axis=1)[:, None, None]
    first_in, second_in = first_moment.transpose(1, 0, 2), second_moment.transpose(1, 0, 2)
    moved = adamw(own, owned_grad, first_in, second_in, RATE_UNITS, DECAY, fix_one, fix_two)
    new_master, new_first, new_second = (
        jnp.where(filled, new, old) for new, old in zip(moved, (own, first_in, second_in))
    )
    new_copy = new_master.astype(jnp.bfloat16)
    new_small, new_small_first, new_small_second = adamw(
        small_params, small_total, small_first, small_second, RATE_SMALL, 0.0, fix_one, fix_two
    )
    scale_new, scale_one, scale_two = adamw(
        logit_scale, grad_scale, scale_first, scale_second, RATE_SCALE, 0.0, fix_one, fix_two
    )
    loss_out = loss_total / (2 * owners * sentences)
    back_order = lambda a: a.transpose(1, 0, 2)
    return (
        saved[0].reshape(tokens.shape),
        back[0].reshape(tokens.shape),
        back_order(new_master),
        back_order(new_first),
        back_order(new_second),
        back_order(new_copy),
        new_small,
        new_small_first,
        new_small_second,
        scale_new,
        scale_one,
        scale_two,
        loss_out,
    )


def solution(mesh):
    rows = P("stream", "batch", None, None)
    blocks = P(None, "batch", None)
    return jax.shard_map(
        per_device,
        mesh=mesh,
        in_specs=(rows, rows, blocks, blocks, blocks) + (P(),) * 8,
        out_specs=(rows, rows, blocks, blocks, blocks, blocks) + (P(),) * 7,
        check_vma=False,
    )
```

time: 1050 us -> 362 us (0.34)
  waiting for transfers between devices: 466 us -> 0 us
  Pallas kernels: 0 us -> 331 us
  local copies, waits for them, and re-layouts: 249 us -> 9.19 us
  matrix products: 183 us -> 0 us
  blocking collectives: 60.2 us -> 0 us
  other arithmetic: 42.5 us -> 10.9 us
  starting transfers between devices: 15.8 us -> 0 us
  between operations: 24.2 us -> 9.95 us
    pallas_call x0 -> x6, Pallas kernels: none -> 331 us  [the longest x1 114 us: reduce_units(): pl.pallas_call(reduce_kernel, name='reduce_units', out_shape=[jax.ShapeDt...]
    reduce_scatter x2 -> x0, waiting for transfers between devices: 323 us -> none  [the longest x1 266 us: per_device(): lax.psum_scatter(jnp.concatenate([jnp.concatenate([outer_rows(flat_blocks...]
    dot_general x29 -> x0, matrix products: 183 us -> none  [the longest x6 76.7 us: project_back(): jnp.einsum('td,rkd->tkr', operand, weight, preferred_element_type=jnp.flo...]
    concatenate x2 -> x0, local copies, waits for them, and re-layouts: 117 us -> none  [the longest x1 117 us: per_device(): jnp.concatenate([jnp.concatenate([outer_rows(flat_blocks, d_queries), out...]
    all_gather x1 -> x0, waiting for transfers between devices: 107 us -> none  [per_device(): all_units = lax.all_gather(own_pieces, 'batch', axis=0, tiled=True)]
    reshape x19 -> x3, local copies, waits for them, and re-layouts: 55.5 us -> 1.59 us  [the longest x1 0.82 us: per_device(): dc, stats = rank_loss(cls.reshape(sentences, width), logit_scale, pair_lang)]
    psum x1 -> x0, blocking collectives: 41.8 us -> none  [per_device(): lax.psum((small_grad_local, grad_scale.reshape(1), loss_local.reshape(1))...]
    all_to_all x2 -> x0, waiting for transfers between devices: 34.6 us -> none  [the longest x1 34.5 us: per_device(): lax.all_to_all(master.astype(jnp.bfloat16), 'batch', split_axis=0, concat...]
  transfers between devices with their start and end apart: 8 -> 0, of which waited for: 5 -> 0; matrix products, arithmetic and copies ran while one was open for 5% -> 0% of each run, Pallas kernels for 0% -> 0%
where the time goes in v1:
time: 362 us; the launch traced here: 361 us
  Pallas kernels  331 us (91%)
  other arithmetic  10.9 us (3%)
  between operations  9.95 us (3%)
  local copies, waits for them, and re-layouts  9.19 us (3%)
    pallas_call x1, Pallas kernels, reduce_units(): pl.pallas_call(reduce_kernel, name='reduce_units', out_shape=[jax.ShapeDt...  114 us
    pallas_call x1, Pallas kernels, gather_units(): pl.pallas_call(gather_kernel, name='gather_units', out_shape=jax.ShapeDty...  70.9 us
    pallas_call x1, Pallas kernels, run_forward(): pl.pallas_call(functools.partial(forward_kernel, edges), name='layer_forw...  56.6 us
    pallas_call x1, Pallas kernels, run_backward(): pl.pallas_call(functools.partial(backward_kernel, edges), name='layer_bac...  48.2 us
    pallas_call x1, Pallas kernels, run_weight_grads(): pl.pallas_call(functools.partial(weight_grad_kernel, edges), name='weight...  22.2 us
    pallas_call x1, Pallas kernels, rank_loss(): pl.pallas_call(rank_kernel, name='rank_loss', out_shape=[jax.ShapeDtypeSt...  19 us
    transpose x1, other arithmetic, per_device(): back_order = lambda a: a.transpose(1, 0, 2)  7.91 us

profile of v1, /device:TPU:8, one launch (start us, length us, event | category | flops | bytes accessed | tf_op | source)
XLA Modules:
  0.0 360.7 jit_solution(11911595608625690688)
XLA Ops:
  0.6 0.9 select_reduce_fusion
  1.6 1.2 multiply_add_fusion.1.pos_ref
  2.7 0.0 copy-start.1
  2.7 1.5 copy-done.1
  4.3 70.9 %gather_units.1.units_hbm = bf16[80,128,768]{2,1,0:T(8,128)(2,1)S(1)} custom-call(f32[5,128,768]{2,1,0:T(8,128)S(1)} %bitcast.42), custom_call_target="tpu_custom_call" | custom-call | tf_op jit(solution)/shard_map/gather_units/pallas_call | solution.py:290
  75.2 0.0 copy-start
  75.2 5.5 %copy-done = bf16[80,128,768]{2,1,0:T(8,128)(2,1)} copy-done((bf16[80,128,768]{2,1,0:T(8,128)(2,1)}, bf16[80,128,768]{2,1,0:T(8,128)(2,1)S(1)}, u32[]{:S(2)}) %copy-start) | copy-done | bytes 15728664
  80.7 0.0 copy-start.3
  80.7 56.6 %layer_forward.1 = (bf16[1024,768]{1,0:T(8,128)(2,1)}, bf16[1024,768]{1,0:T(8,128)(2,1)}, bf16[1024,768]{1,0:T(8,128)(2,1)}, bf16[1024,768]{1,0:T(8,128)(2,1)}, ...) custom-call(s32[72]{0:T(128)} %multiply_add_fusion.1.pos_ref, ...), custom_call_target="tpu_custom_call" | custom-call | tf_op jit(solution)/shard_map/layer_forward/pallas_call | solution.py:785
  137.3 0.8 reshape.63.cls_ref
  138.8 0.0 copy-done.3
  138.8 0.1 copy.27.lang_col
  139.0 19.0 %rank_loss.1 = (f32[16,768]{1,0:T(8,128)S(1)}, f32[8,128]{1,0:T(8,128)S(1)}) custom-call(f32[1]{0:T(128)S(6)} %copy.28.scale_ref, f32[16,768]{1,0:T(8,128)S(1)} %reshape.63.cls_ref, s32[1,256]{1,0:T(1,128)S(1)} %bitcast.44, s32[256,1]{1,0:T(8,128)S(1)} %copy.27.lang_col), custom_call_target="tpu_custom_call" | custom-call | tf_op jit(solution)/shard_map/rank_loss/pallas_call | solution.py:611
  158.0 0.6 reshape.66.dc_ref
  158.6 48.2 %layer_backward.1 = (bf16[1024,768]{1,0:T(8,128)(2,1)}, bf16[1024,768]{1,0:T(8,128)(2,1)}, bf16[1024,3072]{1,0:T(8,128)(2,1)}, bf16[1024,768]{1,0:T(8,128)(2,1)}...) custom-call(s32[72]{0:T(128)} %multiply_add_fusion.1.pos_ref, ...), custom_call_target="tpu_custom_call" | custom-call | tf_op jit(solution)/shard_map/layer_backward/pallas_call | solution.py:895
  206.8 22.2 %weight_grads.1.g_ref = bf16[80,128,768]{2,1,0:T(8,128)(2,1)} custom-call(s32[72]{0:T(128)} %multiply_add_fusion.1.pos_ref, bf16[1024,768]{1,0:T(8,128)(2,1)} %bitcast.46, bf16[1024,768]{1,0:T(8,128)(2,1)} %get-tuple-element.52.ctx_hbm, bf16[1024,3072]{1,0:T(8,128)(2,1)} %get-tuple-element.53.du_hbm, bf16[1024,3072]{1,0:T(8,128)(2,1)} %get-tuple-element.54.act_hbm, ...), custom_call_target="tpu_custom_call" | custom-call | tf_op jit(solution)/shard_map/weight_grads/pallas_call | solution.py:964
  229.0 0.0 copy-start.8
  229.0 0.0 copy-start.2
  229.1 113.8 %reduce_units.1 = (f32[5,128,768]{2,1,0:T(8,128)}, f32[12,768]{1,0:T(8,128)}) custom-call(bf16[80,128,768]{2,1,0:T(8,128)(2,1)} %weight_grads.1.g_ref, f32[12,768]{1,0:T(8,128)} %get-tuple-element.61.small_ref), custom_call_target="tpu_custom_call" | custom-call | tf_op jit(solution)/shard_map/reduce_units/pallas_call | solution.py:498
  342.9 0.0 copy-done.8
  342.9 0.2 compare_reduce_fusion
  343.1 0.0 copy-done.2
  343.1 0.0 copy-start.4
  343.1 0.0 copy-start.5
  343.1 0.0 copy-start.6
  343.1 0.0 copy-start.7
  343.1 7.9 %convert_bitcast_fusion = (bf16[128,5,768]{2,0,1:T(8,128)(2,1)}, f32[5,128,768]{2,1,0:T(8,128)}, f32[128,5,768]{2,0,1:T(8,128)}, f32[128,5,768]{2,0,1:T(8,128)}) fusion(f32[5,128,768]{2,1,0:T(8,128)} %get-tuple-element.62, f32[128,5,768]{2,0,1:T(8,128)} %param.17, f32[128,5,768]{2,0,1:T(8,128)} %param.16, f32[128,5,768]{2,0,1:T(8,128)S(1)} %copy-done.2, ...), kind=kLoop, calls=%fused_computation.10 | loop fusion | flops 9338880 | bytes 14745605 | tf_op jit(solution)/shard_map/transpose | solution.py:1103
  351.0 0.0 copy-done.4
  351.0 0.0 copy-done.5
  351.0 0.0 copy-done.6
  351.1 0.0 copy-done.7
  351.1 0.7 multiply_subtract_fusion
  351.7 0.5 fusion.7
  (1 shorter events, 0.0 us)
Async XLA Ops:
  2.7 1.5 copy-start.1
  75.2 5.5 %copy-start = (bf16[80,128,768]{2,1,0:T(8,128)(2,1)}, bf16[80,128,768]{2,1,0:T(8,128)(2,1)S(1)}, u32[]{:S(2)}) copy-start(bf16[80,128,768]{2,1,0:T(8,128)(2,1)S(1)} %gather_units.1.units_hbm) | copy-start | bytes 47185924
  80.7 58.1 %copy-start.3 = (s32[256]{0:T(256)S(1)}, s32[256]{0:T(256)}, u32[]{:S(2)}) copy-start(s32[256]{0:T(256)} %param.24) | copy-start | bytes 3076
  229.0 113.9 %copy-start.8 = (s32[72]{0:T(128)S(1)}, s32[72]{0:T(128)}, u32[]{:S(2)}) copy-start(s32[72]{0:T(128)} %multiply_add_fusion.1.pos_ref) | copy-start | bytes 868
  229.0 114.0 %copy-start.2 = (f32[128,5,768]{2,0,1:T(8,128)S(1)}, f32[128,5,768]{2,0,1:T(8,128)}, u32[]{:S(2)}) copy-start(f32[128,5,768]{2,0,1:T(8,128)} %param.15) | copy-start | bytes 5898244
  343.1 8.0 %copy-start.4 = (f32[12,768]{1,0:T(8,128)S(1)}, f32[12,768]{1,0:T(8,128)}, u32[]{:S(2)}) copy-start(f32[12,768]{1,0:T(8,128)} %small_ref.3) | copy-start | bytes 110596
  343.1 8.0 %copy-start.5 = (f32[12,768]{1,0:T(8,128)S(1)}, f32[12,768]{1,0:T(8,128)}, u32[]{:S(2)}) copy-start(f32[12,768]{1,0:T(8,128)} %param.19) | copy-start | bytes 110596
  343.1 7.9 %copy-start.6 = (f32[12,768]{1,0:T(8,128)S(1)}, f32[12,768]{1,0:T(8,128)}, u32[]{:S(2)}) copy-start(f32[12,768]{1,0:T(8,128)} %param.20) | copy-start | bytes 110596
  343.1 7.9 %copy-start.7 = (f32[12,768]{1,0:T(8,128)S(1)}, f32[12,768]{1,0:T(8,128)}, u32[]{:S(2)}) copy-start(f32[12,768]{1,0:T(8,128)} %get-tuple-element.63) | copy-start | bytes 110596

commit v2 on v1

--- a/solution.py
+++ b/solution.py
@@ -294,7 +294,7 @@
         in_specs=[pl.BlockSpec(memory_space=pltpu.VMEM)],
         out_specs=pl.BlockSpec(memory_space=pl.ANY),
         scratch_shapes=[pltpu.VMEM((slots, rows, width), jnp.bfloat16), pltpu.SemaphoreType.DMA((slots,))] + line + plane,
-        compiler_params=pltpu.CompilerParams(collective_id=0, has_side_effects=True, vmem_limit_bytes=24 << 20),
+        compiler_params=pltpu.CompilerParams(collective_id=0, has_side_effects=True, vmem_limit_bytes=VMEM_MOST),
     )(own)
 
 
@@ -717,18 +717,19 @@
     v = (dot_nn(x, matrix_of(held, edges[2], edges[3])) + row(1)).astype(jnp.bfloat16)
     v_ref[...] = v
     first, second, is_first = lane_halves()
-    for sent in range(TILE // GROUP):
-        rows = slice(sent * GROUP, (sent + 1) * GROUP)
-        for pair in range(H // 2):
-            lanes = slice(pair * 2 * HD, (pair + 1) * 2 * HD)
-            qq = both_heads(q[rows, lanes], first, second)
-            scores = dot_nt(k[rows, lanes], qq) * HD ** (-0.5)
-            scores = scores - jnp.max(scores, axis=0, keepdims=True)
-            grown = jnp.exp(scores)
-            probs = (grown * (1.0 / jnp.sum(grown, axis=0, keepdims=True))).astype(jnp.bfloat16)
-            probs_ref[sent, pair] = probs
-            mixed = dot_tn(probs, v[rows, lanes])
-            ctx_ref[rows, lanes] = jnp.where(is_first, mixed[:GROUP], mixed[GROUP:]).astype(jnp.bfloat16)
+    every_pair = [slice(pair * 2 * HD, (pair + 1) * 2 * HD) for pair in range(H // 2)]
+    every_sent = [slice(sent * GROUP, (sent + 1) * GROUP) for sent in range(TILE // GROUP)]
+    for sent, rows in enumerate(every_sent):
+        scores = jnp.concatenate(
+            [dot_nt(k[rows, lanes], both_heads(q[rows, lanes], first, second)) for lanes in every_pair], axis=1
+        )
+        grown = jnp.exp((scores - jnp.max(scores, axis=0, keepdims=True)) * HD ** (-0.5))
+        probs = (grown * (1.0 / jnp.sum(grown, axis=0, keepdims=True))).astype(jnp.bfloat16)
+        probs_ref[sent] = probs
+        mixed = [dot_tn(probs[:, lanes], v[rows, lanes]) for lanes in every_pair]
+        ctx_ref[rows, :] = jnp.concatenate(
+            [jnp.where(is_first, m[:GROUP], m[GROUP:]) for m in mixed], axis=1
+        ).astype(jnp.bfloat16)
     need(3)
     attended = dot_nn(ctx_ref[...], matrix_of(held, edges[3], edges[4])) + row(2)
     n1, rs1 = norm_parts(x.astype(jnp.float32) + attended)
@@ -773,14 +774,14 @@
     count = rows // TILE
     sents = TILE // GROUP
     bf, f32 = jnp.bfloat16, jnp.float32
-    probs_shape = (rows // GROUP, H // 2, GROUP, 2 * HD)
+    probs_shape = (rows // GROUP, GROUP, width)
     outs = [
         ((rows, width), bf), ((rows, width), bf), ((rows, width), bf), ((rows, width), bf), (probs_shape, bf),
         ((rows, width), bf), ((rows, width), f32), ((rows, 1), f32), ((rows, width), bf), ((rows, FF), bf),
         ((rows, FF), bf), ((rows, width), f32), ((rows, 1), f32), ((count, sents, width), f32),
     ]
     specs = [tiles(shape) for shape, _ in outs]
-    specs[4] = pl.BlockSpec((sents,) + probs_shape[1:], lambda i, *_: (i, 0, 0, 0))
+    specs[4] = pl.BlockSpec((sents,) + probs_shape[1:], lambda i, *_: (i, 0, 0))
     specs[13] = pl.BlockSpec((1, sents, width), lambda i, *_: (i, 0, 0))
     return pl.pallas_call(
         functools.partial(forward_kernel, edges),
@@ -853,21 +854,28 @@
     need(3)
     dctx_ref[...] = dot_nt(dattn, matrix_of(held, edges[3], edges[4])).astype(jnp.bfloat16)
     first, second, is_first = lane_halves()
+    every_pair = [slice(pair * 2 * HD, (pair + 1) * 2 * HD) for pair in range(H // 2)]
     for sent in range(TILE // GROUP):
         rows = slice(sent * GROUP, (sent + 1) * GROUP)
-        for pair in range(H // 2):
-            lanes = slice(pair * 2 * HD, (pair + 1) * 2 * HD)
-            dcc = both_heads(dctx_ref[rows, lanes], first, second)
-            qq = both_heads(q_ref[rows, lanes], first, second)
-            low = probs_ref[sent, pair]
-            probs = low.astype(jnp.float32)
-            dprobs = dot_nt(v_ref[rows, lanes], dcc)
-            dscores = probs * (dprobs - jnp.sum(dprobs * probs, axis=0, keepdims=True))
-            dscores = dscores.astype(jnp.bfloat16)
-            dv_ref[rows, lanes] = dot_nn(low, dcc).astype(jnp.bfloat16)
-            dk_ref[rows, lanes] = (dot_nn(dscores, qq) * HD ** (-0.5)).astype(jnp.bfloat16)
-            mixed = dot_tn(dscores, k_ref[rows, lanes]) * HD ** (-0.5)
-            dq_ref[rows, lanes] = jnp.where(is_first, mixed[:GROUP], mixed[GROUP:]).astype(jnp.bfloat16)
+        dcc = [both_heads(dctx_ref[rows, lanes], first, second) for lanes in every_pair]
+        dprobs = jnp.concatenate(
+            [dot_nt(v_ref[rows, lanes], wide) for lanes, wide in zip(every_pair, dcc)], axis=1
+        )
+        low = probs_ref[sent]
+        probs = low.astype(jnp.float32)
+        dscores = probs * (dprobs - jnp.sum(dprobs * probs, axis=0, keepdims=True))
+        dscores = (dscores * HD ** (-0.5)).astype(jnp.bfloat16)
+        dv_ref[rows, :] = jnp.concatenate(
+            [dot_nn(low[:, lanes], wide) for lanes, wide in zip(every_pair, dcc)], axis=1
+        ).astype(jnp.bfloat16)
+        qq = [both_heads(q_ref[rows, lanes], first, second) for lanes in every_pair]
+        dk_ref[rows, :] = jnp.concatenate(
+            [dot_nn(dscores[:, lanes], wide) for lanes, wide in zip(every_pair, qq)], axis=1
+        ).astype(jnp.bfloat16)
+        mixed = [dot_tn(dscores[:, lanes], k_ref[rows, lanes]) for lanes in every_pair]
+        dq_ref[rows, :] = jnp.concatenate(
+            [jnp.where(is_first, m[:GROUP], m[GROUP:]) for m in mixed], axis=1
+        ).astype(jnp.bfloat16)
     dx = dr1
     for m, (ref, r) in enumerate(((dq_ref, 0), (dk_ref, None), (dv_ref, 1))):
         need(m)
@@ -888,7 +896,7 @@
     in_specs = [tiles(a.shape) for a in ins]
     in_specs[1] = pl.BlockSpec((1, sents, width), lambda i, *_: (i, 0, 0))
     in_specs[2] = whole(small.shape)
-    in_specs[6] = pl.BlockSpec((sents,) + probs.shape[1:], lambda i, *_: (i, 0, 0, 0))
+    in_specs[6] = pl.BlockSpec((sents,) + probs.shape[1:], lambda i, *_: (i, 0, 0))
     outs = [((rows, width), bf)] * 2 + [((rows, FF), bf)] + [((rows, width), bf)] * 4 + [(small.shape, f32)]
     specs = [tiles(shape) for shape, _ in outs]
     specs[7] = whole(small.shape)

time: 362 us -> 330 us (0.912)
  Pallas kernels: 331 us -> 307 us
  local copies, waits for them, and re-layouts: 9.19 us -> 2.15 us
    pallas_call x1, Pallas kernels: 56.6 us -> 38.8 us  [run_forward(): pl.pallas_call(functools.partial(forward_kernel, edges), name='layer_forw...]
    pallas_call x1, Pallas kernels: 48.2 us -> 38.3 us  [run_backward(): pl.pallas_call(functools.partial(backward_kernel, edges), name='layer_bac...]
    unnamed x18 -> x14, local copies, waits for them, and re-layouts: 7.08 us -> 0.04 us
where the time goes in v2:
time: 330 us
  Pallas kernels  307 us (93%)
  other arithmetic  10.9 us (3%)
  between operations  9.94 us (3%)
    pallas_call x1, Pallas kernels, reduce_units(): pl.pallas_call(reduce_kernel, name='reduce_units', out_shape=[jax.ShapeDt...  114 us
    pallas_call x1, Pallas kernels, gather_units(): pl.pallas_call(gather_kernel, name='gather_units', out_shape=jax.ShapeDty...  73.2 us
    pallas_call x1, Pallas kernels, run_forward(): pl.pallas_call(functools.partial(forward_kernel, edges), name='layer_forw...  38.8 us
    pallas_call x1, Pallas kernels, run_backward(): pl.pallas_call(functools.partial(backward_kernel, edges), name='layer_bac...  38.3 us
    pallas_call x1, Pallas kernels, run_weight_grads(): pl.pallas_call(functools.partial(weight_grad_kernel, edges), name='weight...  22.2 us
    pallas_call x1, Pallas kernels, rank_loss(): pl.pallas_call(rank_kernel, name='rank_loss', out_shape=[jax.ShapeDtypeSt...  20 us
    transpose x1, other arithmetic, per_device(): back_order = lambda a: a.transpose(1, 0, 2)  7.91 us

profile of v2, /device:TPU:8, one launch (start us, length us, event | category | flops | bytes accessed | tf_op | source)
XLA Modules:
  0.0 329.9 jit_solution(11588520503311693465)
XLA Ops:
  0.6 0.9 select_reduce_fusion
  1.6 1.2 multiply_add_fusion.1.pos_ref
  2.7 73.2 %gather_units.1.units_hbm = bf16[80,128,768]{2,1,0:T(8,128)(2,1)} custom-call(f32[5,128,768]{2,1,0:T(8,128)} %bitcast.44), custom_call_target="tpu_custom_call" | custom-call | tf_op jit(solution)/shard_map/gather_units/pallas_call | solution.py:290
  75.9 0.0 copy-start
  76.0 38.8 %layer_forward.1 = (bf16[1024,768]{1,0:T(8,128)(2,1)}, bf16[1024,768]{1,0:T(8,128)(2,1)}, bf16[1024,768]{1,0:T(8,128)(2,1)}, bf16[1024,768]{1,0:T(8,128)(2,1)}, ...) custom-call(s32[72]{0:T(128)} %multiply_add_fusion.1.pos_ref, ...), custom_call_target="tpu_custom_call" | custom-call | tf_op jit(solution)/shard_map/layer_forward/pallas_call | solution.py:786
  114.8 0.8 reshape.63.cls_ref
  116.2 0.0 copy-done
  116.2 0.1 copy.27.lang_col
  116.4 20.0 %rank_loss.1 = (f32[16,768]{1,0:T(8,128)S(1)}, f32[8,128]{1,0:T(8,128)S(1)}) custom-call(f32[1]{0:T(128)S(6)} %copy.28.scale_ref, f32[16,768]{1,0:T(8,128)S(1)} %reshape.63.cls_ref, s32[1,256]{1,0:T(1,128)S(1)} %bitcast.43, s32[256,1]{1,0:T(8,128)S(1)} %copy.27.lang_col), custom_call_target="tpu_custom_call" | custom-call | tf_op jit(solution)/shard_map/rank_loss/pallas_call | solution.py:611
  136.4 0.6 reshape.66.dc_ref
  137.0 38.3 %layer_backward.1 = (bf16[1024,768]{1,0:T(8,128)(2,1)}, bf16[1024,768]{1,0:T(8,128)(2,1)}, bf16[1024,3072]{1,0:T(8,128)(2,1)}, bf16[1024,768]{1,0:T(8,128)(2,1)}...) custom-call(s32[72]{0:T(128)} %multiply_add_fusion.1.pos_ref, ...), custom_call_target="tpu_custom_call" | custom-call | tf_op jit(solution)/shard_map/layer_backward/pallas_call | solution.py:903
  175.3 22.2 %weight_grads.1.g_ref = bf16[80,128,768]{2,1,0:T(8,128)(2,1)} custom-call(s32[72]{0:T(128)} %multiply_add_fusion.1.pos_ref, bf16[1024,768]{1,0:T(8,128)(2,1)} %bitcast.46, bf16[1024,768]{1,0:T(8,128)(2,1)} %get-tuple-element.52.ctx_hbm, bf16[1024,3072]{1,0:T(8,128)(2,1)} %get-tuple-element.53.du_hbm, bf16[1024,3072]{1,0:T(8,128)(2,1)} %get-tuple-element.54.act_hbm, ...), custom_call_target="tpu_custom_call" | custom-call | tf_op jit(solution)/shard_map/weight_grads/pallas_call | solution.py:972
  197.5 0.0 copy-start.6
  197.5 0.0 copy-start.1
  197.5 114.4 %reduce_units.1 = (f32[5,128,768]{2,1,0:T(8,128)}, f32[12,768]{1,0:T(8,128)}) custom-call(bf16[80,128,768]{2,1,0:T(8,128)(2,1)} %weight_grads.1.g_ref, f32[12,768]{1,0:T(8,128)} %get-tuple-element.61.small_ref), custom_call_target="tpu_custom_call" | custom-call | tf_op jit(solution)/shard_map/reduce_units/pallas_call | solution.py:498
  312.0 0.0 copy-done.6
  312.0 0.2 compare_reduce_fusion
  312.2 0.0 copy-done.1
  312.2 0.0 copy-start.2
  312.2 0.0 copy-start.3
  312.2 0.0 copy-start.4
  312.2 0.0 copy-start.5
  312.3 7.9 %convert_bitcast_fusion = (bf16[128,5,768]{2,0,1:T(8,128)(2,1)}, f32[5,128,768]{2,1,0:T(8,128)}, f32[128,5,768]{2,0,1:T(8,128)}, f32[128,5,768]{2,0,1:T(8,128)}) fusion(f32[5,128,768]{2,1,0:T(8,128)} %get-tuple-element.62, f32[128,5,768]{2,0,1:T(8,128)} %param.17, f32[128,5,768]{2,0,1:T(8,128)} %param.16, f32[128,5,768]{2,0,1:T(8,128)S(1)} %copy-done.1, ...), kind=kLoop, calls=%fused_computation.10 | loop fusion | flops 9338880 | bytes 14745605 | tf_op jit(solution)/shard_map/transpose | solution.py:1111
  320.2 0.0 copy-done.2
  320.2 0.0 copy-done.3
  320.2 0.0 copy-done.4
  320.2 0.0 copy-done.5
  320.2 0.7 multiply_subtract_fusion
  320.9 0.5 fusion.7
  (1 shorter events, 0.0 us)
Async XLA Ops:
  75.9 40.3 %copy-start = (s32[256]{0:T(256)S(1)}, s32[256]{0:T(256)}, u32[]{:S(2)}) copy-start(s32[256]{0:T(256)} %param.24) | copy-start | bytes 3076
  197.5 114.5 %copy-start.6 = (s32[72]{0:T(128)S(1)}, s32[72]{0:T(128)}, u32[]{:S(2)}) copy-start(s32[72]{0:T(128)} %multiply_add_fusion.1.pos_ref) | copy-start | bytes 868
  197.5 114.7 %copy-start.1 = (f32[128,5,768]{2,0,1:T(8,128)S(1)}, f32[128,5,768]{2,0,1:T(8,128)}, u32[]{:S(2)}) copy-start(f32[128,5,768]{2,0,1:T(8,128)} %param.15) | copy-start | bytes 5898244
  312.2 8.0 %copy-start.2 = (f32[12,768]{1,0:T(8,128)S(1)}, f32[12,768]{1,0:T(8,128)}, u32[]{:S(2)}) copy-start(f32[12,768]{1,0:T(8,128)} %small_ref.3) | copy-start | bytes 110596
  312.2 8.0 %copy-start.3 = (f32[12,768]{1,0:T(8,128)S(1)}, f32[12,768]{1,0:T(8,128)}, u32[]{:S(2)}) copy-start(f32[12,768]{1,0:T(8,128)} %param.19) | copy-start | bytes 110596
  312.2 7.9 %copy-start.4 = (f32[12,768]{1,0:T(8,128)S(1)}, f32[12,768]{1,0:T(8,128)}, u32[]{:S(2)}) copy-start(f32[12,768]{1,0:T(8,128)} %param.20) | copy-start | bytes 110596
  312.2 7.9 %copy-start.5 = (f32[12,768]{1,0:T(8,128)S(1)}, f32[12,768]{1,0:T(8,128)}, u32[]{:S(2)}) copy-start(f32[12,768]{1,0:T(8,128)} %get-tuple-element.63) | copy-start | bytes 110596

commit v3 on v2

--- a/solution.py
+++ b/solution.py
@@ -296,227 +296,6 @@
         scratch_shapes=[pltpu.VMEM((slots, rows, width), jnp.bfloat16), pltpu.SemaphoreType.DMA((slots,))] + line + plane,
         compiler_params=pltpu.CompilerParams(collective_id=0, has_side_effects=True, vmem_limit_bytes=VMEM_MOST),
     )(own)
-
-
-RX = 32
-RY = UR_ROWS - RX
-
-
-def reduce_kernel(g_ref, small_ref, out_ref, small_out, held, c_in, x_in, y_in, z_in, f_in, t_acc, t_in,
-                  p_sem, c_s, c_r, x_s, x_r, y_s, y_r, zl_s, zl_r, zr_s, zr_r, f_s, f_r, t_s, t_r):
-    s, z, y, c = place()
-    slots = out_ref.shape[0]
-    steps = ZS * slots
-    base = pl.multiple_of(s * RX, 16)
-    only = pl.multiple_of(s * RY, 16)
-    theirs = pl.multiple_of((1 - s) * RY, 16)
-    left = (s, batch_of(z - 1, y, c))
-    right = (s, batch_of(z + 1, y, c))
-    across = (s, batch_of(z, 1 - y, c))
-    other = (1 - s, batch_of(z, y, c))
-    sibling = (s, batch_of(z, y, 1 - c))
-    round_to = (sibling, across, other, (s, batch_of(z + 1 - 2 * (z % 2), y, c)), (s, batch_of((z + 2) % ZS, y, c)))
-    greet(s, z, y, c, "line")
-
-    def remote(src, dst, send, recv, target):
-        return pltpu.make_async_remote_copy(
-            src_ref=src, dst_ref=dst, send_sem=send, recv_sem=recv, device_id=target, device_id_type=MESH
-        )
-
-    def where_of(t):
-        return (3 * (t // slots)) % ZS, t % slots
-
-    def to_sibling(zz, yy, j):
-        row = batch_of(zz, yy, 1 - c) * slots + j
-        return remote(g_ref.at[row], c_in.at[zz, yy, j], c_s.at[zz, yy, j], c_r.at[zz, yy, j], sibling)
-
-    def fetch(zz, yy, j):
-        row = batch_of(zz, yy, c) * slots + j
-        return pltpu.make_async_copy(g_ref.at[row], held.at[zz, yy, j], p_sem.at[zz, yy, j])
-
-    def to_other(zz, yy, j):
-        return remote(held.at[zz, yy, j, pl.ds(theirs, RX)], x_in.at[zz, yy, j], x_s.at[zz, yy, j], x_r.at[zz, yy, j], other)
-
-    def to_across(zz, j):
-        return remote(held.at[zz, 1 - y, j, pl.ds(base, RY)], y_in.at[zz, j], y_s.at[zz, j], y_r.at[zz, j], across)
-
-    def to_left(zz, j):
-        return remote(held.at[zz, y, j, pl.ds(base, RY)], z_in.at[1, zz, j], zl_s.at[zz, j], zl_r.at[zz, j], left)
-
-    def to_right(zz, j):
-        return remote(held.at[zz, y, j, pl.ds(base, RY)], z_in.at[0, zz, j], zr_s.at[zz, j], zr_r.at[zz, j], right)
-
-    def final(j):
-        return remote(held.at[z, y, j, pl.ds(base, RY)], f_in.at[j], f_s.at[j], f_r.at[j], other)
-
-    def turn(r):
-        return remote(t_acc.at[r], t_in.at[r], t_s.at[r], t_r.at[r], round_to[r])
-
-    def add(zz, yy, j, start, size, got):
-        mine = held.at[zz, yy, j, pl.ds(start, size)]
-        mine[...] = (mine[...].astype(jnp.float32) + got[...].astype(jnp.float32)).astype(jnp.bfloat16)
-
-    @pl.loop(0, steps)
-    def _(t):
-        zz, j = where_of(t)
-        for yy in (1 - y, y):
-            to_sibling(zz, yy, j).start()
-            fetch(zz, yy, j).start()
-
-    t_acc[0] = small_ref[...]
-
-    def core_stage(t):
-        zz, j = where_of(t)
-        for yy in (1 - y, y):
-            fetch(zz, yy, j).wait()
-            to_sibling(zz, yy, j).wait_recv()
-            add(zz, yy, j, 0, UR_ROWS, c_in.at[zz, yy, j])
-            to_other(zz, yy, j).start()
-
-    def other_stage(t):
-        zz, j = where_of(t)
-        for yy in (1 - y, y):
-            to_other(zz, yy, j).wait_recv()
-            add(zz, yy, j, only, RX, x_in.at[zz, yy, j])
-        to_across(zz, j).start()
-
-    def across_stage(t):
-        zz, j = where_of(t)
-        to_across(zz, j).wait_recv()
-        add(zz, y, j, base, RY, y_in.at[zz, j])
-
-    def from_left(zz, j):
-        to_right(zz, j).wait_recv()
-        add(zz, y, j, base, RY, z_in.at[0, zz, j])
-
-    def from_right(zz, j):
-        to_left(zz, j).wait_recv()
-        add(zz, y, j, base, RY, z_in.at[1, zz, j])
-
-    def line_stage(t, hops):
-        zz, j = where_of(t)
-
-        @pl.when((zz > z) & (z == hops))
-        def _():
-            if hops > 0:
-                from_left(zz, j)
-            to_right(zz, j).start()
-
-        @pl.when((zz < z) & (ZS - 1 - z == hops))
-        def _():
-            if hops > 0:
-                from_right(zz, j)
-            to_left(zz, j).start()
-
-        @pl.when((zz == z) & (3 - ((z + 2) // 3) * ((5 - z) // 3) == hops))
-        def _():
-            @pl.when(z > 0)
-            def _():
-                from_left(zz, j)
-
-            @pl.when(z < ZS - 1)
-            def _():
-                from_right(zz, j)
-
-            final(j).start()
-
-    def final_stage(t):
-        zz, j = where_of(t)
-
-        @pl.when(zz == z)
-        def _():
-            final(j).wait_recv()
-            f32 = jnp.float32
-            out_ref[j, pl.ds(only, RX)] = held[z, y, j, pl.ds(only, RX)].astype(f32)
-            shared = f_in[j, pl.ds(pl.multiple_of(s * RX, 16), RY - RX)].astype(f32)
-            out_ref[j, pl.ds(RX, RY - RX)] = held[z, y, j, pl.ds(RX, RY - RX)].astype(f32) + shared
-            out_ref[j, pl.ds(theirs, RX)] = f_in[j, pl.ds(pl.multiple_of((1 - s) * (RY - RX), 16), RX)].astype(f32)
-
-    @pl.loop(0, steps + 6)
-    def _(i):
-        @pl.when(i < steps)
-        def _():
-            core_stage(i)
-
-        @pl.when((i >= 1) & (i < steps + 1))
-        def _():
-            other_stage(i - 1)
-
-        @pl.when((i >= 2) & (i < steps + 2))
-        def _():
-            across_stage(i - 2)
-
-        for hops in range(ZS):
-
-            @pl.when((i >= 2 + hops) & (i < steps + 2 + hops))
-            def _():
-                line_stage(i - 2 - hops, hops)
-
-        @pl.when(i >= 6)
-        def _():
-            final_stage(i - 6)
-
-        for r in range(5):
-
-            @pl.when(i == 3 * r)
-            def _():
-                turn(r).start()
-
-            @pl.when(i == 3 * r + 2)
-            def _():
-                turn(r).wait()
-                t_acc[r + 1] = t_acc[r] + t_in[r]
-
-    small_out[...] = t_acc[5]
-
-    @pl.loop(0, steps)
-    def _(t):
-        zz, j = where_of(t)
-        for yy in range(2):
-            to_sibling(zz, yy, j).wait_send()
-            to_other(zz, yy, j).wait_send()
-        to_across(zz, j).wait_send()
-
-        @pl.when(zz > z)
-        def _():
-            to_right(zz, j).wait_send()
-
-        @pl.when(zz < z)
-        def _():
-            to_left(zz, j).wait_send()
-
-        @pl.when(zz == z)
-        def _():
-            final(j).wait_send()
-
-
-def reduce_units(grads, small, slots):
-    owners = lax.axis_size("batch")
-    _, rows, width = grads.shape
-    bf, f32 = jnp.bfloat16, jnp.float32
-    dma = pltpu.SemaphoreType.DMA
-    return pl.pallas_call(
-        reduce_kernel,
-        name="reduce_units",
-        out_shape=[jax.ShapeDtypeStruct((slots, rows, width), f32), jax.ShapeDtypeStruct(small.shape, f32)],
-        in_specs=[pl.BlockSpec(memory_space=pl.ANY), pl.BlockSpec(memory_space=pltpu.VMEM)],
-        out_specs=[pl.BlockSpec(memory_space=pltpu.VMEM)] * 2,
-        scratch_shapes=[
-            pltpu.VMEM((ZS, 2, slots, rows, width), bf),
-            pltpu.VMEM((ZS, 2, slots, rows, width), bf),
-            pltpu.VMEM((ZS, 2, slots, RX, width), bf),
-            pltpu.VMEM((ZS, slots, RY, width), bf),
-            pltpu.VMEM((2, ZS, slots, RY, width), bf),
-            pltpu.VMEM((slots, RY, width), bf),
-            pltpu.VMEM((6,) + small.shape, f32),
-            pltpu.VMEM((5,) + small.shape, f32),
-        ]
-        + [dma((ZS, 2, slots))] * 5
-        + [dma((ZS, slots))] * 6
-        + [dma((slots,))] * 2
-        + [dma((5,))] * 2,
-        compiler_params=pltpu.CompilerParams(collective_id=2, has_side_effects=True, vmem_limit_bytes=VMEM_MOST),
-    )(grads, small)
 
 
 def rank_kernel(scale_ref, cls_ref, lang_row, lang_col, dc_ref, stats_ref, every, weights, z_s, z_r, pair_s, pair_r):
@@ -690,7 +469,7 @@
 def forward_kernel(
     edges, pos_ref, x_ref, small_ref, units_hbm,
     out_ref, q_ref, k_ref, v_ref, probs_ref, ctx_ref, n1_ref, rs1_ref, hb_ref, act_ref, slope_ref, n2_ref, rs2_ref,
-    cls_ref, held, sems,
+    cls_ref, ordered_hbm, held, sems, keep_sem,
 ):
     first_tile = pl.program_id(0) == 0
     width = x_ref.shape[1]
@@ -740,6 +519,12 @@
     hb_ref[...] = hb
     need(4)
     need(5)
+    keep = pltpu.make_async_copy(held, ordered_hbm, keep_sem)
+
+    @pl.when(first_tile)
+    def _():
+        keep.start()
+
     per = (edges[5] - edges[4]) // inner_rows
     total = h1 + row(3 + inner_rows)
     for part in range(inner_rows):
@@ -759,6 +544,10 @@
     for sent in range(TILE // GROUP):
         cls_ref[0, sent : sent + 1, :] = y[sent * GROUP : sent * GROUP + 1, :]
 
+    @pl.when(pl.program_id(0) == pl.num_programs(0) - 1)
+    def _():
+        keep.wait()
+
 
 def tiles(shape):
     rest = len(shape) - 1
@@ -779,10 +568,12 @@
         ((rows, width), bf), ((rows, width), bf), ((rows, width), bf), ((rows, width), bf), (probs_shape, bf),
         ((rows, width), bf), ((rows, width), f32), ((rows, 1), f32), ((rows, width), bf), ((rows, FF), bf),
         ((rows, FF), bf), ((rows, width), f32), ((rows, 1), f32), ((count, sents, width), f32),
+        ((edges[6],) + units.shape[1:], bf),
     ]
     specs = [tiles(shape) for shape, _ in outs]
     specs[4] = pl.BlockSpec((sents,) + probs_shape[1:], lambda i, *_: (i, 0, 0))
     specs[13] = pl.BlockSpec((1, sents, width), lambda i, *_: (i, 0, 0))
+    specs[14] = pl.BlockSpec(memory_space=pl.ANY)
     return pl.pallas_call(
         functools.partial(forward_kernel, edges),
         name="layer_forward",
@@ -791,7 +582,9 @@
             grid=(count,),
             in_specs=[tiles(x.shape), whole(small.shape), pl.BlockSpec(memory_space=pl.ANY)],
             out_specs=specs,
-            scratch_shapes=[pltpu.VMEM((edges[6],) + units.shape[1:], bf), pltpu.SemaphoreType.DMA((6,))],
+            scratch_shapes=[
+                pltpu.VMEM((edges[6],) + units.shape[1:], bf), pltpu.SemaphoreType.DMA((6,)), pltpu.SemaphoreType.DMA,
+            ],
         ),
         out_shape=[jax.ShapeDtypeStruct(shape, kind) for shape, kind in outs],
         compiler_params=pltpu.CompilerParams(vmem_limit_bytes=VMEM_MOST),
@@ -891,7 +684,7 @@
     count = rows // TILE
     sents = TILE // GROUP
     bf, f32 = jnp.bfloat16, jnp.float32
-    _, q, k, v, probs, _, n1, rs1, _, _, slope, n2, rs2, _ = saved
+    _, q, k, v, probs, _, n1, rs1, _, _, slope, n2, rs2, _ = saved[:14]
     ins = [og, dc, small, q, k, v, probs, n1, rs1, slope, n2, rs2]
     in_specs = [tiles(a.shape) for a in ins]
     in_specs[1] = pl.BlockSpec((1, sents, width), lambda i, *_: (i, 0, 0))
@@ -985,6 +778,540 @@
     )(positions, x, ctx, du, act, dq, dk, dv, da, hb, df)
 
 
+STEPS = 6
+BAND = 16
+HALF = 384
+
+
+def step_units(edges):
+    per = edges[1] - edges[0]
+    firsts = [(edges[5] + per * t, edges[4] + per * t) for t in range(4)]
+    return firsts + [(edges[3], edges[0]), (edges[1], edges[2])]
+
+
+def sum_places(edges):
+    per = edges[1] - edges[0]
+    table = [0] * edges[6]
+    for t, firsts in enumerate(step_units(edges)):
+        for m, first in enumerate(firsts):
+            for k in range(per):
+                table[first + k] = (k % 2) * (STEPS * per) + t * per + m * (per // 2) + k // 2
+    return table
+
+
+def backward_reduce_kernel(
+    edges, tab_ref, small_ref, dc_ref, rs1_ref, rs2_ref, og_hbm, n2_hbm, slope_hbm, act_hbm, hb_hbm, n1_hbm, ctx_hbm,
+    q_hbm, k_hbm, v_hbm, x_hbm, probs_hbm, units_hbm,
+    dx_hbm, own_out, small_out,
+    dh, nbuf, p0, p1, p2, p3, p4, p5, p6, p7, p8, wbuf, gbuf, c_in, xa, yb, ya, xb, z_in, fbuf, a_out, a_in, x_in,
+    gsm, t_acc, t_in,
+    l_sem, c_s, c_r, xa_s, xa_r, yb_s, yb_r, ya_s, ya_r, xb_s, xb_r, zr_s, zr_r, zl_s, zl_r, f_s, f_r, a_s, a_r, o_s, o_r,
+    t_s, t_r, c_free,
+):
+    s, z, y, c = place()
+    bf, f32 = jnp.bfloat16, jnp.float32
+    rows_all, width = dh.shape
+    count = rows_all // TILE
+    inner_rows = FF // width
+    per = edges[1] - edges[0]
+    unit_rows = gbuf.shape[4]
+    slots = own_out.shape[0]
+    upper = unit_rows // 2
+    sibling = (s, batch_of(z, y, 1 - c))
+    across = (s, batch_of(z, 1 - y, c))
+    other = (1 - s, batch_of(z, y, c))
+    left = (s, batch_of(z - 1, y, c))
+    right = (s, batch_of(z + 1, y, c))
+    round_to = (sibling, across, other, (s, batch_of(z + 1 - 2 * (z % 2), y, c)), (s, batch_of((z + 2) % ZS, y, c)))
+
+    barrier = pltpu.get_barrier_semaphore()
+
+    def hello(target):
+        pl.semaphore_signal(barrier, inc=1, device_id=target, device_id_type=MESH)
+
+    hello(sibling)
+    hello(other)
+    turns = [(dz, dy) for dz in range(ZS) for dy in range(2) if dz or dy]
+    for dz, dy in turns:
+        hello((s, batch_of((z + dz) % ZS, (y + dy) % 2, c)))
+    pl.semaphore_wait(barrier, 2 + len(turns))
+
+    chunk = lambda ref, p: ref.at[:, pl.ds(p * width, width)]
+    matrix = lambda first: units_hbm.at[pl.ds(first, per)]
+    firsts = step_units(edges)
+    acts, slopes = (p3, p5), (p4, p6)
+    loads = {"og": (og_hbm, p0), "n2": (n2_hbm, nbuf), "hb": (hb_hbm, p2), "n1": (n1_hbm, nbuf), "probs": (probs_hbm, p0),
+             "ctx": (ctx_hbm, p3), "q": (q_hbm, p4), "k": (k_hbm, p7), "v": (v_hbm, p8), "x": (x_hbm, p3)}
+    for p in range(inner_rows):
+        loads["act%d" % p] = (chunk(act_hbm, p), acts[p % 2])
+        loads["slope%d" % p] = (chunk(slope_hbm, p), slopes[p % 2])
+        loads["wo%d" % p] = (matrix(firsts[p][0]), wbuf.at[p % 2, 0])
+        loads["wi%d" % p] = (matrix(firsts[p][1]), wbuf.at[p % 2, 1])
+    for t in (4, 5):
+        for m in range(2):
+            loads["w%d%d" % (t, m)] = (matrix(firsts[t][m]), wbuf.at[t % 2, m])
+    copies = {
+        name: pltpu.make_async_copy(src, dst, l_sem.at[n]) for n, (name, (src, dst)) in enumerate(loads.items())
+    }
+
+    def begin(*names):
+        for name in names:
+            copies[name].start()
+
+    def ready(*names):
+        for name in names:
+            copies[name].wait()
+
+    begin("og", "n2", "slope0", "wo0", "wi0", "act0", "hb", "slope1", "wo1", "wi1", "act1", "k", "v")
+
+    row = lambda r: small_ref[r : r + 1, :]
+    gsm[...] = jnp.zeros_like(gsm)
+
+    def add_small(r, values):
+        gsm[r : r + 1, :] += jnp.sum(values.astype(f32), axis=0, keepdims=True)
+
+    def tile_rows(i):
+        return pl.ds(pl.multiple_of(i * TILE, TILE), TILE)
+
+    def weight(slot, m):
+        return wbuf[slot, m].reshape(per * unit_rows, width)
+
+    def remote(src, dst, send, recv, target):
+        return pltpu.make_async_remote_copy(
+            src_ref=src, dst_ref=dst, send_sem=send, recv_sem=recv, device_id=target, device_id_type=MESH
+        )
+
+    my_rows = pl.ds(pl.multiple_of(s * upper, upper), upper)
+    its_rows = pl.ds(pl.multiple_of((1 - s) * upper, upper), upper)
+    my_cols = pl.ds(pl.multiple_of(y * HALF, 128), HALF)
+    its_cols = pl.ds(pl.multiple_of((1 - y) * HALF, 128), HALF)
+    every = pl.ds(0, per // 2)
+
+    def band(zz):
+        return pl.ds(pl.multiple_of(s * upper + zz * BAND, BAND), BAND)
+
+    def c_copy(t):
+        return remote(gbuf.at[t, :, 1 - c], c_in.at[t % RING], c_s.at[t], c_r.at[t], sibling)
+
+    def xa_copy(t):
+        return remote(gbuf.at[t, 0, c, every, its_rows], xa.at[t], xa_s.at[t], xa_r.at[t], other)
+
+    def yb_copy(t):
+        return remote(gbuf.at[t, 1, c, every, pl.ds(0, unit_rows), its_cols], yb.at[t], yb_s.at[t], yb_r.at[t], across)
+
+    def ya_copy(t):
+        return remote(gbuf.at[t, 0, c, every, my_rows, its_cols], ya.at[t], ya_s.at[t], ya_r.at[t], across)
+
+    def xb_copy(t):
+        return remote(gbuf.at[t, 1, c, every, its_rows, my_cols], xb.at[t], xb_s.at[t], xb_r.at[t], other)
+
+    def z_copy(t, zz, way):
+        send, recv, target = ((zr_s, zr_r, right), (zl_s, zl_r, left))[way]
+        return remote(
+            gbuf.at[t, pl.ds(0, 2), c, every, band(zz), my_cols], z_in.at[way, t, zz], send.at[t, zz], recv.at[t, zz], target
+        )
+
+    def f_copy(t):
+        mine = fbuf.at[pl.ds(c * (STEPS * per) + t * per, per)]
+        return remote(mine, mine, f_s.at[t], f_r.at[t], sibling)
+
+    def turn(r):
+        return remote(t_acc.at[r], t_in.at[r], t_s.at[r], t_r.at[r], round_to[r])
+
+    def add(view, got):
+        @pl.loop(0, per // 2)
+        def _(k):
+            view.at[k][...] = (view.at[k][...].astype(f32) + got.at[k][...].astype(f32)).astype(bf)
+
+    def ev_c_send(t):
+        if t >= RING:
+            pl.semaphore_wait(c_free, 1)
+        c_copy(t).start()
+
+    def ev_c_wait(t):
+        c_copy(t).wait_recv()
+        add(gbuf.at[t, 0, c], c_in.at[t % RING, 0])
+        xa_copy(t).start()
+        add(gbuf.at[t, 1, c], c_in.at[t % RING, 1])
+        if t + RING < STEPS:
+            pl.semaphore_signal(c_free, inc=1, device_id=sibling, device_id_type=MESH)
+        yb_copy(t).start()
+
+    def ev_first(t):
+        xa_copy(t).wait_recv()
+        add(gbuf.at[t, 0, c, every, my_rows], xa.at[t])
+        ya_copy(t).start()
+        yb_copy(t).wait_recv()
+        add(gbuf.at[t, 1, c, every, pl.ds(0, unit_rows), my_cols], yb.at[t])
+        xb_copy(t).start()
+
+    def ev_second(t):
+        ya_copy(t).wait_recv()
+        add(gbuf.at[t, 0, c, every, my_rows, my_cols], ya.at[t])
+        xb_copy(t).wait_recv()
+        add(gbuf.at[t, 1, c, every, my_rows, my_cols], xb.at[t])
+
+    def ev_z(t, hop):
+        @pl.when(z == hop)
+        def _():
+            @pl.loop(0, ZS)
+            def _(zz):
+                @pl.when(zz >= z)
+                def _():
+                    @pl.when(z > 0)
+                    def _():
+                        z_copy(t, zz, 0).wait_recv()
+                        for m in range(2):
+                            add(gbuf.at[t, m, c, every, band(zz), my_cols], z_in.at[0, t, zz, m])
+
+                    @pl.when(zz > z)
+                    def _():
+                        z_copy(t, zz, 0).start()
+
+        @pl.when(ZS - 1 - z == hop)
+        def _():
+            @pl.loop(0, ZS)
+            def _(zz):
+                @pl.when(zz <= z)
+                def _():
+                    @pl.when(z < ZS - 1)
+                    def _():
+                        z_copy(t, zz, 1).wait_recv()
+                        for m in range(2):
+                            add(gbuf.at[t, m, c, every, band(zz), my_cols], z_in.at[1, t, zz, m])
+
+                    @pl.when(zz < z)
+                    def _():
+                        z_copy(t, zz, 1).start()
+
+    def ev_fin(t):
+        for m in range(2):
+
+            @pl.loop(0, per // 2)
+            def _(k):
+                at = c * (STEPS * per) + t * per + m * (per // 2) + k
+                fbuf[at] = gbuf[t, m, c, k, band(z), my_cols]
+
+        f_copy(t).start()
+
+    def ev_turn_start(r):
+        if r == 0:
+            t_acc[0] = gsm[...]
+        turn(r).start()
+
+    def ev_turn_wait(r):
+        turn(r).wait()
+        t_acc[r + 1] = t_acc[r] + t_in[r]
+
+    def sec_start():
+        ready("og", "n2")
+        for i in range(count):
+            rows = slice(i * TILE, (i + 1) * TILE)
+            dh[rows, :] = p0[rows, :].astype(f32)
+            for sent in range(TILE // GROUP):
+                at = i * TILE + sent * GROUP
+                here = i * (TILE // GROUP) + sent
+                dh[at : at + 1, :] += dc_ref[here : here + 1, :]
+            dy = dh[rows, :]
+            n2 = nbuf[rows, :]
+            add_small(6 + inner_rows, dy * n2)
+            add_small(7 + inner_rows, dy)
+            dr2 = norm_back(dy, n2, rs2_ref[rows, :], row(6 + inner_rows))
+            dh[rows, :] = dr2
+            df = dr2.astype(bf)
+            p1[rows, :] = df
+            add_small(3 + inner_rows, df)
+        begin("n1", "probs")
+
+    def store_grads(t, m, lhs, rhs):
+        @pl.loop(0, 2)
+        def _(piece):
+            half = (per // 2) * unit_rows
+            cols = pl.ds(pl.multiple_of(piece * half, 128), half)
+            block = dot_tn(lhs[:, cols], rhs[...]).astype(bf)
+            for i in range(per // 2):
+                part = block[i * unit_rows : (i + 1) * unit_rows]
+
+                @pl.when(piece == 0)
+                def _():
+                    gbuf[t, m, i % 2, i // 2] = part
+
+                @pl.when(piece == 1)
+                def _():
+                    k = per // 2 + i
+                    gbuf[t, m, k % 2, k // 2] = part
+
+    def sec_inner(p):
+        def run():
+            ready("slope%d" % p, "wo%d" % p, "wi%d" % p)
+            slope = slopes[p % 2]
+
+            @pl.loop(0, count)
+            def _(i):
+                rows = tile_rows(i)
+                da = dot_nt(p1[rows, :], weight(p % 2, 0))
+                du = (da * slope[rows, :].astype(f32)).astype(bf)
+                slope[rows, :] = du
+                add_small(3 + p, du)
+                dh[rows, :] += dot_nn(du, weight(p % 2, 1))
+
+            if p == 2:
+                begin("w40", "w41")
+            if p == 3:
+                begin("w50", "w51")
+            if p + 2 < inner_rows:
+                begin("wo%d" % (p + 2), "wi%d" % (p + 2))
+
+        return run
+
+    def sec_outer_grad(p):
+        def run():
+            ready("act%d" % p)
+            store_grads(p, 0, acts[p % 2], p1)
+            if p + 2 < inner_rows:
+                begin("act%d" % (p + 2))
+            if p == 2:
+                begin("ctx")
+
+        return run
+
+    def sec_inner_grad(p):
+        def run():
+            if p == 0:
+                ready("hb")
+            store_grads(p, 1, slopes[p % 2], p2)
+            if p + 2 < inner_rows:
+                begin("slope%d" % (p + 2))
+            if p == 2:
+                begin("q")
+
+        return run
+
+    def sec_norm():
+        ready("n1", "w40", "w41")
+
+        @pl.loop(0, count)
+        def _(i):
+            rows = tile_rows(i)
+            dh1 = dh[rows, :]
+            n1 = nbuf[rows, :]
+            add_small(4 + inner_rows, dh1 * n1)
+            add_small(5 + inner_rows, dh1)
+            dr1 = norm_back(dh1, n1, rs1_ref[rows, :], row(4 + inner_rows))
+            dh[rows, :] = dr1
+            dattn = dr1.astype(bf)
+            p1[rows, :] = dattn
+            add_small(2, dattn)
+            p5[rows, :] = dot_nt(dattn, weight(0, 0)).astype(bf)
+
+    def sec_out_grad():
+        ready("ctx")
+        store_grads(4, 0, p3, p1)
+        begin("x")
+
+    first, second, is_first = lane_halves()
+    every_pair = [slice(pair * 2 * HD, (pair + 1) * 2 * HD) for pair in range(H // 2)]
+
+    def sec_heads(part):
+        def run():
+            if part == 0:
+                ready("probs", "q", "k", "v")
+            amount = rows_all // GROUP // 2
+
+            @pl.loop(part * amount, (part + 1) * amount)
+            def _(sent):
+                rows = pl.ds(pl.multiple_of(sent * GROUP, GROUP), GROUP)
+                dctx, q, k, v, low = p5[rows, :], p4[rows, :], p7[rows, :], p8[rows, :], p0[rows, :]
+                dcc = [both_heads(dctx[:, lanes], first, second) for lanes in every_pair]
+                dprobs = jnp.concatenate([dot_nt(v[:, lanes], wide) for lanes, wide in zip(every_pair, dcc)], axis=1)
+                probs = low.astype(f32)
+                dscores = probs * (dprobs - jnp.sum(dprobs * probs, axis=0, keepdims=True))
+                dscores = (dscores * HD ** (-0.5)).astype(bf)
+                dv = jnp.concatenate(
+                    [dot_nn(low[:, lanes], wide) for lanes, wide in zip(every_pair, dcc)], axis=1
+                ).astype(bf)
+                p6[rows, :] = dv
+                add_small(1, dv)
+                qq = [both_heads(q[:, lanes], first, second) for lanes in every_pair]
+                p2[rows, :] = jnp.concatenate(
+                    [dot_nn(dscores[:, lanes], wide) for lanes, wide in zip(every_pair, qq)], axis=1
+                ).astype(bf)
+                mixed = [dot_tn(dscores[:, lanes], k[:, lanes]) for lanes in every_pair]
+                dq = jnp.concatenate([jnp.where(is_first, m[:GROUP], m[GROUP:]) for m in mixed], axis=1).astype(bf)
+                p1[rows, :] = dq
+                add_small(0, dq)
+
+        return run
+
+    def sec_query_grad():
+        ready("x")
+        store_grads(4, 1, p3, p1)
+
+    def sec_key_grad():
+        store_grads(5, 0, p3, p2)
+
+    def sec_value_grad():
+        store_grads(5, 1, p3, p6)
+
+    def sec_back(part):
+        def run():
+            if part == 0:
+                ready("w50", "w51")
+
+            @pl.loop(part * (count // 2), (part + 1) * (count // 2))
+            def _(i):
+                rows = tile_rows(i)
+                dx = dh[rows, :] + dot_nt(p1[rows, :], weight(0, 1))
+                dx += dot_nt(p2[rows, :], weight(1, 0)) + dot_nt(p6[rows, :], weight(1, 1))
+                p4[rows, :] = dx.astype(bf)
+
+        return run
+
+    sections = [sec_start]
+    for p in range(inner_rows):
+        sections += [sec_inner(p), sec_outer_grad(p), sec_inner_grad(p)]
+    sections += [sec_norm, sec_out_grad, sec_heads(0), sec_heads(1), sec_query_grad, sec_key_grad, sec_value_grad]
+    sections += [sec_back(0), sec_back(1)]
+    done = [3, 6, 9, 12, 17, 19]
+    events = {}
+
+    def at_tick(tick, order, action):
+        events.setdefault(tick, []).append((order, action))
+
+    for t in range(STEPS):
+        base = done[t]
+        at_tick(base, 0, functools.partial(ev_c_send, t))
+        at_tick(base + 1, 1, functools.partial(ev_c_wait, t))
+        at_tick(base + 1 + LAG_FIRST, 2, functools.partial(ev_first, t))
+        at_tick(base + 1 + LAG_FIRST + LAG_SECOND, 3, functools.partial(ev_second, t))
+        for hop in range(ZS):
+            at_tick(base + 1 + LAG_FIRST + LAG_SECOND + hop, 4 + hop, functools.partial(ev_z, t, hop))
+        at_tick(base + 1 + LAG_FIRST + LAG_SECOND + ZS - 1, 9, functools.partial(ev_fin, t))
+    for r in range(5):
+        at_tick(17 + 2 * r, 10, functools.partial(ev_turn_start, r))
+        at_tick(19 + 2 * r, -1, functools.partial(ev_turn_wait, r))
+    for tick in range(max(max(events) + 1, len(sections))):
+        if tick < len(sections):
+            sections[tick]()
+        if tick == len(sections) - 1:
+            dx_copy = pltpu.make_async_copy(p4, dx_hbm, l_sem.at[len(loads)])
+            dx_copy.start()
+        for _, action in sorted(events.get(tick, []), key=lambda item: item[0]):
+            action()
+    small_out[...] = t_acc[5]
+    for t in range(STEPS):
+        its = fbuf.at[pl.ds((1 - c) * (STEPS * per) + t * per, per)]
+        remote(its, its, f_s.at[t], f_r.at[t], sibling).wait_recv()
+
+    def a_copy(zz, yy):
+        return remote(a_out.at[zz, yy], a_in.at[z, y], a_s.at[zz, yy], a_r.at[z, y], (s, batch_of(zz, yy, c)))
+
+    def o_copy(zz, yy):
+        return remote(a_in.at[zz, yy], x_in.at[zz, yy], o_s.at[zz, yy], o_r.at[zz, yy], other)
+
+    for dz, dy in turns:
+        zz, yy = (z + dz) % ZS, (y + dy) % 2
+        for j in range(slots):
+            a_out[zz, yy, j] = fbuf[tab_ref[batch_of(zz, yy, c) * slots + j]]
+        a_copy(zz, yy).start()
+    for j in range(slots):
+        a_in[z, y, j] = fbuf[tab_ref[batch_of(z, y, c) * slots + j]]
+    o_copy(z, y).start()
+
+    def put(zz, yy, ss, got):
+        rows = pl.ds(pl.multiple_of(ss * upper + zz * BAND, BAND), BAND)
+        cols = pl.ds(pl.multiple_of(yy * HALF, 128), HALF)
+        for j in range(slots):
+            own_out[j, rows, cols] = got[zz, yy, j]
+
+    put(z, y, s, a_in)
+    for dz, dy in turns:
+        zz, yy = (z + dz) % ZS, (y + dy) % 2
+        remote(a_in.at[zz, yy], a_in.at[zz, yy], a_s.at[zz, yy], a_r.at[zz, yy], other).wait_recv()
+        o_copy(zz, yy).start()
+        put(zz, yy, s, a_in)
+    for dz, dy in [(0, 0)] + turns:
+        zz, yy = (z + dz) % ZS, (y + dy) % 2
+        o_copy(zz, yy).wait_recv()
+        put(zz, yy, 1 - s, x_in)
+    for t in range(STEPS):
+        for copy in (c_copy, xa_copy, yb_copy, ya_copy, xb_copy, f_copy):
+            copy(t).wait_send()
+
+        @pl.loop(0, ZS)
+        def _(zz):
+            @pl.when(zz > z)
+            def _():
+                z_copy(t, zz, 0).wait_send()
+
+            @pl.when(zz < z)
+            def _():
+                z_copy(t, zz, 1).wait_send()
+
+    for dz, dy in turns:
+        a_copy((z + dz) % ZS, (y + dy) % 2).wait_send()
+    for dz, dy in [(0, 0)] + turns:
+        o_copy((z + dz) % ZS, (y + dy) % 2).wait_send()
+    dx_copy.wait()
+
+
+RING = 3
+LAG_FIRST = 3
+LAG_SECOND = 2
+
+
+def run_backward_reduce(og, dc, small, saved, x, units, table, edges, slots):
+    rows, width = og.shape
+    bf, f32 = jnp.bfloat16, jnp.float32
+    _, q, k, v, probs, ctx, n1, rs1, hb, act, slope, n2, rs2, _ = saved[:14]
+    unit_rows = units.shape[1]
+    per = edges[1] - edges[0]
+    half = per // 2
+    dma = pltpu.SemaphoreType.DMA
+    vm = pltpu.VMEM
+    vmem = pl.BlockSpec(memory_space=pltpu.VMEM)
+    anyw = pl.BlockSpec(memory_space=pl.ANY)
+    upper = unit_rows // 2
+    return pl.pallas_call(
+        functools.partial(backward_reduce_kernel, edges),
+        name="backward_reduce",
+        out_shape=[
+            jax.ShapeDtypeStruct((rows, width), bf),
+            jax.ShapeDtypeStruct((slots, unit_rows, width), bf),
+            jax.ShapeDtypeStruct(small.shape, f32),
+        ],
+        in_specs=[pl.BlockSpec(memory_space=pltpu.SMEM)] + [vmem] * 4 + [anyw] * 13,
+        out_specs=[anyw, vmem, vmem],
+        scratch_shapes=[vm((rows, width), f32)] * 2
+        + [vm((rows, width), bf)] * 9
+        + [
+            vm((2, 2, per, unit_rows, width), bf),
+            vm((STEPS, 2, 2, half, unit_rows, width), bf),
+            vm((RING, 2, half, unit_rows, width), bf),
+            vm((STEPS, half, upper, width), bf),
+            vm((STEPS, half, unit_rows, HALF), bf),
+            vm((STEPS, half, upper, HALF), bf),
+            vm((STEPS, half, upper, HALF), bf),
+            vm((2, STEPS, ZS, 2, half, BAND, HALF), bf),
+            vm((2 * STEPS * per, BAND, HALF), bf),
+            vm((ZS, 2, slots, BAND, HALF), bf),
+            vm((ZS, 2, slots, BAND, HALF), bf),
+            vm((ZS, 2, slots, BAND, HALF), bf),
+            vm(small.shape, f32),
+            vm((6,) + small.shape, f32),
+            vm((5,) + small.shape, f32),
+        ]
+        + [dma((32,))]
+        + [dma((STEPS,))] * 10
+        + [dma((STEPS, ZS))] * 4
+        + [dma((STEPS,))] * 2
+        + [dma((ZS, 2))] * 4
+        + [dma((5,))] * 2
+        + [pltpu.SemaphoreType.REGULAR],
+        compiler_params=pltpu.CompilerParams(collective_id=3, has_side_effects=True, vmem_limit_bytes=63 << 20),
+    )(table, small, dc, rs1, rs2, og, n2, slope, act, hb, n1, ctx, q, k, v, x, probs.reshape(rows, width), units)
+
+
 def unit_positions(owner_list, slot_count):
     unit_total = owner_list.shape[0]
     same_owner = owner_list[:, None] == owner_list[None, :]
@@ -1081,13 +1408,19 @@
     else:
         dc, loss_total, grad_scale = any_size_rank(cls.reshape(sentences, width), logit_scale, pair_lang, owners)
         loss_total, grad_scale = loss_total.reshape(1), grad_scale.reshape(1)
-    back = run_backward(
-        out_grad.reshape(sentences * length, width), dc.reshape(cls.shape), small_params, saved, units, where, edges
-    )
-    grads = run_weight_grads(flat, saved, back, where, edges, places, unit_rows)
+    grad_rows = out_grad.reshape(sentences * length, width)
     if on_block:
-        owned_grad, small_total = reduce_units(grads, back[7], slot_count)
+        slot_units = jnp.arange(places, dtype=jnp.int32)[:, None] == positions[None, :]
+        sum_table = jnp.asarray(sum_places(edges), dtype=jnp.int32)
+        table = jnp.sum(jnp.where(slot_units, sum_table[None, :], 0), axis=1, dtype=jnp.int32)
+        d_tokens, owned_grad, small_total = run_backward_reduce(
+            grad_rows, dc, small_params, saved, flat, saved[14], table, edges, slot_count
+        )
+        owned_grad = owned_grad.astype(jnp.float32)
     else:
+        back = run_backward(grad_rows, dc.reshape(cls.shape), small_params, saved, units, where, edges)
+        grads = run_weight_grads(flat, saved, back, where, edges, places, unit_rows)
+        d_tokens = back[0]
         owned_grad = any_size_sums(grads, positions, owners, slot_count)
         small_total = lax.psum(back[7], ("stream", "batch"))
     step_value = float(STEP)
@@ -1111,7 +1444,7 @@
     back_order = lambda a: a.transpose(1, 0, 2)
     return (
         saved[0].reshape(tokens.shape),
-        back[0].reshape(tokens.shape),
+        d_tokens.reshape(tokens.shape),
         back_order(new_master),
         back_order(new_first),
         back_order(new_second),

time: 330 us -> 300 us (0.909)
  Pallas kernels: 307 us -> 274 us
    pallas_call x3 -> x1, Pallas kernels: 175 us -> 141 us  [run_backward_reduce(): pl.pallas_call(functools.partial(backward_reduce_kernel, edges), name='ba...]
where the time goes in v3:
time: 300 us; the launch traced here: 299 us
  Pallas kernels  274 us (91%)
  other arithmetic  11.9 us (4%)
  between operations  9.95 us (3%)
  local copies, waits for them, and re-layouts  3.27 us (1%)
    pallas_call x1, Pallas kernels, run_backward_reduce(): pl.pallas_call(functools.partial(backward_reduce_kernel, edges), name='ba...  141 us
    pallas_call x1, Pallas kernels, gather_units(): pl.pallas_call(gather_kernel, name='gather_units', out_shape=jax.ShapeDty...  73.2 us
    pallas_call x1, Pallas kernels, run_forward(): pl.pallas_call(functools.partial(forward_kernel, edges), name='layer_forw...  39.9 us
    pallas_call x1, Pallas kernels, rank_loss(): pl.pallas_call(rank_kernel, name='rank_loss', out_shape=[jax.ShapeDtypeSt...  19.9 us
    transpose x1, other arithmetic, per_device(): back_order = lambda a: a.transpose(1, 0, 2)  8.34 us

profile of v3, /device:TPU:8, one launch (start us, length us, event | category | flops | bytes accessed | tf_op | source)
XLA Modules:
  0.0 299.4 jit_solution(4964323830788820570)
XLA Ops:
  0.6 0.9 select_reduce_fusion.1
  1.6 1.2 multiply_add_fusion.1.pos_ref
  2.7 73.2 %gather_units.1.units_hbm = bf16[80,128,768]{2,1,0:T(8,128)(2,1)} custom-call(f32[5,128,768]{2,1,0:T(8,128)} %bitcast.59), custom_call_target="tpu_custom_call" | custom-call | tf_op jit(solution)/shard_map/gather_units/pallas_call | solution.py:290
  75.9 0.0 copy-start.1
  76.0 0.0 copy-start.7
  76.0 0.0 copy-start.8
  76.0 39.9 %layer_forward.1 = (bf16[1024,768]{1,0:T(8,128)(2,1)}, bf16[1024,768]{1,0:T(8,128)(2,1)}, bf16[1024,768]{1,0:T(8,128)(2,1)}, bf16[1024,768]{1,0:T(8,128)(2,1)}, ...) custom-call(s32[72]{0:T(128)} %multiply_add_fusion.1.pos_ref, ...), custom_call_target="tpu_custom_call" | custom-call | tf_op jit(solution)/shard_map/layer_forward/pallas_call | solution.py:577
  115.9 0.8 reshape.63.cls_ref
  117.4 0.0 copy-done.1
  117.4 0.1 copy.28.lang_col
  117.5 19.9 %rank_loss.1 = (f32[16,768]{1,0:T(8,128)S(1)}, f32[8,128]{1,0:T(8,128)S(1)}) custom-call(f32[1]{0:T(128)S(6)} %copy.30.scale_ref, f32[16,768]{1,0:T(8,128)S(1)} %reshape.63.cls_ref, s32[1,256]{1,0:T(1,128)S(1)} %bitcast.58, s32[256,1]{1,0:T(8,128)S(1)} %copy.28.lang_col), custom_call_target="tpu_custom_call" | custom-call | tf_op jit(solution)/shard_map/rank_loss/pallas_call | solution.py:390
  137.5 0.0 copy-start
  137.5 0.6 copy-done
  138.1 0.0 copy-done.7
  138.1 0.0 copy-done.8
  138.1 0.6 select_reduce_fusion.tab_ref
  138.7 141.2 %backward_reduce.1 = (bf16[1024,768]{1,0:T(8,128)(2,1)}, bf16[5,128,768]{2,1,0:T(8,128)(2,1)}, f32[12,768]{1,0:T(8,128)}) custom-call(s32[80]{0:T(128)} %select_reduce_fusion.tab_ref, f32[12,768]{1,0:T(8,128)} %small_ref.3, f32[16,768]{1,0:T(8,128)} %copy-done, f32[1024,1]{1,0:T(8,128)} %get-tuple-element.36.rs1_ref, f32[1024,1]{1,0:T(8,128)} %get-tuple-element.37.rs2_ref, ...), custom_call_target="tpu_custom_call" | custom-call | tf_op jit(solution)/shard_map/backward_reduce/pallas_call | solution.py:1275
  279.9 0.2 compare_reduce_fusion
  280.1 0.0 copy-start.3
  280.1 0.0 copy-start.4
  280.1 0.0 copy-start.5
  280.1 0.0 copy-start.6
  280.1 0.0 copy-start.2
  280.2 8.3 %convert_bitcast_fusion = (bf16[128,5,768]{2,0,1:T(8,128)(2,1)}, f32[5,128,768]{2,1,0:T(8,128)}, f32[128,5,768]{2,0,1:T(8,128)}, f32[128,5,768]{2,0,1:T(8,128)}) fusion(f32[128,5,768]{2,0,1:T(8,128)} %param.18, bf16[5,128,768]{2,1,0:T(8,128)(2,1)} %get-tuple-element.50, f32[128,5,768]{2,0,1:T(8,128)} %param.17, f32[128,5,768]{2,0,1:T(8,128)} %param.16, ...), kind=kLoop, calls=%fused_computation.17 | loop fusion | flops 9830400 | bytes 13762565 | tf_op jit(solution)/shard_map/transpose | solution.py:1444
  288.5 0.0 copy-done.3
  288.5 0.0 copy-done.4
  288.5 0.0 copy-done.5
  288.5 0.0 copy-done.6
  288.5 0.7 multiply_subtract_fusion
  289.2 0.5 fusion.13
  293.7 0.0 copy-done.2
  293.7 1.1 copy.33
  (1 shorter events, 0.0 us)
Async XLA Ops:
  75.9 41.4 %copy-start.1 = (s32[256]{0:T(256)S(1)}, s32[256]{0:T(256)}, u32[]{:S(2)}) copy-start(s32[256]{0:T(256)} %param.25) | copy-start | bytes 3076
  76.0 62.1 %copy-start.7 = (s32[72]{0:T(128)S(1)}, s32[72]{0:T(128)}, u32[]{:S(2)}) copy-start(s32[72]{0:T(128)} %multiply_add_fusion.1.pos_ref) | copy-start | bytes 868
  76.0 62.1 %copy-start.8 = (s32[72]{0:T(128)S(1)}, s32[72]{0:T(128)}, u32[]{:S(2)}) copy-start(s32[72]{0:T(128)} %constant.70.clone) | copy-start | bytes 868
  137.5 0.6 copy-start
  280.1 8.4 %copy-start.3 = (f32[12,768]{1,0:T(8,128)S(1)}, f32[12,768]{1,0:T(8,128)}, u32[]{:S(2)}) copy-start(f32[12,768]{1,0:T(8,128)} %small_ref.3) | copy-start | bytes 110596
  280.1 8.4 %copy-start.4 = (f32[12,768]{1,0:T(8,128)S(1)}, f32[12,768]{1,0:T(8,128)}, u32[]{:S(2)}) copy-start(f32[12,768]{1,0:T(8,128)} %param.20) | copy-start | bytes 110596
  280.1 8.4 %copy-start.5 = (f32[12,768]{1,0:T(8,128)S(1)}, f32[12,768]{1,0:T(8,128)}, u32[]{:S(2)}) copy-start(f32[12,768]{1,0:T(8,128)} %param.21) | copy-start | bytes 110596
  280.1 8.4 %copy-start.6 = (f32[12,768]{1,0:T(8,128)S(1)}, f32[12,768]{1,0:T(8,128)}, u32[]{:S(2)}) copy-start(f32[12,768]{1,0:T(8,128)} %get-tuple-element.51) | copy-start | bytes 110596
  280.1 13.5 %copy-start.2 = (bf16[1024,768]{1,0:T(8,128)(2,1)S(1)}, bf16[1024,768]{1,0:T(8,128)(2,1)}, u32[]{:S(2)}) copy-start(bf16[1024,768]{1,0:T(8,128)(2,1)} %get-tuple-element.49) | copy-start | bytes 4718596

commit v4 on v3

--- a/solution.py
+++ b/solution.py
@@ -779,13 +779,14 @@
 
 
 STEPS = 6
+EARLY = 2
 BAND = 16
 HALF = 384
 
 
 def step_units(edges):
     per = edges[1] - edges[0]
-    firsts = [(edges[5] + per * t, edges[4] + per * t) for t in range(4)]
+    firsts = [(edge + per * t, edge + per * (t + 1)) for edge in (edges[5], edges[4]) for t in (0, 2)]
     return firsts + [(edges[3], edges[0]), (edges[1], edges[2])]
 
 
@@ -803,9 +804,9 @@
     edges, tab_ref, small_ref, dc_ref, rs1_ref, rs2_ref, og_hbm, n2_hbm, slope_hbm, act_hbm, hb_hbm, n1_hbm, ctx_hbm,
     q_hbm, k_hbm, v_hbm, x_hbm, probs_hbm, units_hbm,
     dx_hbm, own_out, small_out,
-    dh, nbuf, p0, p1, p2, p3, p4, p5, p6, p7, p8, wbuf, gbuf, c_in, xa, yb, ya, xb, z_in, fbuf, a_out, a_in, x_in,
+    dh, nbuf, p0, p1, p2, p3, p4, p5, p6, p7, p8, wbuf, gbuf, c_in, xa, yb, ya, xb, ya_low, xb_low, zg, zd, zab, fbuf, a_out, a_in, x_in,
     gsm, t_acc, t_in,
-    l_sem, c_s, c_r, xa_s, xa_r, yb_s, yb_r, ya_s, ya_r, xb_s, xb_r, zr_s, zr_r, zl_s, zl_r, f_s, f_r, a_s, a_r, o_s, o_r,
+    l_sem, c_s, c_r, xa_s, xa_r, yb_s, yb_r, ya_s, ya_r, xb_s, xb_r, z_s, z_r, f_s, f_r, a_s, a_r, o_s, o_r,
     t_s, t_r, c_free,
 ):
     s, z, y, c = place()
@@ -814,14 +815,12 @@
     count = rows_all // TILE
     inner_rows = FF // width
     per = edges[1] - edges[0]
-    unit_rows = gbuf.shape[4]
+    upper = gbuf.shape[5]
+    unit_rows = 2 * upper
     slots = own_out.shape[0]
-    upper = unit_rows // 2
     sibling = (s, batch_of(z, y, 1 - c))
     across = (s, batch_of(z, 1 - y, c))
     other = (1 - s, batch_of(z, y, c))
-    left = (s, batch_of(z - 1, y, c))
-    right = (s, batch_of(z + 1, y, c))
     round_to = (sibling, across, other, (s, batch_of(z + 1 - 2 * (z % 2), y, c)), (s, batch_of((z + 2) % ZS, y, c)))
 
     barrier = pltpu.get_barrier_semaphore()
@@ -839,14 +838,14 @@
     chunk = lambda ref, p: ref.at[:, pl.ds(p * width, width)]
     matrix = lambda first: units_hbm.at[pl.ds(first, per)]
     firsts = step_units(edges)
-    acts, slopes = (p3, p5), (p4, p6)
+    acts, slopes = (p3, p5), (p4, p6, p3, p5)
     loads = {"og": (og_hbm, p0), "n2": (n2_hbm, nbuf), "hb": (hb_hbm, p2), "n1": (n1_hbm, nbuf), "probs": (probs_hbm, p0),
-             "ctx": (ctx_hbm, p3), "q": (q_hbm, p4), "k": (k_hbm, p7), "v": (v_hbm, p8), "x": (x_hbm, p3)}
+             "ctx": (ctx_hbm, p4), "q": (q_hbm, p6), "k": (k_hbm, p7), "v": (v_hbm, p8), "x": (x_hbm, p3)}
     for p in range(inner_rows):
         loads["act%d" % p] = (chunk(act_hbm, p), acts[p % 2])
-        loads["slope%d" % p] = (chunk(slope_hbm, p), slopes[p % 2])
-        loads["wo%d" % p] = (matrix(firsts[p][0]), wbuf.at[p % 2, 0])
-        loads["wi%d" % p] = (matrix(firsts[p][1]), wbuf.at[p % 2, 1])
+        loads["slope%d" % p] = (chunk(slope_hbm, p), slopes[p])
+        loads["wo%d" % p] = (matrix(edges[5] + p * per), wbuf.at[p % 2, 0])
+        loads["wi%d" % p] = (matrix(edges[4] + p * per), wbuf.at[p % 2, 1])
     for t in (4, 5):
         for m in range(2):
             loads["w%d%d" % (t, m)] = (matrix(firsts[t][m]), wbuf.at[t % 2, m])
@@ -862,7 +861,7 @@
         for name in names:
             copies[name].wait()
 
-    begin("og", "n2", "slope0", "wo0", "wi0", "act0", "hb", "slope1", "wo1", "wi1", "act1", "k", "v")
+    begin("og", "n2", "act0", "act1", "slope0", "wo0", "wi0", "hb", "slope1", "wo1", "wi1", "k", "v")
 
     row = lambda r: small_ref[r : r + 1, :]
     gsm[...] = jnp.zeros_like(gsm)
@@ -881,35 +880,58 @@
             src_ref=src, dst_ref=dst, send_sem=send, recv_sem=recv, device_id=target, device_id_type=MESH
         )
 
-    my_rows = pl.ds(pl.multiple_of(s * upper, upper), upper)
-    its_rows = pl.ds(pl.multiple_of((1 - s) * upper, upper), upper)
     my_cols = pl.ds(pl.multiple_of(y * HALF, 128), HALF)
     its_cols = pl.ds(pl.multiple_of((1 - y) * HALF, 128), HALF)
-    every = pl.ds(0, per // 2)
+    blocks = pl.ds(0, per // 2)
+    both = pl.ds(0, 2)
+    lines = pl.ds(0, upper)
 
     def band(zz):
-        return pl.ds(pl.multiple_of(s * upper + zz * BAND, BAND), BAND)
+        return pl.ds(pl.multiple_of(zz * BAND, BAND), BAND)
 
     def c_copy(t):
         return remote(gbuf.at[t, :, 1 - c], c_in.at[t % RING], c_s.at[t], c_r.at[t], sibling)
 
     def xa_copy(t):
-        return remote(gbuf.at[t, 0, c, every, its_rows], xa.at[t], xa_s.at[t], xa_r.at[t], other)
+        return remote(gbuf.at[t, 0, c, blocks, 1 - s], xa.at[t], xa_s.at[t], xa_r.at[t], other)
 
     def yb_copy(t):
-        return remote(gbuf.at[t, 1, c, every, pl.ds(0, unit_rows), its_cols], yb.at[t], yb_s.at[t], yb_r.at[t], across)
+        return remote(gbuf.at[t, 1, c, blocks, both, lines, its_cols], yb.at[t], yb_s.at[t], yb_r.at[t], across)
+
+    def ya_view(t, cols):
+        return gbuf.at[t, 0, c, blocks, s, band(z) if t < EARLY else lines, cols]
+
+    def xb_view(t, ss):
+        return gbuf.at[t, 1, c, blocks, ss, band(z) if t < EARLY else lines, my_cols]
+
+    def ya_land(t):
+        return ya_low.at[t] if t < EARLY else ya.at[t - EARLY]
+
+    def xb_land(t):
+        return xb_low.at[t] if t < EARLY else xb.at[t - EARLY]
 
     def ya_copy(t):
-        return remote(gbuf.at[t, 0, c, every, my_rows, its_cols], ya.at[t], ya_s.at[t], ya_r.at[t], across)
+        return remote(ya_view(t, its_cols), ya_land(t), ya_s.at[t], ya_r.at[t], across)
 
     def xb_copy(t):
-        return remote(gbuf.at[t, 1, c, every, its_rows, my_cols], xb.at[t], xb_s.at[t], xb_r.at[t], other)
-
-    def z_copy(t, zz, way):
-        send, recv, target = ((zr_s, zr_r, right), (zl_s, zl_r, left))[way]
-        return remote(
-            gbuf.at[t, pl.ds(0, 2), c, every, band(zz), my_cols], z_in.at[way, t, zz], send.at[t, zz], recv.at[t, zz], target
-        )
+        return remote(xb_view(t, 1 - s), xb_land(t), xb_s.at[t], xb_r.at[t], other)
+
+    def z_views(t, zz, dz):
+        if t < EARLY:
+            return [
+                (gbuf.at[t, 0, c, blocks, s, band(zz)], zg.at[t, dz - 1]),
+                (gbuf.at[t, 1, c, blocks, both, band(zz), my_cols], zd.at[t, dz - 1]),
+            ]
+        return [
+            (gbuf.at[t, m, c, blocks, s, band(zz), my_cols], zab.at[t - EARLY, dz - 1, m]) for m in range(2)
+        ]
+
+    def z_copies(t, dz):
+        zz = (z + dz) % ZS
+        return [
+            remote(view, land, z_s.at[n, t, dz - 1], z_r.at[n, t, dz - 1], (s, batch_of(zz, y, c)))
+            for n, (view, land) in enumerate(z_views(t, zz, dz))
+        ]
 
     def f_copy(t):
         mine = fbuf.at[pl.ds(c * (STEPS * per) + t * per, per)]
@@ -939,50 +961,34 @@
 
     def ev_first(t):
         xa_copy(t).wait_recv()
-        add(gbuf.at[t, 0, c, every, my_rows], xa.at[t])
+        add(gbuf.at[t, 0, c, blocks, s], xa.at[t])
+        if t >= EARLY:
+            ya_copy(t).start()
+        yb_copy(t).wait_recv()
+        add(gbuf.at[t, 1, c, blocks, both, lines, my_cols], yb.at[t])
+        if t >= EARLY:
+            xb_copy(t).start()
+
+    def ev_second_start(t):
         ya_copy(t).start()
-        yb_copy(t).wait_recv()
-        add(gbuf.at[t, 1, c, every, pl.ds(0, unit_rows), my_cols], yb.at[t])
         xb_copy(t).start()
 
     def ev_second(t):
         ya_copy(t).wait_recv()
-        add(gbuf.at[t, 0, c, every, my_rows, my_cols], ya.at[t])
+        add(ya_view(t, my_cols), ya_land(t))
         xb_copy(t).wait_recv()
-        add(gbuf.at[t, 1, c, every, my_rows, my_cols], xb.at[t])
-
-    def ev_z(t, hop):
-        @pl.when(z == hop)
-        def _():
-            @pl.loop(0, ZS)
-            def _(zz):
-                @pl.when(zz >= z)
-                def _():
-                    @pl.when(z > 0)
-                    def _():
-                        z_copy(t, zz, 0).wait_recv()
-                        for m in range(2):
-                            add(gbuf.at[t, m, c, every, band(zz), my_cols], z_in.at[0, t, zz, m])
-
-                    @pl.when(zz > z)
-                    def _():
-                        z_copy(t, zz, 0).start()
-
-        @pl.when(ZS - 1 - z == hop)
-        def _():
-            @pl.loop(0, ZS)
-            def _(zz):
-                @pl.when(zz <= z)
-                def _():
-                    @pl.when(z < ZS - 1)
-                    def _():
-                        z_copy(t, zz, 1).wait_recv()
-                        for m in range(2):
-                            add(gbuf.at[t, m, c, every, band(zz), my_cols], z_in.at[1, t, zz, m])
-
-                    @pl.when(zz < z)
-                    def _():
-                        z_copy(t, zz, 1).start()
+        add(xb_view(t, s), xb_land(t))
+
+    def ev_z_send(t):
+        for dz in (2, 1, 3):
+            for copy in z_copies(t, dz):
+                copy.start()
+
+    def ev_z_take(t):
+        for dz in (1, 3, 2):
+            for copy, (view, land) in zip(z_copies(t, dz), z_views(t, z, dz)):
+                copy.wait_recv()
+                add(view, land)
 
     def ev_fin(t):
         for m in range(2):
@@ -990,7 +996,7 @@
             @pl.loop(0, per // 2)
             def _(k):
                 at = c * (STEPS * per) + t * per + m * (per // 2) + k
-                fbuf[at] = gbuf[t, m, c, k, band(z), my_cols]
+                fbuf[at] = gbuf[t, m, c, k, s, band(z), my_cols]
 
         f_copy(t).start()
 
@@ -1030,7 +1036,7 @@
             cols = pl.ds(pl.multiple_of(piece * half, 128), half)
             block = dot_tn(lhs[:, cols], rhs[...]).astype(bf)
             for i in range(per // 2):
-                part = block[i * unit_rows : (i + 1) * unit_rows]
+                part = block[i * unit_rows : (i + 1) * unit_rows].reshape(2, upper, width)
 
                 @pl.when(piece == 0)
                 def _():
@@ -1044,7 +1050,7 @@
     def sec_inner(p):
         def run():
             ready("slope%d" % p, "wo%d" % p, "wi%d" % p)
-            slope = slopes[p % 2]
+            slope = slopes[p]
 
             @pl.loop(0, count)
             def _(i):
@@ -1067,11 +1073,11 @@
     def sec_outer_grad(p):
         def run():
             ready("act%d" % p)
-            store_grads(p, 0, acts[p % 2], p1)
+            store_grads(p // 2, p % 2, acts[p % 2], p1)
             if p + 2 < inner_rows:
                 begin("act%d" % (p + 2))
-            if p == 2:
-                begin("ctx")
+            else:
+                begin("slope%d" % p)
 
         return run
 
@@ -1079,11 +1085,9 @@
         def run():
             if p == 0:
                 ready("hb")
-            store_grads(p, 1, slopes[p % 2], p2)
-            if p + 2 < inner_rows:
-                begin("slope%d" % (p + 2))
-            if p == 2:
-                begin("q")
+            store_grads(2 + p // 2, p % 2, slopes[p], p2)
+            if p < 3:
+                begin(("ctx", "q", "x")[p])
 
         return run
 
@@ -1106,8 +1110,7 @@
 
     def sec_out_grad():
         ready("ctx")
-        store_grads(4, 0, p3, p1)
-        begin("x")
+        store_grads(4, 0, p4, p1)
 
     first, second, is_first = lane_halves()
     every_pair = [slice(pair * 2 * HD, (pair + 1) * 2 * HD) for pair in range(H // 2)]
@@ -1121,7 +1124,7 @@
             @pl.loop(part * amount, (part + 1) * amount)
             def _(sent):
                 rows = pl.ds(pl.multiple_of(sent * GROUP, GROUP), GROUP)
-                dctx, q, k, v, low = p5[rows, :], p4[rows, :], p7[rows, :], p8[rows, :], p0[rows, :]
+                dctx, q, k, v, low = p5[rows, :], p6[rows, :], p7[rows, :], p8[rows, :], p0[rows, :]
                 dcc = [both_heads(dctx[:, lanes], first, second) for lanes in every_pair]
                 dprobs = jnp.concatenate([dot_nt(v[:, lanes], wide) for lanes, wide in zip(every_pair, dcc)], axis=1)
                 probs = low.astype(f32)
@@ -1130,7 +1133,7 @@
                 dv = jnp.concatenate(
                     [dot_nn(low[:, lanes], wide) for lanes, wide in zip(every_pair, dcc)], axis=1
                 ).astype(bf)
-                p6[rows, :] = dv
+                p4[rows, :] = dv
                 add_small(1, dv)
                 qq = [both_heads(q[:, lanes], first, second) for lanes in every_pair]
                 p2[rows, :] = jnp.concatenate(
@@ -1151,7 +1154,7 @@
         store_grads(5, 0, p3, p2)
 
     def sec_value_grad():
-        store_grads(5, 1, p3, p6)
+        store_grads(5, 1, p3, p4)
 
     def sec_back(part):
         def run():
@@ -1162,39 +1165,44 @@
             def _(i):
                 rows = tile_rows(i)
                 dx = dh[rows, :] + dot_nt(p1[rows, :], weight(0, 1))
-                dx += dot_nt(p2[rows, :], weight(1, 0)) + dot_nt(p6[rows, :], weight(1, 1))
-                p4[rows, :] = dx.astype(bf)
+                dx += dot_nt(p2[rows, :], weight(1, 0)) + dot_nt(p4[rows, :], weight(1, 1))
+                p6[rows, :] = dx.astype(bf)
 
         return run
 
-    sections = [sec_start]
+    sections = [sec_start] + [sec_outer_grad(p) for p in range(inner_rows)]
     for p in range(inner_rows):
-        sections += [sec_inner(p), sec_outer_grad(p), sec_inner_grad(p)]
+        sections += [sec_inner(p), sec_inner_grad(p)]
     sections += [sec_norm, sec_out_grad, sec_heads(0), sec_heads(1), sec_query_grad, sec_key_grad, sec_value_grad]
     sections += [sec_back(0), sec_back(1)]
-    done = [3, 6, 9, 12, 17, 19]
+    done = [2, 4, 8, 12, 17, 19]
     events = {}
 
     def at_tick(tick, order, action):
         events.setdefault(tick, []).append((order, action))
 
     for t in range(STEPS):
-        base = done[t]
-        at_tick(base, 0, functools.partial(ev_c_send, t))
-        at_tick(base + 1, 1, functools.partial(ev_c_wait, t))
-        at_tick(base + 1 + LAG_FIRST, 2, functools.partial(ev_first, t))
-        at_tick(base + 1 + LAG_FIRST + LAG_SECOND, 3, functools.partial(ev_second, t))
-        for hop in range(ZS):
-            at_tick(base + 1 + LAG_FIRST + LAG_SECOND + hop, 4 + hop, functools.partial(ev_z, t, hop))
-        at_tick(base + 1 + LAG_FIRST + LAG_SECOND + ZS - 1, 9, functools.partial(ev_fin, t))
+        at_tick(done[t], 0, functools.partial(ev_c_send, t))
+        at_tick(PLACES[t][0], 1, functools.partial(ev_c_wait, t))
+        at_tick(PLACES[t][1], 2, functools.partial(ev_first, t))
+        if t < EARLY:
+            at_tick(PLACES[t][1], 2.5, functools.partial(ev_z_send, t))
+            at_tick(PLACES[t][2], 3, functools.partial(ev_z_take, t))
+            at_tick(PLACES[t][2], 3.5, functools.partial(ev_second_start, t))
+            at_tick(PLACES[t][3], 4, functools.partial(ev_second, t))
+        else:
+            at_tick(PLACES[t][2], 3, functools.partial(ev_second, t))
+            at_tick(PLACES[t][2], 3.5, functools.partial(ev_z_send, t))
+            at_tick(PLACES[t][3], 4, functools.partial(ev_z_take, t))
+        at_tick(PLACES[t][3], 5, functools.partial(ev_fin, t))
     for r in range(5):
-        at_tick(17 + 2 * r, 10, functools.partial(ev_turn_start, r))
-        at_tick(19 + 2 * r, -1, functools.partial(ev_turn_wait, r))
+        at_tick(16 + r, 10, functools.partial(ev_turn_start, r))
+        at_tick(17 + r, -1, functools.partial(ev_turn_wait, r))
     for tick in range(max(max(events) + 1, len(sections))):
         if tick < len(sections):
             sections[tick]()
         if tick == len(sections) - 1:
-            dx_copy = pltpu.make_async_copy(p4, dx_hbm, l_sem.at[len(loads)])
+            dx_copy = pltpu.make_async_copy(p6, dx_hbm, l_sem.at[len(loads)])
             dx_copy.start()
         for _, action in sorted(events.get(tick, []), key=lambda item: item[0]):
             action()
@@ -1238,15 +1246,9 @@
         for copy in (c_copy, xa_copy, yb_copy, ya_copy, xb_copy, f_copy):
             copy(t).wait_send()
 
-        @pl.loop(0, ZS)
-        def _(zz):
-            @pl.when(zz > z)
-            def _():
-                z_copy(t, zz, 0).wait_send()
-
-            @pl.when(zz < z)
-            def _():
-                z_copy(t, zz, 1).wait_send()
+        for dz in range(1, ZS):
+            for copy in z_copies(t, dz):
+                copy.wait_send()
 
     for dz, dy in turns:
         a_copy((z + dz) % ZS, (y + dy) % 2).wait_send()
@@ -1256,8 +1258,7 @@
 
 
 RING = 3
-LAG_FIRST = 3
-LAG_SECOND = 2
+PLACES = ((5, 9, 36, 43), (8, 12, 22, 78), (10, 15, 19, 41), (13, 17, 21, 27), (18, 21, 35, 43), (20, 24, 41, 47))
 
 
 def run_backward_reduce(og, dc, small, saved, x, units, table, edges, slots):
@@ -1286,13 +1287,17 @@
         + [vm((rows, width), bf)] * 9
         + [
             vm((2, 2, per, unit_rows, width), bf),
-            vm((STEPS, 2, 2, half, unit_rows, width), bf),
-            vm((RING, 2, half, unit_rows, width), bf),
+            vm((STEPS, 2, 2, half, 2, upper, width), bf),
+            vm((RING, 2, half, 2, upper, width), bf),
             vm((STEPS, half, upper, width), bf),
-            vm((STEPS, half, unit_rows, HALF), bf),
-            vm((STEPS, half, upper, HALF), bf),
-            vm((STEPS, half, upper, HALF), bf),
-            vm((2, STEPS, ZS, 2, half, BAND, HALF), bf),
+            vm((STEPS, half, 2, upper, HALF), bf),
+            vm((STEPS - EARLY, half, upper, HALF), bf),
+            vm((STEPS - EARLY, half, upper, HALF), bf),
+            vm((EARLY, half, BAND, HALF), bf),
+            vm((EARLY, half, BAND, HALF), bf),
+            vm((EARLY, ZS - 1, half, BAND, width), bf),
+            vm((EARLY, ZS - 1, half, 2, BAND, HALF), bf),
+            vm((STEPS - EARLY, ZS - 1, 2, half, BAND, HALF), bf),
             vm((2 * STEPS * per, BAND, HALF), bf),
             vm((ZS, 2, slots, BAND, HALF), bf),
             vm((ZS, 2, slots, BAND, HALF), bf),
@@ -1303,7 +1308,7 @@
         ]
         + [dma((32,))]
         + [dma((STEPS,))] * 10
-        + [dma((STEPS, ZS))] * 4
+        + [dma((2, STEPS, ZS - 1))] * 2
         + [dma((STEPS,))] * 2
         + [dma((ZS, 2))] * 4
         + [dma((5,))] * 2

time: 300 us -> 289 us (0.963)
  Pallas kernels: 274 us -> 263 us
    pallas_call x1, Pallas kernels: 141 us -> 130 us  [run_backward_reduce(): pl.pallas_call(functools.partial(backward_reduce_kernel, edges), name='ba...]
where the time goes in v4:
time: 289 us; the launch traced here: 288 us
  Pallas kernels  263 us (91%)
  other arithmetic  11.9 us (4%)
  between operations  9.95 us (3%)
  local copies, waits for them, and re-layouts  3.27 us (1%)
    pallas_call x1, Pallas kernels, run_backward_reduce(): pl.pallas_call(functools.partial(backward_reduce_kernel, edges), name='ba...  130 us
    pallas_call x1, Pallas kernels, gather_units(): pl.pallas_call(gather_kernel, name='gather_units', out_shape=jax.ShapeDty...  73.2 us
    pallas_call x1, Pallas kernels, run_forward(): pl.pallas_call(functools.partial(forward_kernel, edges), name='layer_forw...  39.9 us
    pallas_call x1, Pallas kernels, rank_loss(): pl.pallas_call(rank_kernel, name='rank_loss', out_shape=[jax.ShapeDtypeSt...  19.9 us
    transpose x1, other arithmetic, per_device(): back_order = lambda a: a.transpose(1, 0, 2)  8.34 us

profile of v4, /device:TPU:8, one launch (start us, length us, event | category | flops | bytes accessed | tf_op | source)
XLA Modules:
  0.0 288.4 jit_solution(7409840999539626529)
XLA Ops:
  0.6 0.9 select_reduce_fusion.1
  1.6 1.2 multiply_add_fusion.1.pos_ref
  2.7 73.2 %gather_units.1.units_hbm = bf16[80,128,768]{2,1,0:T(8,128)(2,1)} custom-call(f32[5,128,768]{2,1,0:T(8,128)} %bitcast.59), custom_call_target="tpu_custom_call" | custom-call | tf_op jit(solution)/shard_map/gather_units/pallas_call | solution.py:290
  75.9 0.0 copy-start.1
  76.0 0.0 copy-start.7
  76.0 0.0 copy-start.8
  76.0 39.9 %layer_forward.1 = (bf16[1024,768]{1,0:T(8,128)(2,1)}, bf16[1024,768]{1,0:T(8,128)(2,1)}, bf16[1024,768]{1,0:T(8,128)(2,1)}, bf16[1024,768]{1,0:T(8,128)(2,1)}, ...) custom-call(s32[72]{0:T(128)} %multiply_add_fusion.1.pos_ref, ...), custom_call_target="tpu_custom_call" | custom-call | tf_op jit(solution)/shard_map/layer_forward/pallas_call | solution.py:577
  115.9 0.8 reshape.63.cls_ref
  117.4 0.0 copy-done.1
  117.4 0.1 copy.28.lang_col
  117.5 19.9 %rank_loss.1 = (f32[16,768]{1,0:T(8,128)S(1)}, f32[8,128]{1,0:T(8,128)S(1)}) custom-call(f32[1]{0:T(128)S(6)} %copy.30.scale_ref, f32[16,768]{1,0:T(8,128)S(1)} %reshape.63.cls_ref, s32[1,256]{1,0:T(1,128)S(1)} %bitcast.58, s32[256,1]{1,0:T(8,128)S(1)} %copy.28.lang_col), custom_call_target="tpu_custom_call" | custom-call | tf_op jit(solution)/shard_map/rank_loss/pallas_call | solution.py:390
  137.5 0.0 copy-start
  137.5 0.6 copy-done
  138.1 0.0 copy-done.7
  138.1 0.0 copy-done.8
  138.1 0.6 select_reduce_fusion.tab_ref
  138.7 130.2 %backward_reduce.1 = (bf16[1024,768]{1,0:T(8,128)(2,1)}, bf16[5,128,768]{2,1,0:T(8,128)(2,1)}, f32[12,768]{1,0:T(8,128)}) custom-call(s32[80]{0:T(128)} %select_reduce_fusion.tab_ref, f32[12,768]{1,0:T(8,128)} %small_ref.3, f32[16,768]{1,0:T(8,128)} %copy-done, f32[1024,1]{1,0:T(8,128)} %get-tuple-element.36.rs1_ref, f32[1024,1]{1,0:T(8,128)} %get-tuple-element.37.rs2_ref, ...), custom_call_target="tpu_custom_call" | custom-call | tf_op jit(solution)/shard_map/backward_reduce/pallas_call | solution.py:1276
  269.0 0.2 compare_reduce_fusion
  269.1 0.0 copy-start.3
  269.1 0.0 copy-start.4
  269.2 0.0 copy-start.5
  269.2 0.0 copy-start.6
  269.2 0.0 copy-start.2
  269.2 8.3 %convert_bitcast_fusion = (bf16[128,5,768]{2,0,1:T(8,128)(2,1)}, f32[5,128,768]{2,1,0:T(8,128)}, f32[128,5,768]{2,0,1:T(8,128)}, f32[128,5,768]{2,0,1:T(8,128)}) fusion(f32[128,5,768]{2,0,1:T(8,128)} %param.18, bf16[5,128,768]{2,1,0:T(8,128)(2,1)} %get-tuple-element.50, f32[128,5,768]{2,0,1:T(8,128)} %param.17, f32[128,5,768]{2,0,1:T(8,128)} %param.16, ...), kind=kLoop, calls=%fused_computation.17 | loop fusion | flops 9830400 | bytes 13762565 | tf_op jit(solution)/shard_map/transpose | solution.py:1449
  277.5 0.0 copy-done.3
  277.5 0.0 copy-done.4
  277.5 0.0 copy-done.5
  277.5 0.0 copy-done.6
  277.5 0.7 multiply_subtract_fusion
  278.2 0.5 fusion.13
  282.7 0.0 copy-done.2
  282.7 1.1 copy.33
  (1 shorter events, 0.0 us)
Async XLA Ops:
  75.9 41.4 %copy-start.1 = (s32[256]{0:T(256)S(1)}, s32[256]{0:T(256)}, u32[]{:S(2)}) copy-start(s32[256]{0:T(256)} %param.25) | copy-start | bytes 3076
  76.0 62.1 %copy-start.7 = (s32[72]{0:T(128)S(1)}, s32[72]{0:T(128)}, u32[]{:S(2)}) copy-start(s32[72]{0:T(128)} %multiply_add_fusion.1.pos_ref) | copy-start | bytes 868
  76.0 62.1 %copy-start.8 = (s32[72]{0:T(128)S(1)}, s32[72]{0:T(128)}, u32[]{:S(2)}) copy-start(s32[72]{0:T(128)} %constant.70.clone) | copy-start | bytes 868
  137.5 0.6 copy-start
  269.1 8.4 %copy-start.3 = (f32[12,768]{1,0:T(8,128)S(1)}, f32[12,768]{1,0:T(8,128)}, u32[]{:S(2)}) copy-start(f32[12,768]{1,0:T(8,128)} %small_ref.3) | copy-start | bytes 110596
  269.1 8.4 %copy-start.4 = (f32[12,768]{1,0:T(8,128)S(1)}, f32[12,768]{1,0:T(8,128)}, u32[]{:S(2)}) copy-start(f32[12,768]{1,0:T(8,128)} %param.20) | copy-start | bytes 110596
  269.2 8.4 %copy-start.5 = (f32[12,768]{1,0:T(8,128)S(1)}, f32[12,768]{1,0:T(8,128)}, u32[]{:S(2)}) copy-start(f32[12,768]{1,0:T(8,128)} %param.21) | copy-start | bytes 110596
  269.2 8.4 %copy-start.6 = (f32[12,768]{1,0:T(8,128)S(1)}, f32[12,768]{1,0:T(8,128)}, u32[]{:S(2)}) copy-start(f32[12,768]{1,0:T(8,128)} %get-tuple-element.51) | copy-start | bytes 110596
  269.2 13.5 %copy-start.2 = (bf16[1024,768]{1,0:T(8,128)(2,1)S(1)}, bf16[1024,768]{1,0:T(8,128)(2,1)}, u32[]{:S(2)}) copy-start(bf16[1024,768]{1,0:T(8,128)(2,1)} %get-tuple-element.49) | copy-start | bytes 4718596

commit v5 on v4

--- a/solution.py
+++ b/solution.py
@@ -296,110 +296,6 @@
         scratch_shapes=[pltpu.VMEM((slots, rows, width), jnp.bfloat16), pltpu.SemaphoreType.DMA((slots,))] + line + plane,
         compiler_params=pltpu.CompilerParams(collective_id=0, has_side_effects=True, vmem_limit_bytes=VMEM_MOST),
     )(own)
-
-
-def rank_kernel(scale_ref, cls_ref, lang_row, lang_col, dc_ref, stats_ref, every, weights, z_s, z_r, pair_s, pair_r):
-    s, z, y, c = place()
-    sents, width = cls_ref.shape
-    pairs = lang_row.shape[1]
-    greet(s, z, y, c, "line")
-    cls = cls_ref[...]
-    root = lax.rsqrt(jnp.sum(cls * cls, axis=-1, keepdims=True) + NORM_EPS)
-    unit = cls * root
-    every[s, z, y, c] = unit.astype(jnp.bfloat16)
-
-    def along(to, frm):
-        return pltpu.make_async_remote_copy(
-            src_ref=every.at[s, frm, y, c], dst_ref=every.at[s, frm, y, c], send_sem=z_s.at[to], recv_sem=z_r.at[frm],
-            device_id=(s, batch_of(to, y, c)), device_id_type=MESH,
-        )
-
-    for to in range(ZS):
-
-        @pl.when(z != to)
-        def _():
-            along(to, z).start()
-
-    for frm in range(ZS):
-
-        @pl.when(z != frm)
-        def _():
-            along(frm, frm).wait_recv()
-
-    def swap(view, n, target):
-        copy = pltpu.make_async_remote_copy(
-            src_ref=view, dst_ref=view, send_sem=pair_s.at[n], recv_sem=pair_r.at[n], device_id=target,
-            device_id_type=MESH,
-        )
-        copy.start()
-        return copy
-
-    first = swap(every.at[s, :, y, c], 0, (s, batch_of(z, 1 - y, c)))
-    first.wait_recv()
-    then = swap(every.at[s, :, :, c], 1, (1 - s, batch_of(z, y, c)))
-    then.wait_recv()
-    last = swap(every.at[:, :, :, c], 2, (s, batch_of(z, y, 1 - c)))
-    last.wait_recv()
-    scale = scale_ref[0]
-    e_zero = every[0].reshape(pairs, width)
-    e_one = every[1].reshape(pairs, width)
-    cosines = lax.dot_general(e_zero, e_one, (((1,), (1,)), ((), ())), preferred_element_type=jnp.float32)
-    own = lax.broadcasted_iota(jnp.int32, (pairs, pairs), 0) == lax.broadcasted_iota(jnp.int32, (pairs, pairs), 1)
-    same = lang_col[...] == lang_row[...]
-    diagonal = jnp.where(own, 1.0, 0.0)
-    shifted = cosines - MARGIN * diagonal
-    logits = scale * shifted
-    masked = jnp.where(same, logits, -1e30)
-    both = -2.0 * diagonal
-    total = -2.0 * jnp.sum(logits * diagonal)
-    for axis in range(2):
-        top = jnp.max(masked, axis=axis, keepdims=True)
-        grown = jnp.where(same, jnp.exp(masked - top), 0.0)
-        summed = jnp.sum(grown, axis=axis, keepdims=True)
-        both += grown / summed
-        total += jnp.sum(jnp.log(summed) + top)
-    line = lax.broadcasted_iota(jnp.int32, stats_ref.shape, 0)
-    stats_ref[...] = jnp.where(line == 0, total, jnp.sum(both * shifted))
-    weights[0] = both
-    weights[1] = both.T
-    rows = weights[s, pl.ds(pl.multiple_of(batch_of(z, y, c) * sents, 16), sents), :]
-    partners = every[1 - s].reshape(pairs, width)
-    high = rows.astype(jnp.bfloat16)
-    rest = (rows - high.astype(jnp.float32)).astype(jnp.bfloat16)
-    mix = (((1,), (0,)), ((), ()))
-    de = lax.dot_general(high, partners, mix, preferred_element_type=jnp.float32)
-    de += lax.dot_general(rest, partners, mix, preferred_element_type=jnp.float32)
-    de = scale * de
-    dc_ref[...] = (de - unit * jnp.sum(unit * de, axis=-1, keepdims=True)) * root
-    for to in range(ZS):
-
-        @pl.when(z != to)
-        def _():
-            along(to, z).wait_send()
-
-    first.wait_send()
-    then.wait_send()
-    last.wait_send()
-
-
-def rank_loss(cls, scale, langs):
-    sents, width = cls.shape
-    pairs = langs.shape[0]
-    dma = pltpu.SemaphoreType.DMA
-    vmem = pl.BlockSpec(memory_space=pltpu.VMEM)
-    return pl.pallas_call(
-        rank_kernel,
-        name="rank_loss",
-        out_shape=[jax.ShapeDtypeStruct((sents, width), jnp.float32), jax.ShapeDtypeStruct((8, 128), jnp.float32)],
-        in_specs=[pl.BlockSpec(memory_space=pltpu.SMEM), vmem, vmem, vmem],
-        out_specs=[vmem, vmem],
-        scratch_shapes=[
-            pltpu.VMEM((2, ZS, 2, 2, sents, width), jnp.bfloat16),
-            pltpu.VMEM((2, pairs, pairs), jnp.float32),
-            dma((ZS,)), dma((ZS,)), dma((3,)), dma((3,)),
-        ],
-        compiler_params=pltpu.CompilerParams(collective_id=1, has_side_effects=True, vmem_limit_bytes=24 << 20),
-    )(scale, cls, langs.reshape(1, pairs), langs.reshape(pairs, 1))
 
 
 TILE = 256
@@ -801,13 +697,13 @@
 
 
 def backward_reduce_kernel(
-    edges, tab_ref, small_ref, dc_ref, rs1_ref, rs2_ref, og_hbm, n2_hbm, slope_hbm, act_hbm, hb_hbm, n1_hbm, ctx_hbm,
+    edges, tab_ref, scale_ref, small_ref, cls_ref, lang_row, lang_col, rs1_ref, rs2_ref, og_hbm, n2_hbm, slope_hbm, act_hbm, hb_hbm, n1_hbm, ctx_hbm,
     q_hbm, k_hbm, v_hbm, x_hbm, probs_hbm, units_hbm,
-    dx_hbm, own_out, small_out,
+    dx_hbm, own_out, small_out, stats_ref,
     dh, nbuf, p0, p1, p2, p3, p4, p5, p6, p7, p8, wbuf, gbuf, c_in, xa, yb, ya, xb, ya_low, xb_low, zg, zd, zab, fbuf, a_out, a_in, x_in,
-    gsm, t_acc, t_in,
+    gsm, t_acc, t_in, pooled, dlogits,
     l_sem, c_s, c_r, xa_s, xa_r, yb_s, yb_r, ya_s, ya_r, xb_s, xb_r, z_s, z_r, f_s, f_r, a_s, a_r, o_s, o_r,
-    t_s, t_r, c_free,
+    t_s, t_r, g_s, g_r, h_s, h_r, c_free,
 ):
     s, z, y, c = place()
     bf, f32 = jnp.bfloat16, jnp.float32
@@ -1009,24 +905,117 @@
         turn(r).wait()
         t_acc[r + 1] = t_acc[r] + t_in[r]
 
+    sents = cls_ref.shape[0]
+    pairs = lang_row.shape[1]
+    cls = cls_ref[...]
+    root = lax.rsqrt(jnp.sum(cls * cls, axis=-1, keepdims=True) + NORM_EPS)
+    unit = cls * root
+    pooled[s, z, y, c] = unit.astype(bf)
+    all_z, low_z, high_z = pl.ds(0, ZS), pl.ds(0, ZS // 2), pl.ds(ZS // 2, ZS // 2)
+
+    def g_copy(dz):
+        mine = pooled.at[s, z, y, c]
+        return remote(mine, mine, g_s.at[dz - 1], g_r.at[dz - 1], (s, batch_of((z + dz) % ZS, y, c)))
+
+    def h_copy(n, view, target):
+        return remote(view, view, h_s.at[n], h_r.at[n], target)
+
+    swaps = [
+        h_copy(0, pooled.at[s, all_z, y, c], across),
+        h_copy(1, pooled.at[s, all_z, y, c], other),
+        h_copy(2, pooled.at[1 - s, low_z, y, c], across),
+        h_copy(3, pooled.at[s, high_z, 1 - y, c], other),
+        h_copy(4, pooled.at[s, all_z, y, c], sibling),
+        h_copy(5, pooled.at[s, all_z, 1 - y, c], sibling),
+        h_copy(6, pooled.at[1 - s, all_z, y, c], sibling),
+        h_copy(7, pooled.at[1 - s, all_z, 1 - y, c], sibling),
+    ]
+    for dz in (2, 1, 3):
+        g_copy(dz).start()
+
+    def tile_start(i):
+        rows = slice(i * TILE, (i + 1) * TILE)
+        later = lax.broadcasted_iota(jnp.int32, (TILE, 1), 0) % GROUP != 0
+        dy = jnp.where(later, p0[rows, :].astype(f32), 0.0)
+        n2 = nbuf[rows, :]
+        add_small(6 + inner_rows, dy * n2)
+        add_small(7 + inner_rows, dy)
+        dr2 = norm_back(dy, n2, rs2_ref[rows, :], row(6 + inner_rows))
+        dh[rows, :] = dr2
+        df = dr2.astype(bf)
+        p1[rows, :] = df
+        add_small(3 + inner_rows, df)
+
+    def rank_rows():
+        scale = scale_ref[0]
+        mix = (((1,), (0,)), ((), ()))
+        e_zero = pooled[0].reshape(pairs, width)
+        e_one = pooled[1].reshape(pairs, width)
+        cosines = dot_nt(e_zero, e_one)
+        own = lax.broadcasted_iota(jnp.int32, (pairs, pairs), 0) == lax.broadcasted_iota(jnp.int32, (pairs, pairs), 1)
+        same = lang_col[...] == lang_row[...]
+        diagonal = jnp.where(own, 1.0, 0.0)
+        shifted = cosines - MARGIN * diagonal
+        logits = scale * shifted
+        masked = jnp.where(same, logits, -1e30)
+        twice = -2.0 * diagonal
+        total = -2.0 * jnp.sum(logits * diagonal)
+        for axis in range(2):
+            top = jnp.max(masked, axis=axis, keepdims=True)
+            grown = jnp.where(same, jnp.exp(masked - top), 0.0)
+            summed = jnp.sum(grown, axis=axis, keepdims=True)
+            twice += grown / summed
+            total += jnp.sum(jnp.log(summed) + top)
+        line = lax.broadcasted_iota(jnp.int32, stats_ref.shape, 0)
+        stats_ref[...] = jnp.where(line == 0, total, jnp.sum(twice * shifted))
+        dlogits[0] = twice
+        dlogits[1] = twice.T
+        mine = dlogits[s, pl.ds(pl.multiple_of(batch_of(z, y, c) * sents, 16), sents), :]
+        partners = pooled[1 - s].reshape(pairs, width)
+        upper_part = mine.astype(bf)
+        rest = (mine - upper_part.astype(f32)).astype(bf)
+        de = lax.dot_general(upper_part, partners, mix, preferred_element_type=f32)
+        de += lax.dot_general(rest, partners, mix, preferred_element_type=f32)
+        de = scale * de
+        return (de - unit * jnp.sum(unit * de, axis=-1, keepdims=True)) * root
+
     def sec_start():
         ready("og", "n2")
-        for i in range(count):
-            rows = slice(i * TILE, (i + 1) * TILE)
-            dh[rows, :] = p0[rows, :].astype(f32)
-            for sent in range(TILE // GROUP):
-                at = i * TILE + sent * GROUP
-                here = i * (TILE // GROUP) + sent
-                dh[at : at + 1, :] += dc_ref[here : here + 1, :]
-            dy = dh[rows, :]
-            n2 = nbuf[rows, :]
-            add_small(6 + inner_rows, dy * n2)
-            add_small(7 + inner_rows, dy)
-            dr2 = norm_back(dy, n2, rs2_ref[rows, :], row(6 + inner_rows))
-            dh[rows, :] = dr2
-            df = dr2.astype(bf)
-            p1[rows, :] = df
-            add_small(3 + inner_rows, df)
+        tile_start(0)
+        for dz in range(1, ZS):
+            back = pooled.at[s, (z - dz) % ZS, y, c]
+            remote(back, back, g_s.at[dz - 1], g_r.at[dz - 1], other).wait_recv()
+        for n in (0, 1, 4):
+            swaps[n].start()
+        tile_start(1)
+        tile_start(2)
+        swaps[0].wait_recv()
+        swaps[1].wait_recv()
+        for n in (2, 3, 5, 6):
+            swaps[n].start()
+        for i in range(3, count):
+            tile_start(i)
+        swaps[2].wait_recv()
+        swaps[3].wait_recv()
+        swaps[7].start()
+        for n in (4, 5, 6, 7):
+            swaps[n].wait_recv()
+        dc = rank_rows()
+        head = [pl.ds(sent * GROUP, 1) for sent in range(sents)]
+        og = jnp.concatenate([p0[sent * GROUP : sent * GROUP + 16, :].astype(f32)[:1] for sent in range(sents)], axis=0)
+        n2 = jnp.concatenate([nbuf[at, :] for at in head], axis=0)
+        rs2 = jnp.concatenate([rs2_ref[at, :] for at in head], axis=0)
+        dy = og + dc
+        add_small(6 + inner_rows, dy * n2)
+        add_small(7 + inner_rows, dy)
+        dr2 = norm_back(dy, n2, rs2, row(6 + inner_rows))
+        add_small(3 + inner_rows, dr2.astype(bf))
+        top = lax.broadcasted_iota(jnp.int32, (16, 1), 0) == 0
+        for sent in range(sents):
+            mine = dr2[sent : sent + 1, :]
+            dh[head[sent], :] = mine
+            block = slice(sent * GROUP, sent * GROUP + 16)
+            p1[block, :] = jnp.where(top, mine, p1[block, :].astype(f32)).astype(bf)
         begin("n1", "probs")
 
     def store_grads(t, m, lhs, rhs):
@@ -1250,6 +1239,10 @@
             for copy in z_copies(t, dz):
                 copy.wait_send()
 
+    for dz in range(1, ZS):
+        g_copy(dz).wait_send()
+    for swap in swaps:
+        swap.wait_send()
     for dz, dy in turns:
         a_copy((z + dz) % ZS, (y + dy) % 2).wait_send()
     for dz, dy in [(0, 0)] + turns:
@@ -1261,13 +1254,14 @@
 PLACES = ((5, 9, 36, 43), (8, 12, 22, 78), (10, 15, 19, 41), (13, 17, 21, 27), (18, 21, 35, 43), (20, 24, 41, 47))
 
 
-def run_backward_reduce(og, dc, small, saved, x, units, table, edges, slots):
+def run_backward_reduce(og, cls, scale, langs, small, saved, x, units, table, edges, slots):
     rows, width = og.shape
     bf, f32 = jnp.bfloat16, jnp.float32
     _, q, k, v, probs, ctx, n1, rs1, hb, act, slope, n2, rs2, _ = saved[:14]
     unit_rows = units.shape[1]
     per = edges[1] - edges[0]
     half = per // 2
+    pairs = langs.shape[0]
     dma = pltpu.SemaphoreType.DMA
     vm = pltpu.VMEM
     vmem = pl.BlockSpec(memory_space=pltpu.VMEM)
@@ -1280,9 +1274,10 @@
             jax.ShapeDtypeStruct((rows, width), bf),
             jax.ShapeDtypeStruct((slots, unit_rows, width), bf),
             jax.ShapeDtypeStruct(small.shape, f32),
+            jax.ShapeDtypeStruct((8, 128), f32),
         ],
-        in_specs=[pl.BlockSpec(memory_space=pltpu.SMEM)] + [vmem] * 4 + [anyw] * 13,
-        out_specs=[anyw, vmem, vmem],
+        in_specs=[pl.BlockSpec(memory_space=pltpu.SMEM)] * 2 + [vmem] * 6 + [anyw] * 13,
+        out_specs=[anyw, vmem, vmem, vmem],
         scratch_shapes=[vm((rows, width), f32)] * 2
         + [vm((rows, width), bf)] * 9
         + [
@@ -1305,6 +1300,8 @@
             vm(small.shape, f32),
             vm((6,) + small.shape, f32),
             vm((5,) + small.shape, f32),
+            vm((2, ZS, 2, 2) + cls.shape, bf),
+            vm((2, pairs, pairs), f32),
         ]
         + [dma((32,))]
         + [dma((STEPS,))] * 10
@@ -1312,9 +1309,11 @@
         + [dma((STEPS,))] * 2
         + [dma((ZS, 2))] * 4
         + [dma((5,))] * 2
+        + [dma((ZS - 1,))] * 2
+        + [dma((8,))] * 2
         + [pltpu.SemaphoreType.REGULAR],
         compiler_params=pltpu.CompilerParams(collective_id=3, has_side_effects=True, vmem_limit_bytes=63 << 20),
-    )(table, small, dc, rs1, rs2, og, n2, slope, act, hb, n1, ctx, q, k, v, x, probs.reshape(rows, width), units)
+    )(table, scale, small, cls, langs.reshape(1, pairs), langs.reshape(pairs, 1), rs1, rs2, og, n2, slope, act, hb, n1, ctx, q, k, v, x, probs.reshape(rows, width), units)
 
 
 def unit_positions(owner_list, slot_count):
@@ -1331,6 +1330,33 @@
     new_two = BETA_TWO * moment_two + (1.0 - BETA_TWO) * gradient * gradient
     stepped = new_one / fix_one / (jnp.sqrt(new_two / fix_two) + ADAM_EPS)
     return (weight_in - rate_value * (stepped + decay_value * weight_in), new_one, new_two)
+
+
+def adamw_kernel(fixes, filled_ref, weight_ref, grad_ref, first_ref, second_ref, new_ref, one_ref, two_ref, low_ref):
+    weight, first, second = weight_ref[...], first_ref[...], second_ref[...]
+    gradient = grad_ref[...].astype(jnp.float32)
+    moved = adamw(weight, gradient, first, second, RATE_UNITS, DECAY, *fixes)
+    used = filled_ref[pl.program_id(0)] > 0
+    new = jnp.where(used, moved[0], weight)
+    new_ref[...] = new
+    one_ref[...] = jnp.where(used, moved[1], first)
+    two_ref[...] = jnp.where(used, moved[2], second)
+    low_ref[...] = new.astype(jnp.bfloat16)
+
+
+def run_adamw(weight, gradient, first, second, filled, fixes):
+    slots, rows, width = weight.shape
+    block = pl.BlockSpec((1, rows // 2, width), lambda i, j, *_: (i, j, 0))
+    kinds = [jnp.float32] * 3 + [jnp.bfloat16]
+    return pl.pallas_call(
+        functools.partial(adamw_kernel, fixes),
+        name="adamw_units",
+        grid_spec=pltpu.PrefetchScalarGridSpec(
+            num_scalar_prefetch=1, grid=(slots, 2), in_specs=[block] * 4, out_specs=[block] * 4
+        ),
+        out_shape=[jax.ShapeDtypeStruct(weight.shape, kind) for kind in kinds],
+        compiler_params=pltpu.CompilerParams(vmem_limit_bytes=VMEM_MOST),
+    )(filled, weight, gradient, first, second)
 
 
 def any_size_units(own, positions, owners):
@@ -1407,22 +1433,19 @@
     flat = tokens.reshape(sentences * length, width)
     saved = run_forward(flat, small_params, units, where, edges)
     cls = saved[13]
-    if on_block:
-        dc, stats = rank_loss(cls.reshape(sentences, width), logit_scale, pair_lang)
-        loss_total, grad_scale = stats[0, :1], stats[1, :1]
-    else:
-        dc, loss_total, grad_scale = any_size_rank(cls.reshape(sentences, width), logit_scale, pair_lang, owners)
-        loss_total, grad_scale = loss_total.reshape(1), grad_scale.reshape(1)
     grad_rows = out_grad.reshape(sentences * length, width)
     if on_block:
         slot_units = jnp.arange(places, dtype=jnp.int32)[:, None] == positions[None, :]
         sum_table = jnp.asarray(sum_places(edges), dtype=jnp.int32)
         table = jnp.sum(jnp.where(slot_units, sum_table[None, :], 0), axis=1, dtype=jnp.int32)
-        d_tokens, owned_grad, small_total = run_backward_reduce(
-            grad_rows, dc, small_params, saved, flat, saved[14], table, edges, slot_count
+        d_tokens, owned_grad, small_total, stats = run_backward_reduce(
+            grad_rows, cls.reshape(sentences, width), logit_scale, pair_lang, small_params, saved, flat, saved[14], table, edges,
+            slot_count,
         )
-        owned_grad = owned_grad.astype(jnp.float32)
+        loss_total, grad_scale = stats[0, :1], stats[1, :1]
     else:
+        dc, loss_total, grad_scale = any_size_rank(cls.reshape(sentences, width), logit_scale, pair_lang, owners)
+        loss_total, grad_scale = loss_total.reshape(1), grad_scale.reshape(1)
         back = run_backward(grad_rows, dc.reshape(cls.shape), small_params, saved, units, where, edges)
         grads = run_weight_grads(flat, saved, back, where, edges, places, unit_rows)
         d_tokens = back[0]
@@ -1432,13 +1455,10 @@
     fix_one = 1.0 - BETA_ONE**step_value
     fix_two = 1.0 - BETA_TWO**step_value
     my_places = here_batch * slot_count + jnp.arange(slot_count, dtype=jnp.int32)
-    filled = jnp.any(my_places[:, None] == positions[None, :], axis=1)[:, None, None]
-    first_in, second_in = first_moment.transpose(1, 0, 2), second_moment.transpose(1, 0, 2)
-    moved = adamw(own, owned_grad, first_in, second_in, RATE_UNITS, DECAY, fix_one, fix_two)
-    new_master, new_first, new_second = (
-        jnp.where(filled, new, old) for new, old in zip(moved, (own, first_in, second_in))
+    filled = jnp.any(my_places[:, None] == positions[None, :], axis=1).astype(jnp.int32)
+    new_master, new_first, new_second, new_copy = run_adamw(
+        own, owned_grad, first_moment.transpose(1, 0, 2), second_moment.transpose(1, 0, 2), filled, (fix_one, fix_two)
     )
-    new_copy = new_master.astype(jnp.bfloat16)
     new_small, new_small_first, new_small_second = adamw(
         small_params, small_total, small_first, small_second, RATE_SMALL, 0.0, fix_one, fix_two
     )

time: 289 us -> 283 us (0.979)
  other arithmetic: 11.9 us -> 4.08 us
    pallas_call x1, Pallas kernels: 130 us -> 140 us  [run_backward_reduce(): pl.pallas_call(functools.partial(backward_reduce_kernel, edges), name='ba...]
    pallas_call x1, Pallas kernels: 19.9 us -> 10.6 us  [run_adamw(): pl.pallas_call(functools.partial(adamw_kernel, fixes), name='adamw_units'...]
    transpose x1 -> x0, other arithmetic: 8.34 us -> none  [per_device(): back_order = lambda a: a.transpose(1, 0, 2)]
where the time goes in v5:
time: 283 us
  Pallas kernels  264 us (93%)
  between operations  9.92 us (4%)
  local copies, waits for them, and re-layouts  4.68 us (2%)
  other arithmetic  4.08 us (1%)
    pallas_call x1, Pallas kernels, run_backward_reduce(): pl.pallas_call(functools.partial(backward_reduce_kernel, edges), name='ba...  140 us
    pallas_call x1, Pallas kernels, gather_units(): pl.pallas_call(gather_kernel, name='gather_units', out_shape=jax.ShapeDty...  73.2 us
    pallas_call x1, Pallas kernels, run_forward(): pl.pallas_call(functools.partial(forward_kernel, edges), name='layer_forw...  39.9 us
    pallas_call x1, Pallas kernels, run_adamw(): pl.pallas_call(functools.partial(adamw_kernel, fixes), name='adamw_units'...  10.6 us

profile of v5, /device:TPU:8, one launch (start us, length us, event | category | flops | bytes accessed | tf_op | source)
XLA Modules:
  0.0 282.5 jit_solution(2023877317327288289)
XLA Ops:
  0.6 0.9 select_reduce_fusion.1
  1.6 1.2 multiply_add_fusion.1.pos_ref
  2.7 73.2 %gather_units.1.units_hbm = bf16[80,128,768]{2,1,0:T(8,128)(2,1)} custom-call(f32[5,128,768]{2,1,0:T(8,128)} %bitcast.16), custom_call_target="tpu_custom_call" | custom-call | tf_op jit(solution)/shard_map/gather_units/pallas_call | solution.py:290
  75.9 0.0 copy-start.6
  76.0 0.0 copy-start.7
  76.0 0.0 copy-start.5
  76.0 39.9 %layer_forward.1 = (bf16[1024,768]{1,0:T(8,128)(2,1)}, bf16[1024,768]{1,0:T(8,128)(2,1)}, bf16[1024,768]{1,0:T(8,128)(2,1)}, bf16[1024,768]{1,0:T(8,128)(2,1)}, ...) custom-call(s32[72]{0:T(128)} %multiply_add_fusion.1.pos_ref, ...), custom_call_target="tpu_custom_call" | custom-call | tf_op jit(solution)/shard_map/layer_forward/pallas_call | solution.py:473
  115.9 1.4 reshape.62.cls_ref
  117.3 0.0 copy-done.6
  117.3 0.0 copy-done.7
  117.3 0.6 select_reduce_fusion.tab_ref
  118.6 0.0 copy-done.5
  118.6 0.8 copy.28.lang_col
  119.4 140.1 %backward_reduce.1 = (bf16[1024,768]{1,0:T(8,128)(2,1)}, bf16[5,128,768]{2,1,0:T(8,128)(2,1)}, f32[12,768]{1,0:T(8,128)}, f32[8,128]{1,0:T(8,128)}) custom-call(s32[80]{0:T(128)} %select_reduce_fusion.tab_ref, f32[1]{0:T(128)S(6)} %copy.30.scale_ref, f32[12,768]{1,0:T(8,128)} %small_ref.3, f32[16,768]{1,0:T(8,128)} %reshape.62.cls_ref, s32[1,256]{1,0:T(1,128)} %bitcast.25, ...), custom_call_target="tpu_custom_call" | custom-call | tf_op jit(solution)/shard_map/backward_reduce/pallas_call | solution.py:1270
  259.5 1.3 fusion.3
  264.2 0.2 compare_reduce_fusion
  264.4 0.5 convert_element_type.3.filled_ref
  264.9 0.0 copy-start.1
  264.9 0.0 copy-start.2
  264.9 0.0 copy-start.3
  264.9 0.0 copy-start.4
  264.9 0.0 copy-start
  264.9 10.6 %adamw_units.1 = (f32[5,128,768]{2,1,0:T(8,128)}, f32[5,128,768]{2,1,0:T(8,128)}, f32[5,128,768]{2,1,0:T(8,128)}, bf16[5,128,768]{2,1,0:T(8,128)(2,1)}) custom-call(s32[5]{0:T(128)} %convert_element_type.3.filled_ref, f32[5,128,768]{2,1,0:T(8,128)} %bitcast.17, bf16[5,128,768]{2,1,0:T(8,128)(2,1)} %get-tuple-element.52.grad_ref, f32[5,128,768]{2,1,0:T(8,128)} %bitcast.20, ...), custom_call_target="tpu_custom_call" | custom-call | tf_op jit(solution)/shard_map/adamw_units/pallas_call | solution.py:1351
  275.5 0.0 copy-done.1
  275.5 0.0 copy-done.2
  275.5 0.0 copy-done.3
  275.5 0.0 copy-done.4
  275.5 0.7 multiply_subtract_fusion
  276.9 0.0 copy-done
  276.9 1.1 copy.33
  (1 shorter events, 0.0 us)
Async XLA Ops:
  75.9 41.4 %copy-start.6 = (s32[72]{0:T(128)S(1)}, s32[72]{0:T(128)}, u32[]{:S(2)}) copy-start(s32[72]{0:T(128)} %multiply_add_fusion.1.pos_ref) | copy-start | bytes 868
  76.0 41.4 %copy-start.7 = (s32[72]{0:T(128)S(1)}, s32[72]{0:T(128)}, u32[]{:S(2)}) copy-start(s32[72]{0:T(128)} %constant.57.clone) | copy-start | bytes 868
  76.0 42.6 %copy-start.5 = (s32[256]{0:T(256)S(1)}, s32[256]{0:T(256)}, u32[]{:S(2)}) copy-start(s32[256]{0:T(256)} %param.25) | copy-start | bytes 3076
  264.9 10.6 %copy-start.1 = (f32[12,768]{1,0:T(8,128)S(1)}, f32[12,768]{1,0:T(8,128)}, u32[]{:S(2)}) copy-start(f32[12,768]{1,0:T(8,128)} %small_ref.3) | copy-start | bytes 110596
  264.9 10.6 %copy-start.2 = (f32[12,768]{1,0:T(8,128)S(1)}, f32[12,768]{1,0:T(8,128)}, u32[]{:S(2)}) copy-start(f32[12,768]{1,0:T(8,128)} %param.20) | copy-start | bytes 110596
  264.9 10.6 %copy-start.3 = (f32[12,768]{1,0:T(8,128)S(1)}, f32[12,768]{1,0:T(8,128)}, u32[]{:S(2)}) copy-start(f32[12,768]{1,0:T(8,128)} %param.21) | copy-start | bytes 110596
  264.9 10.6 %copy-start.4 = (f32[12,768]{1,0:T(8,128)S(1)}, f32[12,768]{1,0:T(8,128)}, u32[]{:S(2)}) copy-start(f32[12,768]{1,0:T(8,128)} %get-tuple-element.57) | copy-start | bytes 110596
  264.9 12.0 %copy-start = (bf16[1024,768]{1,0:T(8,128)(2,1)S(1)}, bf16[1024,768]{1,0:T(8,128)(2,1)}, u32[]{:S(2)}) copy-start(bf16[1024,768]{1,0:T(8,128)(2,1)} %get-tuple-element.51) | copy-start | bytes 4718596

commit v6 on v5

--- a/solution.py
+++ b/solution.py
@@ -438,7 +438,8 @@
     y = n2 * row(6 + inner_rows) + row(7 + inner_rows)
     out_ref[...] = y.astype(jnp.bfloat16)
     for sent in range(TILE // GROUP):
-        cls_ref[0, sent : sent + 1, :] = y[sent * GROUP : sent * GROUP + 1, :]
+        here = pl.program_id(0) * (TILE // GROUP) + sent
+        cls_ref[pl.ds(here, 1), :] = y[sent * GROUP : sent * GROUP + 1, :]
 
     @pl.when(pl.program_id(0) == pl.num_programs(0) - 1)
     def _():
@@ -463,12 +464,12 @@
     outs = [
         ((rows, width), bf), ((rows, width), bf), ((rows, width), bf), ((rows, width), bf), (probs_shape, bf),
         ((rows, width), bf), ((rows, width), f32), ((rows, 1), f32), ((rows, width), bf), ((rows, FF), bf),
-        ((rows, FF), bf), ((rows, width), f32), ((rows, 1), f32), ((count, sents, width), f32),
+        ((rows, FF), bf), ((rows, width), f32), ((rows, 1), f32), ((rows // GROUP, width), f32),
         ((edges[6],) + units.shape[1:], bf),
     ]
     specs = [tiles(shape) for shape, _ in outs]
     specs[4] = pl.BlockSpec((sents,) + probs_shape[1:], lambda i, *_: (i, 0, 0))
-    specs[13] = pl.BlockSpec((1, sents, width), lambda i, *_: (i, 0, 0))
+    specs[13] = whole(outs[13][0])
     specs[14] = pl.BlockSpec(memory_space=pl.ANY)
     return pl.pallas_call(
         functools.partial(forward_kernel, edges),
@@ -675,7 +676,7 @@
 
 
 STEPS = 6
-EARLY = 2
+EARLY = 1
 BAND = 16
 HALF = 384
 
@@ -697,9 +698,9 @@
 
 
 def backward_reduce_kernel(
-    edges, tab_ref, scale_ref, small_ref, cls_ref, lang_row, lang_col, rs1_ref, rs2_ref, og_hbm, n2_hbm, slope_hbm, act_hbm, hb_hbm, n1_hbm, ctx_hbm,
+    edges, tab_ref, scale_ref, small_ref, cls_ref, lang_row, rs1_ref, rs2_ref, og_hbm, n2_hbm, slope_hbm, act_hbm, hb_hbm, n1_hbm, ctx_hbm,
     q_hbm, k_hbm, v_hbm, x_hbm, probs_hbm, units_hbm,
-    dx_hbm, own_out, small_out, stats_ref,
+    dx_hbm, own_out, small_out, loss_out, gscale_out,
     dh, nbuf, p0, p1, p2, p3, p4, p5, p6, p7, p8, wbuf, gbuf, c_in, xa, yb, ya, xb, ya_low, xb_low, zg, zd, zab, fbuf, a_out, a_in, x_in,
     gsm, t_acc, t_in, pooled, dlogits,
     l_sem, c_s, c_r, xa_s, xa_r, yb_s, yb_r, ya_s, ya_r, xb_s, xb_r, z_s, z_r, f_s, f_r, a_s, a_r, o_s, o_r,
@@ -953,7 +954,8 @@
         e_one = pooled[1].reshape(pairs, width)
         cosines = dot_nt(e_zero, e_one)
         own = lax.broadcasted_iota(jnp.int32, (pairs, pairs), 0) == lax.broadcasted_iota(jnp.int32, (pairs, pairs), 1)
-        same = lang_col[...] == lang_row[...]
+        langs = jnp.broadcast_to(lang_row[...].astype(f32), (pairs, pairs))
+        same = langs == langs.T
         diagonal = jnp.where(own, 1.0, 0.0)
         shifted = cosines - MARGIN * diagonal
         logits = scale * shifted
@@ -966,8 +968,8 @@
             summed = jnp.sum(grown, axis=axis, keepdims=True)
             twice += grown / summed
             total += jnp.sum(jnp.log(summed) + top)
-        line = lax.broadcasted_iota(jnp.int32, stats_ref.shape, 0)
-        stats_ref[...] = jnp.where(line == 0, total, jnp.sum(twice * shifted))
+        loss_out[0] = total
+        gscale_out[0] = jnp.sum(twice * shifted)
         dlogits[0] = twice
         dlogits[1] = twice.T
         mine = dlogits[s, pl.ds(pl.multiple_of(batch_of(z, y, c) * sents, 16), sents), :]
@@ -1251,7 +1253,7 @@
 
 
 RING = 3
-PLACES = ((5, 9, 36, 43), (8, 12, 22, 78), (10, 15, 19, 41), (13, 17, 21, 27), (18, 21, 35, 43), (20, 24, 41, 47))
+PLACES = ((5, 12, 18, 22), (8, 12, 15, 20), (10, 14, 18, 24), (15, 19, 22, 26), (19, 22, 25, 26), (24, 26, 32, 42))
 
 
 def run_backward_reduce(og, cls, scale, langs, small, saved, x, units, table, edges, slots):
@@ -1274,10 +1276,11 @@
             jax.ShapeDtypeStruct((rows, width), bf),
             jax.ShapeDtypeStruct((slots, unit_rows, width), bf),
             jax.ShapeDtypeStruct(small.shape, f32),
-            jax.ShapeDtypeStruct((8, 128), f32),
+            jax.ShapeDtypeStruct((1,), f32),
+            jax.ShapeDtypeStruct((1,), f32),
         ],
-        in_specs=[pl.BlockSpec(memory_space=pltpu.SMEM)] * 2 + [vmem] * 6 + [anyw] * 13,
-        out_specs=[anyw, vmem, vmem, vmem],
+        in_specs=[pl.BlockSpec(memory_space=pltpu.SMEM)] * 2 + [vmem] * 5 + [anyw] * 13,
+        out_specs=[anyw, vmem, vmem] + [pl.BlockSpec(memory_space=pltpu.SMEM)] * 2,
         scratch_shapes=[vm((rows, width), f32)] * 2
         + [vm((rows, width), bf)] * 9
         + [
@@ -1313,7 +1316,7 @@
         + [dma((8,))] * 2
         + [pltpu.SemaphoreType.REGULAR],
         compiler_params=pltpu.CompilerParams(collective_id=3, has_side_effects=True, vmem_limit_bytes=63 << 20),
-    )(table, scale, small, cls, langs.reshape(1, pairs), langs.reshape(pairs, 1), rs1, rs2, og, n2, slope, act, hb, n1, ctx, q, k, v, x, probs.reshape(rows, width), units)
+    )(table, scale, small, cls, langs.reshape(1, pairs), rs1, rs2, og, n2, slope, act, hb, n1, ctx, q, k, v, x, probs.reshape(rows, width), units)
 
 
 def unit_positions(owner_list, slot_count):
@@ -1328,35 +1331,98 @@
 def adamw(weight_in, gradient, moment_one, moment_two, rate_value, decay_value, fix_one, fix_two):
     new_one = BETA_ONE * moment_one + (1.0 - BETA_ONE) * gradient
     new_two = BETA_TWO * moment_two + (1.0 - BETA_TWO) * gradient * gradient
-    stepped = new_one / fix_one / (jnp.sqrt(new_two / fix_two) + ADAM_EPS)
+    stepped = new_one * (1.0 / fix_one) / (jnp.sqrt(new_two * (1.0 / fix_two)) + ADAM_EPS)
     return (weight_in - rate_value * (stepped + decay_value * weight_in), new_one, new_two)
 
 
-def adamw_kernel(fixes, filled_ref, weight_ref, grad_ref, first_ref, second_ref, new_ref, one_ref, two_ref, low_ref):
-    weight, first, second = weight_ref[...], first_ref[...], second_ref[...]
-    gradient = grad_ref[...].astype(jnp.float32)
-    moved = adamw(weight, gradient, first, second, RATE_UNITS, DECAY, *fixes)
-    used = filled_ref[pl.program_id(0)] > 0
-    new = jnp.where(used, moved[0], weight)
-    new_ref[...] = new
-    one_ref[...] = jnp.where(used, moved[1], first)
-    two_ref[...] = jnp.where(used, moved[2], second)
-    low_ref[...] = new.astype(jnp.bfloat16)
-
-
-def run_adamw(weight, gradient, first, second, filled, fixes):
-    slots, rows, width = weight.shape
-    block = pl.BlockSpec((1, rows // 2, width), lambda i, j, *_: (i, j, 0))
-    kinds = [jnp.float32] * 3 + [jnp.bfloat16]
+def adamw_kernel(
+    fixes, mean_by, filled_ref, weight_hbm, grad_hbm, first_hbm, second_hbm, small_ref, small_grad, small_one, small_two,
+    scale_ref, scale_grad, scale_one, scale_two, loss_ref, pass_hbm,
+    new_hbm, one_hbm, two_hbm, low_hbm, new_small, new_small_one, new_small_two, new_scale, new_scale_one, new_scale_two,
+    new_loss, passed_hbm,
+    weight_v, grad_v, first_v, second_v, low_v, pass_v, in_sem, out_sem, pass_sem,
+):
+    slots = weight_v.shape[0]
+
+    def copy(src, dst, sem):
+        return pltpu.make_async_copy(src, dst, sem)
+
+    ins = [
+        [
+            copy(hbm.at[j], held.at[j], in_sem.at[n, j])
+            for n, (hbm, held) in enumerate(
+                ((weight_hbm, weight_v), (grad_hbm, grad_v), (first_hbm, first_v), (second_hbm, second_v))
+            )
+        ]
+        for j in range(slots)
+    ]
+    outs = [
+        [
+            copy(held.at[j], hbm.at[j], out_sem.at[n, j])
+            for n, (hbm, held) in enumerate(
+                ((new_hbm, weight_v), (one_hbm, first_v), (two_hbm, second_v), (low_hbm, low_v))
+            )
+        ]
+        for j in range(slots)
+    ]
+    for group in ins:
+        for item in group:
+            item.start()
+    pass_in, pass_out = copy(pass_hbm, pass_v, pass_sem.at[0]), copy(pass_v, passed_hbm, pass_sem.at[1])
+    pass_in.start()
+    new_small[...], new_small_one[...], new_small_two[...] = adamw(
+        small_ref[...], small_grad[...], small_one[...], small_two[...], RATE_SMALL, 0.0, *fixes
+    )
+    spread = lambda ref: jnp.full((8, 128), ref[0], dtype=jnp.float32)
+    turned = adamw(spread(scale_ref), spread(scale_grad), spread(scale_one), spread(scale_two), RATE_SCALE, 0.0, *fixes)
+    for ref, value in zip((new_scale, new_scale_one, new_scale_two), turned):
+        ref[0] = jnp.max(value)
+    new_loss[0] = loss_ref[0] * mean_by
+    for j in range(slots):
+        for item in ins[j]:
+            item.wait()
+        weight, first, second = weight_v[j], first_v[j], second_v[j]
+        moved = adamw(weight, grad_v[j].astype(jnp.float32), first, second, RATE_UNITS, DECAY, *fixes)
+        used = filled_ref[j] > 0
+        new = jnp.where(used, moved[0], weight)
+        weight_v[j] = new
+        first_v[j] = jnp.where(used, moved[1], first)
+        second_v[j] = jnp.where(used, moved[2], second)
+        low_v[j] = new.astype(jnp.bfloat16)
+        for item in outs[j]:
+            item.start()
+        if j == 0:
+            pass_in.wait()
+            pass_out.start()
+    for group in outs:
+        for item in group:
+            item.wait()
+    pass_out.wait()
+
+
+def run_adamw(units, small, scale, loss, filled, fixes, mean_by, passed):
+    weight, gradient = units[:2]
+    f32, bf = jnp.float32, jnp.bfloat16
+    slots = weight.shape[0]
+    anyw = pl.BlockSpec(memory_space=pl.ANY)
+    flat = pl.BlockSpec(memory_space=pltpu.VMEM)
+    single = pl.BlockSpec(memory_space=pltpu.SMEM)
+    outs = [(weight.shape, f32)] * 3 + [(weight.shape, bf)] + [(small[0].shape, f32)] * 3 + [((1,), f32)] * 4
+    outs += [(passed.shape, passed.dtype)]
+    dma = pltpu.SemaphoreType.DMA
     return pl.pallas_call(
-        functools.partial(adamw_kernel, fixes),
-        name="adamw_units",
-        grid_spec=pltpu.PrefetchScalarGridSpec(
-            num_scalar_prefetch=1, grid=(slots, 2), in_specs=[block] * 4, out_specs=[block] * 4
-        ),
-        out_shape=[jax.ShapeDtypeStruct(weight.shape, kind) for kind in kinds],
+        functools.partial(adamw_kernel, fixes, mean_by),
+        name="adamw_all",
+        in_specs=[single] + [anyw] * 4 + [flat] * 4 + [single] * 5 + [anyw],
+        out_specs=[anyw] * 4 + [flat] * 3 + [single] * 4 + [anyw],
+        scratch_shapes=[
+            pltpu.VMEM(weight.shape, f32), pltpu.VMEM(weight.shape, gradient.dtype), pltpu.VMEM(weight.shape, f32),
+            pltpu.VMEM(weight.shape, f32), pltpu.VMEM(weight.shape, bf), pltpu.VMEM(passed.shape, passed.dtype),
+            dma((4, slots)), dma((4, slots)), dma((2,)),
+        ],
+        out_shape=[jax.ShapeDtypeStruct(shape, kind) for shape, kind in outs],
         compiler_params=pltpu.CompilerParams(vmem_limit_bytes=VMEM_MOST),
-    )(filled, weight, gradient, first, second)
+    )(filled, *units, *small, *scale, loss, passed)
 
 
 def any_size_units(own, positions, owners):
@@ -1438,15 +1504,14 @@
         slot_units = jnp.arange(places, dtype=jnp.int32)[:, None] == positions[None, :]
         sum_table = jnp.asarray(sum_places(edges), dtype=jnp.int32)
         table = jnp.sum(jnp.where(slot_units, sum_table[None, :], 0), axis=1, dtype=jnp.int32)
-        d_tokens, owned_grad, small_total, stats = run_backward_reduce(
-            grad_rows, cls.reshape(sentences, width), logit_scale, pair_lang, small_params, saved, flat, saved[14], table, edges,
+        d_tokens, owned_grad, small_total, loss_total, grad_scale = run_backward_reduce(
+            grad_rows, cls, logit_scale, pair_lang, small_params, saved, flat, saved[14], table, edges,
             slot_count,
         )
-        loss_total, grad_scale = stats[0, :1], stats[1, :1]
     else:
-        dc, loss_total, grad_scale = any_size_rank(cls.reshape(sentences, width), logit_scale, pair_lang, owners)
+        dc, loss_total, grad_scale = any_size_rank(cls, logit_scale, pair_lang, owners)
         loss_total, grad_scale = loss_total.reshape(1), grad_scale.reshape(1)
-        back = run_backward(grad_rows, dc.reshape(cls.shape), small_params, saved, units, where, edges)
+        back = run_backward(grad_rows, dc.reshape(-1, TILE // GROUP, width), small_params, saved, units, where, edges)
         grads = run_weight_grads(flat, saved, back, where, edges, places, unit_rows)
         d_tokens = back[0]
         owned_grad = any_size_sums(grads, positions, owners, slot_count)
@@ -1456,16 +1521,19 @@
     fix_two = 1.0 - BETA_TWO**step_value
     my_places = here_batch * slot_count + jnp.arange(slot_count, dtype=jnp.int32)
     filled = jnp.any(my_places[:, None] == positions[None, :], axis=1).astype(jnp.int32)
-    new_master, new_first, new_second, new_copy = run_adamw(
-        own, owned_grad, first_moment.transpose(1, 0, 2), second_moment.transpose(1, 0, 2), filled, (fix_one, fix_two)
+    (
+        new_master, new_first, new_second, new_copy, new_small, new_small_first, new_small_second, scale_new, scale_one,
+        scale_two, loss_out, d_tokens,
+    ) = run_adamw(
+        (own, owned_grad, first_moment.transpose(1, 0, 2), second_moment.transpose(1, 0, 2)),
+        (small_params, small_total, small_first, small_second),
+        (logit_scale, grad_scale, scale_first, scale_second),
+        loss_total,
+        filled,
+        (fix_one, fix_two),
+        1.0 / (2 * owners * sentences),
+        d_tokens,
     )
-    new_small, new_small_first, new_small_second = adamw(
-        small_params, small_total, small_first, small_second, RATE_SMALL, 0.0, fix_one, fix_two
-    )
-    scale_new, scale_one, scale_two = adamw(
-        logit_scale, grad_scale, scale_first, scale_second, RATE_SCALE, 0.0, fix_one, fix_two
-    )
-    loss_out = loss_total / (2 * owners * sentences)
     back_order = lambda a: a.transpose(1, 0, 2)
     return (
         saved[0].reshape(tokens.shape),

time: 283 us -> 263 us (0.929)
  Pallas kernels: 264 us -> 256 us
  between operations: 9.92 us -> 2.85 us
  local copies, waits for them, and re-layouts: 4.68 us -> 0.01 us
    pallas_call x1, Pallas kernels: 140 us -> 133 us  [run_backward_reduce(): pl.pallas_call(functools.partial(backward_reduce_kernel, edges), name='ba...]
where the time goes in v6:
time: 263 us; the launch traced here: 262 us
  Pallas kernels  256 us (97%)
  other arithmetic  3.47 us (1%)
  between operations  2.85 us (1%)
    pallas_call x1, Pallas kernels, run_backward_reduce(): pl.pallas_call(functools.partial(backward_reduce_kernel, edges), name='ba...  133 us
    pallas_call x1, Pallas kernels, gather_units(): pl.pallas_call(gather_kernel, name='gather_units', out_shape=jax.ShapeDty...  73.2 us
    pallas_call x1, Pallas kernels, run_forward(): pl.pallas_call(functools.partial(forward_kernel, edges), name='layer_forw...  39.9 us
    pallas_call x1, Pallas kernels, run_adamw(): pl.pallas_call(functools.partial(adamw_kernel, fixes, mean_by), name='ada...  10.1 us

profile of v6, /device:TPU:8, one launch (start us, length us, event | category | flops | bytes accessed | tf_op | source)
XLA Modules:
  0.0 262.3 jit_solution(9993347578722678730)
XLA Ops:
  0.6 0.9 select_reduce_fusion.1
  1.6 1.2 multiply_add_fusion.pos_ref
  2.7 73.2 %gather_units.1.units_hbm = bf16[80,128,768]{2,1,0:T(8,128)(2,1)} custom-call(f32[5,128,768]{2,1,0:T(8,128)} %bitcast.13), custom_call_target="tpu_custom_call" | custom-call | tf_op jit(solution)/shard_map/gather_units/pallas_call | solution.py:290
  75.9 0.0 copy-start
  76.0 0.0 copy-start.1
  76.0 39.9 %layer_forward.1 = (bf16[1024,768]{1,0:T(8,128)(2,1)}, bf16[1024,768]{1,0:T(8,128)(2,1)}, bf16[1024,768]{1,0:T(8,128)(2,1)}, bf16[1024,768]{1,0:T(8,128)(2,1)}, ...) custom-call(s32[72]{0:T(128)} %multiply_add_fusion.pos_ref, ...), custom_call_target="tpu_custom_call" | custom-call | tf_op jit(solution)/shard_map/layer_forward/pallas_call | solution.py:474
  115.9 0.0 copy-done
  115.9 0.0 copy-done.1
  115.9 0.6 select_reduce_fusion.tab_ref
  117.2 132.8 %backward_reduce.1 = (bf16[1024,768]{1,0:T(8,128)(2,1)}, bf16[5,128,768]{2,1,0:T(8,128)(2,1)}, f32[12,768]{1,0:T(8,128)}, f32[1]{0:T(128)}, f32[1]{0:T(128)}) custom-call(s32[80]{0:T(128)} %select_reduce_fusion.tab_ref, f32[1]{0:T(128)S(6)} %copy.27.scale_ref, f32[12,768]{1,0:T(8,128)} %small_ref.5, f32[16,768]{1,0:T(8,128)} %get-tuple-element.46.cls_ref, ...), custom_call_target="tpu_custom_call" | custom-call | tf_op jit(solution)/shard_map/backward_reduce/pallas_call | solution.py:1272
  249.9 0.2 compare_reduce_fusion
  250.1 0.6 convert_element_type.3.filled_ref
  252.0 10.1 %adamw_all.1 = (f32[5,128,768]{2,1,0:T(8,128)}, f32[5,128,768]{2,1,0:T(8,128)}, f32[5,128,768]{2,1,0:T(8,128)}, bf16[5,128,768]{2,1,0:T(8,128)(2,1)}, f32[12,768...) custom-call(s32[5]{0:T(128)} %convert_element_type.3.filled_ref, ...), custom_call_target="tpu_custom_call" | custom-call | tf_op jit(solution)/shard_map/adamw_all/pallas_call | solution.py:1413
  (1 shorter events, 0.0 us)
Async XLA Ops:
  75.9 39.9 %copy-start = (s32[72]{0:T(128)S(1)}, s32[72]{0:T(128)}, u32[]{:S(2)}) copy-start(s32[72]{0:T(128)} %multiply_add_fusion.pos_ref) | copy-start | bytes 868
  76.0 39.9 %copy-start.1 = (s32[72]{0:T(128)S(1)}, s32[72]{0:T(128)}, u32[]{:S(2)}) copy-start(s32[72]{0:T(128)} %constant.5.clone) | copy-start | bytes 868

commit v7 on v6

--- a/solution.py
+++ b/solution.py
@@ -299,6 +299,7 @@
 
 
 TILE = 256
+PART = 6
 GROUP = LEN_ROWS
 
 
@@ -421,17 +422,26 @@
     def _():
         keep.start()
 
-    per = (edges[5] - edges[4]) // inner_rows
+    unit_rows = units_hbm.shape[1]
     total = h1 + row(3 + inner_rows)
-    for part in range(inner_rows):
-        cols = slice(part * width, (part + 1) * width)
-        w_in = matrix_of(held, edges[4] + part * per, edges[4] + (part + 1) * per)
-        u = dot_nt(hb, w_in) + row(3 + part)
+    parts = FF // (PART * unit_rows)
+
+    def inner_part(part):
+        at = part * PART * unit_rows
+        bias = small_ref[3 + at // width : 4 + at // width, at % width : at % width + PART * unit_rows]
+        return dot_nt(hb, matrix_of(held, edges[4] + part * PART, edges[4] + (part + 1) * PART)) + bias
+
+    ahead = inner_part(0)
+    for part in range(parts):
+        u = ahead
+        if part + 1 < parts:
+            ahead = inner_part(part + 1)
+        cols = slice(part * PART * unit_rows, (part + 1) * PART * unit_rows)
         value, slope = gelu_parts(u)
         act = value.astype(jnp.bfloat16)
         act_ref[:, cols] = act
         slope_ref[:, cols] = slope.astype(jnp.bfloat16)
-        total += dot_nn(act, matrix_of(held, edges[5] + part * per, edges[5] + (part + 1) * per))
+        total += dot_nn(act, matrix_of(held, edges[5] + part * PART, edges[5] + (part + 1) * PART))
     n2, rs2 = norm_parts(total)
     n2_ref[...] = n2
     rs2_ref[...] = rs2

time: 263 us -> 261 us (level)
  no operation moved by 1% of the time
where the time goes in v7:
time: 261 us
  Pallas kernels  255 us (98%)
  other arithmetic  3.47 us (1%)
  between operations  2.85 us (1%)
    pallas_call x1, Pallas kernels, run_backward_reduce(): pl.pallas_call(functools.partial(backward_reduce_kernel, edges), name='ba...  133 us
    pallas_call x1, Pallas kernels, gather_units(): pl.pallas_call(gather_kernel, name='gather_units', out_shape=jax.ShapeDty...  73.2 us
    pallas_call x1, Pallas kernels, run_forward(): pl.pallas_call(functools.partial(forward_kernel, edges), name='layer_forw...  38.6 us
    pallas_call x1, Pallas kernels, run_adamw(): pl.pallas_call(functools.partial(adamw_kernel, fixes, mean_by), name='ada...  10.1 us

profile of v7, /device:TPU:8, one launch (start us, length us, event | category | flops | bytes accessed | tf_op | source)
XLA Modules:
  0.0 261.0 jit_solution(9183187482768913501)
XLA Ops:
  0.6 0.9 select_reduce_fusion.1
  1.6 1.2 multiply_add_fusion.pos_ref
  2.7 73.2 %gather_units.1.units_hbm = bf16[80,128,768]{2,1,0:T(8,128)(2,1)} custom-call(f32[5,128,768]{2,1,0:T(8,128)} %bitcast.13), custom_call_target="tpu_custom_call" | custom-call | tf_op jit(solution)/shard_map/gather_units/pallas_call | solution.py:290
  75.9 0.0 copy-start
  76.0 0.0 copy-start.1
  76.0 38.6 %layer_forward.1 = (bf16[1024,768]{1,0:T(8,128)(2,1)}, bf16[1024,768]{1,0:T(8,128)(2,1)}, bf16[1024,768]{1,0:T(8,128)(2,1)}, bf16[1024,768]{1,0:T(8,128)(2,1)}, ...) custom-call(s32[72]{0:T(128)} %multiply_add_fusion.pos_ref, ...), custom_call_target="tpu_custom_call" | custom-call | tf_op jit(solution)/shard_map/layer_forward/pallas_call | solution.py:484
  114.6 0.0 copy-done
  114.6 0.0 copy-done.1
  114.6 0.6 select_reduce_fusion.tab_ref
  115.9 132.7 %backward_reduce.1 = (bf16[1024,768]{1,0:T(8,128)(2,1)}, bf16[5,128,768]{2,1,0:T(8,128)(2,1)}, f32[12,768]{1,0:T(8,128)}, f32[1]{0:T(128)}, f32[1]{0:T(128)}) custom-call(s32[80]{0:T(128)} %select_reduce_fusion.tab_ref, f32[1]{0:T(128)S(6)} %copy.27.scale_ref, f32[12,768]{1,0:T(8,128)} %small_ref.5, f32[16,768]{1,0:T(8,128)} %get-tuple-element.46.cls_ref, ...), custom_call_target="tpu_custom_call" | custom-call | tf_op jit(solution)/shard_map/backward_reduce/pallas_call | solution.py:1282
  248.7 0.2 compare_reduce_fusion
  248.8 0.6 convert_element_type.3.filled_ref
  250.7 10.1 %adamw_all.1 = (f32[5,128,768]{2,1,0:T(8,128)}, f32[5,128,768]{2,1,0:T(8,128)}, f32[5,128,768]{2,1,0:T(8,128)}, bf16[5,128,768]{2,1,0:T(8,128)(2,1)}, f32[12,768...) custom-call(s32[5]{0:T(128)} %convert_element_type.3.filled_ref, ...), custom_call_target="tpu_custom_call" | custom-call | tf_op jit(solution)/shard_map/adamw_all/pallas_call | solution.py:1423
  (1 shorter events, 0.0 us)
Async XLA Ops:
  75.9 38.7 %copy-start = (s32[72]{0:T(128)S(1)}, s32[72]{0:T(128)}, u32[]{:S(2)}) copy-start(s32[72]{0:T(128)} %multiply_add_fusion.pos_ref) | copy-start | bytes 868
  76.0 38.7 %copy-start.1 = (s32[72]{0:T(128)S(1)}, s32[72]{0:T(128)}, u32[]{:S(2)}) copy-start(s32[72]{0:T(128)} %constant.5.clone) | copy-start | bytes 868
